TPU v7x, 512 devices: a whole 4x8x8 slice. The times are simulated.
512 devices in a mesh: prow: 16 (over z_hi, x), pcol: 32 (over y, z_lo, core).
Axes of the slice: x: 4, y: 8, z: 8 (z_hi: 4, z_lo: 2; z = z_hi * 2 + z_lo), core: 2. Of those that a mesh axis runs over, the one named last changes fastest.
Arguments:
- matrix: bfloat16 [16384, 16384], P('prow', 'pcol'), may hold values from -6 to 6
- panels: bfloat16 [6, 16384, 256], P(None, ('prow', 'pcol')), may hold values from -0.375 to 0.375
- diag_blocks: float32 [6, 256, 256], replicated, may hold values from -0.1875 to 0.1875
- pivots: int32 [6, 256], replicated, may hold values from 0 to 16383, as said below
Outputs:
- updated: bfloat16 [16384, 16384], P('prow', 'pcol')
Inputs may be any that keep to these rules, and one draw needn't show every extreme that they name: `pivots`: within one step the 256 pivot rows are distinct, and no pivot row lies in a diagonal block row of any of the 6 steps.
All inputs are finite; a program needn't handle non-finite values.
Results may differ from a plain program's by a relative error of at most 0.0091.
Values may be sent and summed in bfloat16 or wider, within the bound.
No kernel may reach another device: no remote copies, remote signals or barrier semaphores. Data moves between devices by JAX's collectives and lax.ppermute only.
A program may use at most 64 MiB of HBM per device.

v0:
```python
import jax
import jax.numpy as jnp
from jax import lax
from jax.sharding import PartitionSpec as P

STEPS = 6


def spread(x, axis, root):
    mine = lax.axis_index(axis) == root
    return lax.psum(jnp.where(mine, x, jnp.zeros_like(x)), axis)


def body(matrix, panels, diag_blocks, pivots):
    n_rows = lax.axis_size("prow")
    local_rows = matrix.shape[0]
    width = diag_blocks.shape[1]
    my_row = lax.axis_index("prow")
    first = my_row * local_rows
    local_ids = jnp.arange(local_rows, dtype=jnp.int32)
    current = matrix
    finished = jnp.zeros((local_rows,), dtype=bool)
    for step in range(STEPS):
        owner = step % n_rows
        offset = step // n_rows * width
        owns = my_row == owner
        shifted = pivots[step] - first
        inside = (shifted >= 0) & (shifted < local_rows)
        target = jnp.where(inside, shifted, local_rows)
        picked = jnp.take(current, target, axis=0, mode="fill", fill_value=0).astype(jnp.float32)
        diag_rows = current[offset : offset + width]
        new_top = lax.psum(picked.astype(jnp.bfloat16), "prow").astype(jnp.float32)
        old_rows = spread(diag_rows, "prow", owner)
        current = current.at[target].set(old_rows, mode="drop")
        solved = lax.linalg.triangular_solve(
            diag_blocks[step], new_top, left_side=True, lower=True, unit_diagonal=True
        )
        upper = solved.astype(jnp.bfloat16)
        finished = finished | owns & (local_ids >= offset) & (local_ids < offset + width)
        product = jnp.dot(
            lax.all_gather(panels[step], "pcol", axis=0, tiled=True),
            upper,
            preferred_element_type=jnp.float32,
        )
        changed = (current.astype(jnp.float32) - product).astype(jnp.bfloat16)
        current = jnp.where(finished[:, None], current, changed)
        block_now = current[offset : offset + width]
        current = current.at[offset : offset + width].set(jnp.where(owns, upper, block_now))
    return current


def solution(mesh):
    return jax.shard_map(
        body,
        mesh=mesh,
        in_specs=(P("prow", "pcol"), P(None, ("prow", "pcol"), None), P(), P()),
        out_specs=P("prow", "pcol"),
        check_vma=False,
    )
```

profile of v0, /device:TPU:1, one launch (start us, length us, event | category | flops | bytes accessed | tf_op | source)
XLA Modules:
  0.0 1096.8 jit_solution(13615284867030070986)
XLA Ops:
  12.2 2.4 convert_add_fusion
  14.7 4.0 while.18
  19.9 4.0 while.19
  25.6 19.7 %custom-call.8 = f32[2,128,128]{1,2,0:T(8,128)S(1)} custom-call(f32[2,128,128]{2,1,0:T(8,128)S(1)} %get-tuple-element.117), custom_call_target="InvertDiagBlocksLowerTriangular" | custom-call | tf_op jit(solution)/shard_map/triangular_solve/custom-call.1 | solution.py:35
  45.3 19.7 %custom-call.9 = f32[2,128,128]{1,2,0:T(8,128)S(1)} custom-call(f32[2,128,128]{2,1,0:T(8,128)S(1)} %get-tuple-element.118), custom_call_target="InvertDiagBlocksLowerTriangular" | custom-call | tf_op jit(solution)/shard_map/triangular_solve/custom-call.1 | solution.py:35
  65.0 41.2 %all-gather = bf16[1,1024,256]{2,1,0:T(8,128)(2,1)} all-gather(bf16[1,32,256]{2,1,0:T(8,128)(2,1)S(1)} %get-tuple-element.243), channel_id=2, replica_groups=mesh['prow'=16,'pcol'=32] {'pcol'}, dimensions={1}, use_global_device_ids=true | all-gather | bytes 540672 | tf_op jit(solution)/shard_map/all_gather | solution.py:41
  106.2 36.7 %all-gather.1 = bf16[1,1024,256]{2,1,0:T(8,128)(2,1)} all-gather(bf16[1,32,256]{2,1,0:T(8,128)(2,1)S(1)} %get-tuple-element.242), channel_id=3, replica_groups=mesh['prow'=16,'pcol'=32] {'pcol'}, dimensions={1}, use_global_device_ids=true | all-gather | bytes 540672 | tf_op jit(solution)/shard_map/all_gather | solution.py:41
  142.9 36.9 %all-reduce.23.cloned.1.call-done = (bf16[256,512]{1,0:T(8,128)(2,1)}, bf16[256,512]{1,0:T(8,128)(2,1)}) async-done(((bf16[256,512]{1,0:T(8,128)(2,1)}, bf16[256,512]{1,0:T(8,128)(2,1)}), (bf16[256,512]{1,0:T(8,128)(2,1)}, bf16[256,512]{1,0:T(8,128)(2,1)})) %all-reduce.23.cloned.1.call-update) | async-done | bytes 524304 | tf_op jit(solution)/shard_map/psum | solution.py:11
  182.1 2.2 scatter_fusion
  189.0 3.9 while.20
  193.0 166.7 %all-reduce.21.cloned.1.call-done = (bf16[256,512]{1,0:T(8,128)(2,1)}, bf16[256,512]{1,0:T(8,128)(2,1)}) async-done(((bf16[256,512]{1,0:T(8,128)(2,1)}, bf16[256,512]{1,0:T(8,128)(2,1)}), (bf16[256,512]{1,0:T(8,128)(2,1)}, bf16[256,512]{1,0:T(8,128)(2,1)})) %all-reduce.21.cloned.1.call-update) | async-done | bytes 524304 | tf_op jit(solution)/shard_map/psum | solution.py:11
  362.0 2.7 scatter_fusion.1
  369.0 5.3 while.21
  374.2 20.5 %custom-call.10 = f32[2,128,128]{1,2,0:T(8,128)S(1)} custom-call(f32[2,128,128]{2,1,0:T(8,128)} %copy-done.11), custom_call_target="InvertDiagBlocksLowerTriangular" | custom-call | tf_op jit(solution)/shard_map/triangular_solve/custom-call.1 | solution.py:35
  394.7 20.3 %custom-call.11 = f32[2,128,128]{1,2,0:T(8,128)} custom-call(f32[2,128,128]{2,1,0:T(8,128)S(1)} %get-tuple-element.120), custom_call_target="InvertDiagBlocksLowerTriangular" | custom-call | tf_op jit(solution)/shard_map/triangular_solve/custom-call.1 | solution.py:35
  416.2 45.9 %all-gather.2 = bf16[1,1024,256]{2,1,0:T(8,128)(2,1)S(1)} all-gather(bf16[1,32,256]{2,1,0:T(8,128)(2,1)S(1)} %copy-done.15), channel_id=4, replica_groups=mesh['prow'=16,'pcol'=32] {'pcol'}, dimensions={1}, use_global_device_ids=true | all-gather | bytes 540672 | tf_op jit(solution)/shard_map/all_gather | solution.py:41
  462.1 78.1 %all-reduce.19.cloned.1.call-done = (bf16[256,512]{1,0:T(8,128)(2,1)}, bf16[256,512]{1,0:T(8,128)(2,1)}) async-done(((bf16[256,512]{1,0:T(8,128)(2,1)}, bf16[256,512]{1,0:T(8,128)(2,1)}), (bf16[256,512]{1,0:T(8,128)(2,1)}, bf16[256,512]{1,0:T(8,128)(2,1)})) %all-reduce.19.cloned.1.call-update) | async-done | bytes 524304 | tf_op jit(solution)/shard_map/psum | solution.py:11
  544.1 2.2 scatter_fusion.2
  551.8 46.1 %all-gather.3 = bf16[1,1024,256]{2,1,0:T(8,128)(2,1)S(1)} all-gather(bf16[1,32,256]{2,1,0:T(8,128)(2,1)S(1)} %copy-done.14), channel_id=5, replica_groups=mesh['prow'=16,'pcol'=32] {'pcol'}, dimensions={1}, use_global_device_ids=true | all-gather | bytes 540672 | tf_op jit(solution)/shard_map/all_gather | solution.py:41
  597.9 124.0 %all-reduce.17.cloned.1.call-done = (bf16[256,512]{1,0:T(8,128)(2,1)}, bf16[256,512]{1,0:T(8,128)(2,1)}) async-done(((bf16[256,512]{1,0:T(8,128)(2,1)}, bf16[256,512]{1,0:T(8,128)(2,1)}), (bf16[256,512]{1,0:T(8,128)(2,1)}, bf16[256,512]{1,0:T(8,128)(2,1)})) %all-reduce.17.cloned.1.call-update) | async-done | bytes 524304 | tf_op jit(solution)/shard_map/psum | solution.py:11
  725.1 2.2 scatter_fusion.3
  731.6 4.2 while.22
  735.8 19.7 %custom-call.12 = f32[2,128,128]{1,2,0:T(8,128)S(1)} custom-call(f32[2,128,128]{2,1,0:T(8,128)S(1)} %get-tuple-element.121), custom_call_target="InvertDiagBlocksLowerTriangular" | custom-call | tf_op jit(solution)/shard_map/triangular_solve/custom-call.1 | solution.py:35
  755.5 45.9 %all-gather.4 = bf16[1,1024,256]{2,1,0:T(8,128)(2,1)S(1)} all-gather(bf16[1,32,256]{2,1,0:T(8,128)(2,1)S(1)} %copy-done.13), channel_id=6, replica_groups=mesh['prow'=16,'pcol'=32] {'pcol'}, dimensions={1}, use_global_device_ids=true | all-gather | bytes 540672 | tf_op jit(solution)/shard_map/all_gather | solution.py:41
  801.4 101.5 %all-reduce.15.cloned.1.call-done = (bf16[256,512]{1,0:T(8,128)(2,1)}, bf16[256,512]{1,0:T(8,128)(2,1)}) async-done(((bf16[256,512]{1,0:T(8,128)(2,1)}, bf16[256,512]{1,0:T(8,128)(2,1)}), (bf16[256,512]{1,0:T(8,128)(2,1)}, bf16[256,512]{1,0:T(8,128)(2,1)})) %all-reduce.15.cloned.1.call-update) | async-done | bytes 524304 | tf_op jit(solution)/shard_map/psum | solution.py:11
  905.2 2.4 scatter_fusion.4
  910.8 4.1 while.23
  915.0 19.7 %custom-call.13 = f32[2,128,128]{1,2,0:T(8,128)S(1)} custom-call(f32[2,128,128]{2,1,0:T(8,128)S(1)} %get-tuple-element.122), custom_call_target="InvertDiagBlocksLowerTriangular" | custom-call | tf_op jit(solution)/shard_map/triangular_solve/custom-call.1 | solution.py:35
  934.7 45.9 %all-gather.5 = bf16[1,1024,256]{2,1,0:T(8,128)(2,1)S(1)} all-gather(bf16[1,32,256]{2,1,0:T(8,128)(2,1)S(1)} %get-tuple-element.239), channel_id=7, replica_groups=mesh['prow'=16,'pcol'=32] {'pcol'}, dimensions={1}, use_global_device_ids=true | all-gather | bytes 540672 | tf_op jit(solution)/shard_map/all_gather | solution.py:41
  980.6 101.4 %all-reduce.13.cloned.1.call-done = (bf16[256,512]{1,0:T(8,128)(2,1)}, bf16[256,512]{1,0:T(8,128)(2,1)}) async-done(((bf16[256,512]{1,0:T(8,128)(2,1)}, bf16[256,512]{1,0:T(8,128)(2,1)}), (bf16[256,512]{1,0:T(8,128)(2,1)}, bf16[256,512]{1,0:T(8,128)(2,1)})) %all-reduce.13.cloned.1.call-update) | async-done | bytes 524304 | tf_op jit(solution)/shard_map/psum | solution.py:11
  1084.3 2.1 scatter_fusion.5
  1087.8 1.7 fusion.18
  (188 shorter events, 74.2 us)
Async XLA Ops:
  6.5 173.3 %all-reduce.23.cloned.1.call-start = ((), (), s32[]{:S(2)}) async-start(), calls=%async_computation.5 | async-start | bytes 1048576 | tf_op jit(solution)/shard_map/psum | solution.py:11
  11.6 348.0 %all-reduce.21.cloned.1.call-start = ((), (), s32[]{:S(2)}) async-start(), calls=%async_computation.4 | async-start | bytes 1048576 | tf_op jit(solution)/shard_map/psum | solution.py:11
  12.2 6.4 copy-start.12
  23.8 156.0 %copy-start.30 = (s32[2,2]{1,0:T(2,128)}, s32[2,2]{1,0:T(2,128)S(1)}, u32[]{:S(2)}) copy-start(s32[2,2]{1,0:T(2,128)S(1)} %get-tuple-element.592) | copy-start | bytes 52
  179.8 2.3 copy-start.4
  186.7 2.3 copy-start.31
  188.9 351.2 %all-reduce.19.cloned.1.call-start = ((), (), s32[]{:S(2)}) async-start(), calls=%async_computation.3 | async-start | bytes 1048576 | tf_op jit(solution)/shard_map/psum | solution.py:11
  192.9 168.2 %copy-start.11 = (f32[2,128,128]{2,1,0:T(8,128)}, f32[2,128,128]{2,1,0:T(8,128)S(1)}, u32[]{:S(2)}) copy-start(f32[2,128,128]{2,1,0:T(8,128)S(1)} %get-tuple-element.119) | copy-start | bytes 393220
  192.9 169.0 %copy-start.2 = (f32[256,256]{1,0:T(8,128)}, f32[256,256]{1,0:T(8,128)S(1)}, u32[]{:S(2)}) copy-start(f32[256,256]{1,0:T(8,128)S(1)} %get-tuple-element.552) | copy-start | bytes 786436
  361.9 2.7 copy-start.3
  366.6 2.4 copy-start.1
  368.0 47.0 %copy-start.21 = (s32[256]{0:T(256)S(1)}, s32[256]{0:T(256)}, u32[]{:S(2)}) copy-start(s32[256]{0:T(256)} %get-tuple-element.196) | copy-start | bytes 3076
  368.0 48.2 %copy-start.15 = (bf16[1,32,256]{2,1,0:T(8,128)(2,1)S(1)}, bf16[1,32,256]{2,1,0:T(8,128)(2,1)}, u32[]{:S(2)}) copy-start(bf16[1,32,256]{2,1,0:T(8,128)(2,1)} %get-tuple-element.241) | copy-start | bytes 49156
  368.9 353.1 %all-reduce.17.cloned.1.call-start = ((), (), s32[]{:S(2)}) async-start(), calls=%async_computation.2 | async-start | bytes 1048576 | tf_op jit(solution)/shard_map/psum | solution.py:11
  394.7 146.5 %copy-start.10 = (f32[2,128,128]{1,2,0:T(8,128)}, f32[2,128,128]{1,2,0:T(8,128)S(1)}, u32[]{:S(2)}) copy-start(f32[2,128,128]{1,2,0:T(8,128)S(1)} %custom-call.10) | copy-start | bytes 393220
  540.2 4.0 copy-start.5
  548.3 2.3 copy-start.19
  548.3 2.3 copy-start.20
  548.3 3.5 copy-start.14
  549.7 173.3 %copy-start.9 = (f32[2,128,128]{1,2,0:T(8,128)S(1)}, f32[2,128,128]{1,2,0:T(8,128)}, u32[]{:S(2)}) copy-start(f32[2,128,128]{1,2,0:T(8,128)} %custom-call.11) | copy-start | bytes 393220
  550.6 352.3 %all-reduce.15.cloned.1.call-start = ((), (), s32[]{:S(2)}) async-start(), calls=%async_computation.1 | async-start | bytes 1048576 | tf_op jit(solution)/shard_map/psum | solution.py:11
  722.0 3.1 copy-start.8
  729.2 2.4 copy-start
  729.2 2.4 copy-start.32
  730.7 24.8 %copy-start.22 = (s32[256]{0:T(256)S(1)}, s32[256]{0:T(256)}, u32[]{:S(2)}) copy-start(s32[256]{0:T(256)} %get-tuple-element.188) | copy-start | bytes 3076
  730.7 24.8 %copy-start.13 = (bf16[1,32,256]{2,1,0:T(8,128)(2,1)S(1)}, bf16[1,32,256]{2,1,0:T(8,128)(2,1)}, u32[]{:S(2)}) copy-start(bf16[1,32,256]{2,1,0:T(8,128)(2,1)} %get-tuple-element.244) | copy-start | bytes 49156
  731.5 350.4 %all-reduce.13.cloned.1.call-start = ((), (), s32[]{:S(2)}) async-start(), calls=%async_computation | async-start | bytes 1048576 | tf_op jit(solution)/shard_map/psum | solution.py:11
  755.5 149.6 %copy-start.18 = (s32[256,1]{0,1:T(1,128)S(1)}, s32[256,1]{0,1:T(1,128)}, u32[]{:S(2)}) copy-start(s32[256,1]{0,1:T(1,128)} %get-tuple-element.251) | copy-start | bytes 3076
  902.9 2.3 copy-start.7
  905.2 2.4 copy-start.29
  934.7 149.6 %copy-start.17 = (s32[256,1]{0,1:T(1,128)S(1)}, s32[256,1]{0,1:T(1,128)}, u32[]{:S(2)}) copy-start(s32[256,1]{0,1:T(1,128)} %get-tuple-element.189) | copy-start | bytes 3076
  1082.0 2.3 copy-start.6
  (8 other events, 16.6 us)
Sparse Core Ops, SparseCore 0:
  11.8 168.0 all-reduce.22
  189.1 170.5 all-reduce.20
  369.0 171.1 all-reduce.18
  550.7 171.1 all-reduce.16
  731.7 171.1 all-reduce.14
  910.9 170.9 all-reduce.12
where the time goes:
time: 1120 us; the launch traced here: 1100 us
  waiting for transfers between devices  609 us (54%)
  blocking collectives  262 us (23%)
  other arithmetic  146 us (13%)
  local copies, waits for them, and re-layouts  49 us (4%)
  matrix products  16.4 us (1%)
  between operations  14.7 us (1%)
    psum x6, waiting for transfers between devices, spread(): return lax.psum(jnp.where(mine, x, jnp.zeros_like(x)), axis)  609 us
    all_gather x6, blocking collectives, body(): lax.all_gather(panels[step], 'pcol', axis=0, tiled=True)  262 us
    another operation x9, other arithmetic, body(): lax.linalg.triangular_solve(diag_blocks[step], new_top, left_side=True, l...  122 us
    another operation x43, local copies, waits for them, and re-layouts, body(): lax.linalg.triangular_solve(diag_blocks[step], new_top, left_side=True, l...  25.2 us
  transfers between devices with their start and end apart: 6, of which 6 were waited for; matrix products, arithmetic and copies ran while one was open for 14% of the time, Pallas kernels for 0%

commit v1 on v0

v1 whole, which is shorter than its diff:
```python
import jax
import jax.numpy as jnp
from jax import lax
from jax.experimental import pallas as pl
from jax.experimental.pallas import tpu as pltpu
from jax.sharding import Mesh
from jax.sharding import PartitionSpec as P

STEPS = 6
NB = 256
ROWS = 1024
FINE = ("zh", "x", "y", "zl", "c")
PAIRS = [(s, k) for k in range(STEPS) for s in range(k + 1, STEPS)]


def split(v):
    high = v.astype(jnp.bfloat16)
    return high, (v - high.astype(jnp.float32)).astype(jnp.bfloat16)


def dot(a, b):
    return jnp.dot(a, b, preferred_element_type=jnp.float32)


def dot3(a, b):
    ah, al = split(a)
    bh, bl = split(b)
    return dot(ah, bh) + (dot(ah, bl) + dot(al, bh))


def inverse_kernel(l_ref, high_ref, low_ref):
    row = lax.broadcasted_iota(jnp.int32, (NB, NB), 0)
    col = lax.broadcasted_iota(jnp.int32, (NB, NB), 1)
    eye = (row == col).astype(jnp.float32)
    lower = [l_ref[s] for s in range(STEPS)]
    inv = [eye] * STEPS
    size = 1
    while size < NB:
        joins = (row // (2 * size) == col // (2 * size)) & (row // size > col // size)
        parts = [jnp.where(joins, m, 0.0) for m in lower]
        if size == 1:
            inv = [eye - m for m in parts]
        else:
            left = [dot3(m, x) for m, x in zip(parts, inv)]
            inv = [x - dot3(x, m) for x, m in zip(inv, left)]
        size *= 2
    for s in range(STEPS):
        high_ref[s], low_ref[s] = split(inv[s])


def inverses(diag_blocks):
    out = jax.ShapeDtypeStruct((STEPS, NB, NB), jnp.bfloat16)
    spec = pl.BlockSpec(memory_space=pltpu.VMEM)
    return pl.pallas_call(
        inverse_kernel,
        out_shape=(out, out),
        in_specs=[spec],
        out_specs=(spec, spec),
        compiler_params=pltpu.CompilerParams(vmem_limit_bytes=48 * 2**20),
        cost_estimate=pl.CostEstimate(flops=2 * 42 * 6 * NB**3, bytes_accessed=3 * 2**20, transcendentals=0),
    )(diag_blocks)


def exchange(v, axis):
    return lax.all_to_all(v, axis, 0, 0)


def everyone(v, axis):
    n = lax.axis_size(axis)
    return exchange(jnp.broadcast_to(v[None], (n,) + v.shape), axis)


def add_up(v):
    return jnp.sum(v.astype(jnp.float32), axis=0).astype(v.dtype)


def swap(v, axis):
    other = lax.ppermute(v, axis, [(0, 1), (1, 0)])
    first = lax.axis_index(axis) == 0
    return jnp.stack([jnp.where(first, v, other), jnp.where(first, other, v)])


def picks(ids, held):
    return (ids[:, None] == held[None, :]).astype(jnp.bfloat16)


def body(matrix, panels, diag_blocks, pivots):
    width = matrix.shape[1]
    zh, x, y = lax.axis_index("zh"), lax.axis_index("x"), lax.axis_index("y")
    zl, c = lax.axis_index("zl"), lax.axis_index("c")
    me = zh * 4 + x
    first = me * ROWS

    same = pivots[:, :, None, None] == pivots[None, None]
    t_ids = jnp.arange(STEPS, dtype=jnp.int32)
    i_ids = jnp.arange(NB, dtype=jnp.int32)
    before = (t_ids[None, :] < t_ids[:, None])[:, None, :, None]
    code = jnp.where(same & before, t_ids[:, None] * ROWS + i_ids[None, :], -1)
    origin = jnp.max(code, axis=(2, 3))
    base = jnp.where(origin >= 0, origin, pivots)
    swapped_at = jnp.where(origin >= 0, origin // ROWS, -1)

    high, low = inverses(diag_blocks)

    by_y = everyone(panels, "y")
    mine = by_y.transpose(1, 0, 2, 3).reshape(STEPS, 8 * 32, NB)
    held = (
        first
        + (jnp.arange(8, dtype=jnp.int32) * 128)[:, None]
        + zl * 64
        + c * 32
        + jnp.arange(32, dtype=jnp.int32)[None, :]
    ).reshape(-1)

    j_y = y * 32 + jnp.arange(32, dtype=jnp.int32)
    piv_y = lax.dynamic_slice_in_dim(pivots, y * 32, 32, 1)
    org_y = lax.dynamic_slice_in_dim(origin, y * 32, 32, 1)
    at_y = lax.dynamic_slice_in_dim(swapped_at, y * 32, 32, 1)
    parts = []
    for k in range(STEPS - 1):
        later = slice(k + 1, STEPS)
        l_ids = jnp.where(at_y[later] > k, org_y[later], piv_y[later])
        d_ids = (t_ids[later] * ROWS)[:, None] + j_y[None, :]
        ids = jnp.stack([l_ids, d_ids], axis=1).reshape(-1)
        parts.append(dot(picks(ids, held), mine[k]).astype(jnp.bfloat16))
    rows = jnp.concatenate(parts).reshape(15, 2, 4, 8, NB).transpose(2, 0, 1, 3, 4)
    chunk = add_up(exchange(rows, ("zl", "c")))
    chunk = add_up(everyone(chunk, "x"))
    chunk = add_up(everyone(chunk, "zh"))
    chunk = swap(swap(everyone(chunk, "y"), "zl"), "c")
    blocks = chunk.transpose(3, 4, 2, 1, 0, 5, 6).reshape(15, 2, NB, NB)

    whole = swap(swap(by_y, "zl"), "c")
    whole = whole.transpose(3, 2, 1, 0, 4, 5).reshape(STEPS, ROWS, NB)

    local = first + jnp.arange(ROWS, dtype=jnp.int32)
    picked = dot(picks(base.reshape(-1), local), matrix).astype(jnp.bfloat16)
    picked = picked.reshape(STEPS, 4, 64, width).transpose(1, 0, 2, 3)
    diag = matrix[:NB].reshape(4, 1, 64, width)
    part = exchange(jnp.concatenate([picked, diag], axis=1), "x")
    some = add_up(part[:, :STEPS])
    both = jnp.concatenate([some, part[:, STEPS]], axis=0).reshape(10, 4, 16, width).transpose(1, 0, 2, 3)
    part = exchange(both, "zh")
    active = jnp.concatenate([add_up(part[:, :STEPS]), part[0, STEPS:], part[1, STEPS : STEPS + 2]])
    active = everyone(everyone(active, "zh"), "x")
    active = active.transpose(2, 0, 1, 3, 4).reshape(2, STEPS, NB, width)

    tops = [active[0, s] for s in range(STEPS)]
    olds = [active[1, s] for s in range(STEPS)]
    current = matrix
    uppers = []
    place = {pair: n for n, pair in enumerate(PAIRS)}

    def less(a, b, u):
        return (a.astype(jnp.float32) - dot(b, u)).astype(jnp.bfloat16)

    for s in range(STEPS):
        u = (dot(high[s], tops[s]) + dot(low[s], tops[s])).astype(jnp.bfloat16)
        uppers.append(u)
        for t in range(s + 1, STEPS):
            n = place[(t, s)]
            tops[t] = less(tops[t], blocks[n, 0], u)
            olds[t] = less(olds[t], blocks[n, 1], u)
        put = picks(local, pivots[s])
        hit = jnp.any(put > 0, axis=1)
        moved = dot(put, olds[s]).astype(jnp.bfloat16)
        current = less(jnp.where(hit[:, None], moved, current), whole[s], u)
    own = lax.dynamic_index_in_dim(jnp.stack(uppers), jnp.minimum(me, STEPS - 1), 0, keepdims=False)
    head = jnp.where(me < STEPS, own, current[:NB])
    return jnp.concatenate([head, current[NB:]])


def solution(mesh):
    fine = Mesh(mesh.devices.reshape(4, 4, 8, 2, 2), FINE)
    prow, pcol = ("zh", "x"), ("y", "zl", "c")
    return jax.shard_map(
        body,
        mesh=fine,
        in_specs=(P(prow, pcol), P(None, prow + pcol, None), P(), P()),
        out_specs=P(prow, pcol),
        check_vma=False,
    )
```

time: 1120 us -> 284 us (0.25)
  the two profiles are of different devices: /device:TPU:1 before, /device:TPU:192 now
where the time goes in v1:
time: 284 us; the launch traced here: 283 us
  waiting for transfers between devices  112 us (39%)
  matrix products  62.7 us (22%)
  starting transfers between devices  56.7 us (20%)
  other arithmetic  20.6 us (7%)
  local copies, waits for them, and re-layouts  19.2 us (7%)
  Pallas kernels  9.87 us (3%)
    all_to_all x9, waiting for transfers between devices, exchange(): return lax.all_to_all(v, axis, 0, 0)  112 us
    dot_general x55, matrix products, dot(): return jnp.dot(a, b, preferred_element_type=jnp.float32)  62.7 us
    all_to_all x9, starting transfers between devices, exchange(): return lax.all_to_all(v, axis, 0, 0)  47.6 us
    pallas_call x1, Pallas kernels, inverses(): pl.pallas_call(inverse_kernel, out_shape=(out, out), in_specs=[spec], out...  9.87 us
    another operation x7, other arithmetic, swap(): return jnp.stack([jnp.where(first, v, other), jnp.where(first, other, v)])  9.62 us
    ppermute x4, starting transfers between devices, swap(): other = lax.ppermute(v, axis, [(0, 1), (1, 0)])  9.11 us
    broadcast_in_dim x6, local copies, waits for them, and re-layouts, everyone(): return exchange(jnp.broadcast_to(v[None], (n,) + v.shape), axis)  7.74 us
  transfers between devices with their start and end apart: 13, of which 9 were waited for; matrix products, arithmetic and copies ran while one was open for 11% of the time, Pallas kernels for 3%

profile of v1, /device:TPU:192, one launch (start us, length us, event | category | flops | bytes accessed | tf_op | source)
XLA Modules:
  0.0 282.7 jit_solution(13232009119652819701)
XLA Ops:
  1.9 7.1 %all-to-all-start.4 = ((bf16[8,6,32,256]{3,2,1,0:T(8,128)(2,1)}), bf16[8,6,32,256]{3,2,1,0:T(8,128)(2,1)S(1)}, u32[]{:S(2)}, u32[]{:S(2)}) async-start(bf16[8,6,32,256]{3,2,1,0:T(8,128)(2,1)} %broadcast_in_dim.59), calls=%async_computation.4 | async-start | bytes 1572864 | tf_op jit(solution)/shard_map/all_to_all | solution.py:65
  9.1 3.2 %select_reduce_fusion = s32[6,256]{1,0:T(8,128)S(1)} fusion(s32[6,256]{1,0:T(8,128)S(1)} %iota_add_fusion, s32[6,256]{1,0:T(8,128)} %param.7, pred[6,6]{1,0:T(8,128)(4,1)S(1)} %iota_compare_fusion), kind=kLoop, calls=%fused_computation | loop fusion | flops 9435648 | bytes 18468 | tf_op jit(solution)/shard_map/reduce_max | solution.py:99
  16.4 15.7 %all-to-all-done.4 = bf16[8,6,32,256]{3,2,1,0:T(8,128)(2,1)S(1)} async-done(((bf16[8,6,32,256]{3,2,1,0:T(8,128)(2,1)}), bf16[8,6,32,256]{3,2,1,0:T(8,128)(2,1)S(1)}, u32[]{:S(2)}, u32[]{:S(2)}) %all-to-all-start.4) | async-done | bytes 786464 | tf_op jit(solution)/shard_map/all_to_all | solution.py:65
  34.1 3.5 %all-to-all-start.5 = ((bf16[4,15,2,8,256]{4,3,2,1,0:T(8,128)(2,1)}), bf16[4,15,2,8,256]{4,3,2,1,0:T(8,128)(2,1)S(1)}, u32[]{:S(2)}, u32[]{:S(2)}) async-start(bf16[4,15,2,8,256]{4,3,2,1,0:T(8,128)(2,1)} %bitcast.363), calls=%async_computation.5 | async-start | bytes 983040 | tf_op jit(solution)/shard_map/all_to_all | solution.py:65
  37.6 6.6 %all-to-all-done.5 = bf16[4,15,2,8,256]{4,3,2,1,0:T(8,128)(2,1)S(1)} async-done(((bf16[4,15,2,8,256]{4,3,2,1,0:T(8,128)(2,1)}), bf16[4,15,2,8,256]{4,3,2,1,0:T(8,128)(2,1)S(1)}, u32[]{:S(2)}, u32[]{:S(2)}) %all-to-all-start.5) | async-done | bytes 491552 | tf_op jit(solution)/shard_map/all_to_all | solution.py:65
  45.1 4.3 %all-to-all-start.6 = ((bf16[4,15,2,8,256]{4,3,2,1,0:T(8,128)(2,1)}), bf16[4,15,2,8,256]{4,3,2,1,0:T(8,128)(2,1)S(1)}, u32[]{:S(2)}, u32[]{:S(2)}) async-start(bf16[4,15,2,8,256]{4,3,2,1,0:T(8,128)(2,1)} %broadcast_in_dim.60), calls=%async_computation.6 | async-start | bytes 983040 | tf_op jit(solution)/shard_map/all_to_all | solution.py:65
  53.6 5.0 %all-to-all-done.6 = bf16[4,15,2,8,256]{4,3,2,1,0:T(8,128)(2,1)S(1)} async-done(((bf16[4,15,2,8,256]{4,3,2,1,0:T(8,128)(2,1)}), bf16[4,15,2,8,256]{4,3,2,1,0:T(8,128)(2,1)S(1)}, u32[]{:S(2)}, u32[]{:S(2)}) %all-to-all-start.6) | async-done | bytes 491552 | tf_op jit(solution)/shard_map/all_to_all | solution.py:65
  58.6 3.6 %all-to-all-start = ((bf16[4,7,64,512]{3,2,1,0:T(8,128)(2,1)}), bf16[4,7,64,512]{3,2,1,0:T(8,128)(2,1)S(1)}, u32[]{:S(2)}, u32[]{:S(2)}) async-start(bf16[4,7,64,512]{3,2,1,0:T(8,128)(2,1)} %pad_maximum_fusion.2), calls=%async_computation | async-start | bytes 3670016 | tf_op jit(solution)/shard_map/all_to_all | solution.py:65
  62.3 22.3 %all-to-all-done = bf16[4,7,64,512]{3,2,1,0:T(8,128)(2,1)S(1)} async-done(((bf16[4,7,64,512]{3,2,1,0:T(8,128)(2,1)}), bf16[4,7,64,512]{3,2,1,0:T(8,128)(2,1)S(1)}, u32[]{:S(2)}, u32[]{:S(2)}) %all-to-all-start) | async-done | bytes 1835040 | tf_op jit(solution)/shard_map/all_to_all | solution.py:65
  85.4 8.8 %all-to-all-start.7 = ((bf16[4,15,2,8,256]{4,3,2,1,0:T(8,128)(2,1)}), bf16[4,15,2,8,256]{4,3,2,1,0:T(8,128)(2,1)S(1)}, u32[]{:S(2)}, u32[]{:S(2)}) async-start(bf16[4,15,2,8,256]{4,3,2,1,0:T(8,128)(2,1)} %broadcast_in_dim.61), calls=%async_computation.7 | async-start | bytes 983040 | tf_op jit(solution)/shard_map/all_to_all | solution.py:65
  95.4 10.2 %all-to-all-done.7 = bf16[4,15,2,8,256]{4,3,2,1,0:T(8,128)(2,1)S(1)} async-done(((bf16[4,15,2,8,256]{4,3,2,1,0:T(8,128)(2,1)}), bf16[4,15,2,8,256]{4,3,2,1,0:T(8,128)(2,1)S(1)}, u32[]{:S(2)}, u32[]{:S(2)}) %all-to-all-start.7) | async-done | bytes 491552 | tf_op jit(solution)/shard_map/all_to_all | solution.py:65
  105.6 4.9 %all-to-all-start.1 = ((bf16[4,10,16,512]{3,2,1,0:T(8,128)(2,1)}), bf16[4,10,16,512]{3,2,1,0:T(8,128)(2,1)S(1)}, u32[]{:S(2)}, u32[]{:S(2)}) async-start(bf16[4,10,16,512]{3,2,1,0:T(8,128)(2,1)} %copy.35), calls=%async_computation.1 | async-start | bytes 1310720 | tf_op jit(solution)/shard_map/all_to_all | solution.py:65
  110.6 13.0 %all-to-all-done.1 = bf16[4,10,16,512]{3,2,1,0:T(8,128)(2,1)S(1)} async-done(((bf16[4,10,16,512]{3,2,1,0:T(8,128)(2,1)}), bf16[4,10,16,512]{3,2,1,0:T(8,128)(2,1)S(1)}, u32[]{:S(2)}, u32[]{:S(2)}) %all-to-all-start.1) | async-done | bytes 655392 | tf_op jit(solution)/shard_map/all_to_all | solution.py:65
  124.6 3.6 %all-to-all-start.8 = ((bf16[8,15,2,8,256]{4,3,2,1,0:T(8,128)(2,1)}), bf16[8,15,2,8,256]{4,3,2,1,0:T(8,128)(2,1)S(1)}, u32[]{:S(2)}, u32[]{:S(2)}) async-start(bf16[8,15,2,8,256]{4,3,2,1,0:T(8,128)(2,1)} %broadcast_in_dim.62), calls=%async_computation.8 | async-start | bytes 1966080 | tf_op jit(solution)/shard_map/all_to_all | solution.py:65
  128.2 3.4 %collective-permute-start.2 = (bf16[8,6,32,256]{3,2,0,1:T(8,128)(2,1)S(1)}, bf16[8,6,32,256]{3,2,0,1:T(8,128)(2,1)}, u32[]{:S(2)}, u32[]{:S(2)}) collective-permute-start(bf16[8,6,32,256]{3,2,0,1:T(8,128)(2,1)S(1)} %copy.49), channel_id=1, source_target_pairs={{0,2},{2,0},{1,3},{3,1},{4,6},{6,4},{5,7},{7,5},{8,10},{10,8},{9,1... | collective-permute-start | bytes 2359304 | tf_op jit(solution)/shard_map/ppermute | solution.py:78
  131.8 19.0 %all-to-all-done.8 = bf16[8,15,2,8,256]{4,3,2,1,0:T(8,128)(2,1)S(1)} async-done(((bf16[8,15,2,8,256]{4,3,2,1,0:T(8,128)(2,1)}), bf16[8,15,2,8,256]{4,3,2,1,0:T(8,128)(2,1)S(1)}, u32[]{:S(2)}, u32[]{:S(2)}) %all-to-all-start.8) | async-done | bytes 983072 | tf_op jit(solution)/shard_map/all_to_all | solution.py:65
  151.9 6.9 %all-to-all-start.2 = ((bf16[4,12,16,512]{3,2,1,0:T(8,128)(2,1)}), bf16[4,12,16,512]{3,2,1,0:T(8,128)(2,1)S(1)}, u32[]{:S(2)}, u32[]{:S(2)}) async-start(bf16[4,12,16,512]{3,2,1,0:T(8,128)(2,1)} %broadcast_in_dim.54), calls=%async_computation.2 | async-start | bytes 1572864 | tf_op jit(solution)/shard_map/all_to_all | solution.py:65
  167.2 9.6 %all-to-all-done.2 = bf16[4,12,16,512]{3,2,1,0:T(8,128)(2,1)S(1)} async-done(((bf16[4,12,16,512]{3,2,1,0:T(8,128)(2,1)}), bf16[4,12,16,512]{3,2,1,0:T(8,128)(2,1)S(1)}, u32[]{:S(2)}, u32[]{:S(2)}) %all-to-all-start.2) | async-done | bytes 786464 | tf_op jit(solution)/shard_map/all_to_all | solution.py:65
  176.8 2.1 broadcast_in_dim.58
  178.9 5.0 %all-to-all-start.3 = ((bf16[4,4,12,16,512]{4,3,1,2,0:T(8,128)(2,1)}), bf16[4,4,12,16,512]{4,3,1,2,0:T(8,128)(2,1)}, u32[]{:S(2)}, u32[]{:S(2)}) async-start(bf16[4,4,12,16,512]{4,3,1,2,0:T(8,128)(2,1)} %broadcast_in_dim.58), calls=%async_computation.3 | async-start | bytes 6291456 | tf_op jit(solution)/shard_map/all_to_all | solution.py:65
  183.9 9.9 %shard_map.46 = (bf16[6,256,256]{2,1,0:T(8,128)(2,1)S(1)}, bf16[6,256,256]{2,1,0:T(8,128)(2,1)S(1)}) custom-call(f32[6,256,256]{2,1,0:T(8,128)S(1)} %copy-done), custom_call_target="tpu_custom_call" | custom-call | flops 8455716864 | bytes 3145728 | tf_op jit(solution)/shard_map/pallas_call | solution.py:54
  200.7 2.1 select_bitcast_fusion.3
  204.8 10.8 %all-to-all-done.3 = bf16[4,4,12,16,512]{4,3,1,2,0:T(8,128)(2,1)} async-done(((bf16[4,4,12,16,512]{4,3,1,2,0:T(8,128)(2,1)}), bf16[4,4,12,16,512]{4,3,1,2,0:T(8,128)(2,1)}, u32[]{:S(2)}, u32[]{:S(2)}) %all-to-all-start.3) | async-done | bytes 3145760 | tf_op jit(solution)/shard_map/all_to_all | solution.py:65
  215.6 2.3 copy.37
  226.3 2.7 convolution_convert_fusion.1
  231.0 2.1 fusion.61
  254.3 2.8 %convolution_convert_fusion.2 = bf16[1024,512]{1,0:T(8,128)(2,1)} fusion(f32[256,512]{1,0:T(8,128)} %fusion.66, bf16[512,256]{0,1:T(8,128)(2,1)S(1)} %get-tuple-element.50, s32[256]{0:T(256)S(1)} %bitcast.432, s32[1024]{0:T(1024)S(1)} %iota_add_fusion.2, bf16[15,2,256,256]{3,2,1,0:T(8,128)(2,1)} %bitcast.384), kind=kOutput, calls=%fused_computation.25 | convolution fusion | flops 336592896 | bytes 1971200 | tf_op jit(solution)/shard_map/dot_general | solution.py:22
  258.5 2.5 convolution_convert_fusion.3
  263.5 2.5 convolution_convert_fusion.4
  270.5 2.7 convolution_convert_fusion.5
  273.3 2.1 bitcast_dynamic-update-slice_fusion
  275.4 2.2 fusion.8
  (186 shorter events, 78.9 us)
Async XLA Ops:
  1.9 30.2 %all-to-all-start.4 = ((bf16[8,6,32,256]{3,2,1,0:T(8,128)(2,1)}), bf16[8,6,32,256]{3,2,1,0:T(8,128)(2,1)S(1)}, u32[]{:S(2)}, u32[]{:S(2)}) async-start(bf16[8,6,32,256]{3,2,1,0:T(8,128)(2,1)} %broadcast_in_dim.59), calls=%async_computation.4 | async-start | bytes 1572864 | tf_op jit(solution)/shard_map/all_to_all | solution.py:65
  32.1 17.3 %copy-start.21 = (bf16[1024,512]{1,0:T(8,128)(2,1)S(1)}, bf16[1024,512]{1,0:T(8,128)(2,1)}, u32[]{:S(2)}) copy-start(bf16[1024,512]{1,0:T(8,128)(2,1)} %param.4) | copy-start | bytes 3145732
  34.1 10.1 %all-to-all-start.5 = ((bf16[4,15,2,8,256]{4,3,2,1,0:T(8,128)(2,1)}), bf16[4,15,2,8,256]{4,3,2,1,0:T(8,128)(2,1)S(1)}, u32[]{:S(2)}, u32[]{:S(2)}) async-start(bf16[4,15,2,8,256]{4,3,2,1,0:T(8,128)(2,1)} %bitcast.363), calls=%async_computation.5 | async-start | bytes 983040 | tf_op jit(solution)/shard_map/all_to_all | solution.py:65
  45.1 13.5 %all-to-all-start.6 = ((bf16[4,15,2,8,256]{4,3,2,1,0:T(8,128)(2,1)}), bf16[4,15,2,8,256]{4,3,2,1,0:T(8,128)(2,1)S(1)}, u32[]{:S(2)}, u32[]{:S(2)}) async-start(bf16[4,15,2,8,256]{4,3,2,1,0:T(8,128)(2,1)} %broadcast_in_dim.60), calls=%async_computation.6 | async-start | bytes 983040 | tf_op jit(solution)/shard_map/all_to_all | solution.py:65
  58.6 26.0 %all-to-all-start = ((bf16[4,7,64,512]{3,2,1,0:T(8,128)(2,1)}), bf16[4,7,64,512]{3,2,1,0:T(8,128)(2,1)S(1)}, u32[]{:S(2)}, u32[]{:S(2)}) async-start(bf16[4,7,64,512]{3,2,1,0:T(8,128)(2,1)} %pad_maximum_fusion.2), calls=%async_computation | async-start | bytes 3670016 | tf_op jit(solution)/shard_map/all_to_all | solution.py:65
  85.4 20.2 %all-to-all-start.7 = ((bf16[4,15,2,8,256]{4,3,2,1,0:T(8,128)(2,1)}), bf16[4,15,2,8,256]{4,3,2,1,0:T(8,128)(2,1)S(1)}, u32[]{:S(2)}, u32[]{:S(2)}) async-start(bf16[4,15,2,8,256]{4,3,2,1,0:T(8,128)(2,1)} %broadcast_in_dim.61), calls=%async_computation.7 | async-start | bytes 983040 | tf_op jit(solution)/shard_map/all_to_all | solution.py:65
  105.6 18.0 %all-to-all-start.1 = ((bf16[4,10,16,512]{3,2,1,0:T(8,128)(2,1)}), bf16[4,10,16,512]{3,2,1,0:T(8,128)(2,1)S(1)}, u32[]{:S(2)}, u32[]{:S(2)}) async-start(bf16[4,10,16,512]{3,2,1,0:T(8,128)(2,1)} %copy.35), calls=%async_computation.1 | async-start | bytes 1310720 | tf_op jit(solution)/shard_map/all_to_all | solution.py:65
  124.6 26.1 %all-to-all-start.8 = ((bf16[8,15,2,8,256]{4,3,2,1,0:T(8,128)(2,1)}), bf16[8,15,2,8,256]{4,3,2,1,0:T(8,128)(2,1)S(1)}, u32[]{:S(2)}, u32[]{:S(2)}) async-start(bf16[8,15,2,8,256]{4,3,2,1,0:T(8,128)(2,1)} %broadcast_in_dim.62), calls=%async_computation.8 | async-start | bytes 1966080 | tf_op jit(solution)/shard_map/all_to_all | solution.py:65
  128.2 33.5 %collective-permute-start.2 = (bf16[8,6,32,256]{3,2,0,1:T(8,128)(2,1)S(1)}, bf16[8,6,32,256]{3,2,0,1:T(8,128)(2,1)}, u32[]{:S(2)}, u32[]{:S(2)}) collective-permute-start(bf16[8,6,32,256]{3,2,0,1:T(8,128)(2,1)S(1)} %copy.49), channel_id=1, source_target_pairs={{0,2},{2,0},{1,3},{3,1},{4,6},{6,4},{5,7},{7,5},{8,10},{10,8},{9,1... | collective-permute-start | bytes 2359304 | tf_op jit(solution)/shard_map/ppermute | solution.py:78
  150.7 12.3 %copy-start.3 = (bf16[8,15,2,8,256]{4,3,2,1,0:T(8,128)(2,1)}, bf16[8,15,2,8,256]{4,3,2,1,0:T(8,128)(2,1)S(1)}, u32[]{:S(2)}) copy-start(bf16[8,15,2,8,256]{4,3,2,1,0:T(8,128)(2,1)S(1)} %all-to-all-done.8) | copy-start | bytes 2949124
  151.9 24.9 %all-to-all-start.2 = ((bf16[4,12,16,512]{3,2,1,0:T(8,128)(2,1)}), bf16[4,12,16,512]{3,2,1,0:T(8,128)(2,1)S(1)}, u32[]{:S(2)}, u32[]{:S(2)}) async-start(bf16[4,12,16,512]{3,2,1,0:T(8,128)(2,1)} %broadcast_in_dim.54), calls=%async_computation.2 | async-start | bytes 1572864 | tf_op jit(solution)/shard_map/all_to_all | solution.py:65
  159.9 34.0 %collective-permute-start = (bf16[8,15,2,8,256]{4,3,0,2,1:T(8,128)(2,1)}, bf16[8,15,2,8,256]{4,3,0,2,1:T(8,128)(2,1)}, u32[]{:S(2)}, u32[]{:S(2)}) collective-permute-start(bf16[8,15,2,8,256]{4,3,0,2,1:T(8,128)(2,1)} %copy.44), channel_id=1, source_target_pairs={{0,2},{2,0},{1,3},{3,1},{4,6},{6,4},{5,7},{7,5},{8,10},{10,8},{9,1... | collective-permute-start | bytes 2949128 | tf_op jit(solution)/shard_map/ppermute | solution.py:78
  163.1 2.2 copy-start.8
  165.3 35.5 %collective-permute-start.3 = (bf16[2,8,6,32,256]{4,3,0,1,2:T(8,128)(2,1)}, bf16[2,8,6,32,256]{4,3,0,1,2:T(8,128)(2,1)}, u32[]{:S(2)}, u32[]{:S(2)}) collective-permute-start(bf16[2,8,6,32,256]{4,3,0,1,2:T(8,128)(2,1)} %pad_maximum_fusion.3), channel_id=1, source_target_pairs={{0,1},{1,0},{2,3},{3,2},{4,5},{5,4},{6,7},{7,6},{8,9},{9,8},{10,11... | collective-permute-start | bytes 4718600 | tf_op jit(solution)/shard_map/ppermute | solution.py:78
  178.9 5.0 %copy-start = (f32[6,256,256]{2,1,0:T(8,128)S(1)}, f32[6,256,256]{2,1,0:T(8,128)}, u32[]{:S(2)}) copy-start(f32[6,256,256]{2,1,0:T(8,128)} %l_ref.1) | copy-start | bytes 4718596
  178.9 36.7 %all-to-all-start.3 = ((bf16[4,4,12,16,512]{4,3,1,2,0:T(8,128)(2,1)}), bf16[4,4,12,16,512]{4,3,1,2,0:T(8,128)(2,1)}, u32[]{:S(2)}, u32[]{:S(2)}) async-start(bf16[4,4,12,16,512]{4,3,1,2,0:T(8,128)(2,1)} %broadcast_in_dim.58), calls=%async_computation.3 | async-start | bytes 6291456 | tf_op jit(solution)/shard_map/all_to_all | solution.py:65
  183.9 9.9 %copy-start.4 = (bf16[8,15,2,8,256]{4,3,2,1,0:T(8,128)(2,1)S(1)}, bf16[8,15,2,8,256]{4,3,2,1,0:T(8,128)(2,1)}, u32[]{:S(2)}) copy-start(bf16[8,15,2,8,256]{4,3,2,1,0:T(8,128)(2,1)} %copy-done.3) | copy-start | bytes 2949124
  193.8 5.8 %copy-start.23 = (s32[6,256]{1,0:T(8,128)S(1)}, s32[6,256]{1,0:T(8,128)}, u32[]{:S(2)}) copy-start(s32[6,256]{1,0:T(8,128)} %param.7) | copy-start | bytes 18436
  197.7 23.4 %collective-permute-start.1 = (bf16[2,8,15,2,8,256]{5,4,0,1,3,2:T(8,128)(2,1)}, bf16[2,8,15,2,8,256]{5,4,0,1,3,2:T(8,128)(2,1)}, u32[]{:S(2)}, u32[]{:S(2)}) collective-permute-start(bf16[2,8,15,2,8,256]{5,4,0,1,3,2:T(8,128)(2,1)} %pad_maximum_fusion.1), channel_id=1, source_target_pairs={{0,1},{1,0},{2,3},{3,2},{4,5},{5,4},{6,7},{7,6},{8,9},{9,8},{10,11... | collective-permute-start | bytes 5898248 | tf_op jit(solution)/shard_map/ppermute | solution.py:78
  215.6 3.5 %copy-start.22 = (bf16[1024,512]{1,0:T(8,128)(2,1)S(1)}, bf16[1024,512]{1,0:T(8,128)(2,1)}, u32[]{:S(2)}) copy-start(bf16[1024,512]{1,0:T(8,128)(2,1)} %param.4) | copy-start | bytes 3145732
  217.9 8.1 %copy-start.2 = (bf16[12,4,4,16,512]{4,3,2,1,0:T(8,128)(2,1)}, bf16[12,4,4,16,512]{4,3,2,1,0:T(8,128)(2,1)S(1)}, u32[]{:S(2)}) copy-start(bf16[12,4,4,16,512]{4,3,2,1,0:T(8,128)(2,1)S(1)} %copy.37) | copy-start | bytes 9437188
  218.0 3.1 %copy-start.6 = (bf16[1,8,15,2,8,256]{5,4,0,1,3,2:T(8,128)(2,1)S(1)}, bf16[1,8,15,2,8,256]{5,4,0,1,3,2:T(8,128)(2,1)}, u32[]{:S(2)}) copy-start(bf16[1,8,15,2,8,256]{5,4,0,1,3,2:T(8,128)(2,1)} %copy-done.5) | copy-start | bytes 2949124
  223.2 2.8 copy-start.1
  231.0 7.3 %copy-start.20 = (f32[256,512]{1,0:T(8,128)S(1)}, f32[256,512]{1,0:T(8,128)}, u32[]{:S(2)}) copy-start(f32[256,512]{1,0:T(8,128)} %fusion.36) | copy-start | bytes 1572868
  237.2 3.7 %copy-start.19 = (f32[256,512]{1,0:T(8,128)S(1)}, f32[256,512]{1,0:T(8,128)}, u32[]{:S(2)}) copy-start(f32[256,512]{1,0:T(8,128)} %fusion.24) | copy-start | bytes 1572868
  267.4 8.0 %copy-start.17 = (bf16[1,8,2,2,32,256]{5,4,3,2,1,0:T(8,128)(2,1)S(1)}, bf16[1,8,2,2,32,256]{5,4,3,2,1,0:T(8,128)(2,1)}, u32[]{:S(2)}) copy-start(bf16[1,8,2,2,32,256]{5,4,3,2,1,0:T(8,128)(2,1)} %get-tuple-element.22) | copy-start | bytes 1572868
  273.2 4.3 %copy-start.10 = (bf16[1024,512]{1,0:T(8,128)(2,1)S(1)}, bf16[1024,512]{1,0:T(8,128)(2,1)}, u32[]{:S(2)}) copy-start(bf16[1024,512]{1,0:T(8,128)(2,1)} %convolution_convert_fusion.2) | copy-start | bytes 3145732
  273.2 4.3 %copy-start.16 = (bf16[1,8,2,2,32,256]{5,4,3,2,1,0:T(8,128)(2,1)S(1)}, bf16[1,8,2,2,32,256]{5,4,3,2,1,0:T(8,128)(2,1)}, u32[]{:S(2)}) copy-start(bf16[1,8,2,2,32,256]{5,4,3,2,1,0:T(8,128)(2,1)} %get-tuple-element.21) | copy-start | bytes 1572868
  275.4 2.8 copy-start.9
  275.4 2.8 copy-start.15
  277.6 1.3 copy-start.14
  278.2 1.5 copy-start.13
  (6 other events, 6.6 us)

commit v2 on v1

v2 whole, which is shorter than its diff:
```python
import jax
import jax.numpy as jnp
from jax import lax
from jax.experimental import pallas as pl
from jax.experimental.pallas import tpu as pltpu
from jax.sharding import Mesh
from jax.sharding import PartitionSpec as P

STEPS = 6
NB = 256
ROWS = 1024
FINE = ("zh", "x", "y", "zl", "c")
PAIRS = [(s, k) for k in range(STEPS) for s in range(k + 1, STEPS)] + [(0, 0)]
PLACE = {pair: n for n, pair in enumerate(PAIRS)}
SLOTS = 32


def split(v):
    high = v.astype(jnp.bfloat16)
    return high, (v - high.astype(jnp.float32)).astype(jnp.bfloat16)


def dot(a, b):
    return jnp.dot(a, b, preferred_element_type=jnp.float32)


def dot3(a, b):
    ah, al = split(a)
    bh, bl = split(b)
    return dot(ah, bh) + (dot(ah, bl) + dot(al, bh))


def inverse_kernel(l_ref, high_ref, low_ref):
    row = lax.broadcasted_iota(jnp.int32, (NB, NB), 0)
    col = lax.broadcasted_iota(jnp.int32, (NB, NB), 1)
    eye = (row == col).astype(jnp.float32)
    lower = [l_ref[s] for s in range(STEPS)]
    inv = [eye] * STEPS
    size = 1
    while size < NB:
        joins = (row // (2 * size) == col // (2 * size)) & (row // size > col // size)
        parts = [jnp.where(joins, m, 0.0) for m in lower]
        if size == 1:
            inv = [eye - m for m in parts]
        else:
            left = [dot3(m, x) for m, x in zip(parts, inv)]
            inv = [x - dot3(x, m) for x, m in zip(inv, left)]
        size *= 2
    for s in range(STEPS):
        high_ref[s], low_ref[s] = split(inv[s])


def inverses(diag_blocks):
    out = jax.ShapeDtypeStruct((STEPS, NB, NB), jnp.bfloat16)
    spec = pl.BlockSpec(memory_space=pltpu.VMEM)
    return pl.pallas_call(
        inverse_kernel,
        out_shape=(out, out),
        in_specs=[spec],
        out_specs=(spec, spec),
        compiler_params=pltpu.CompilerParams(vmem_limit_bytes=48 * 2**20),
        cost_estimate=pl.CostEstimate(flops=2 * 42 * 6 * NB**3, bytes_accessed=3 * 2**20, transcendentals=0),
    )(diag_blocks)


def exchange(v, axis):
    return lax.all_to_all(v, axis, 0, 0)


def everyone(v, axis):
    n = lax.axis_size(axis)
    return exchange(jnp.broadcast_to(v[None], (n,) + v.shape), axis)


def add_up(v):
    return jnp.sum(v.astype(jnp.float32), axis=0).astype(v.dtype)


def shift(v, axis, by):
    n = lax.axis_size(axis)
    return lax.ppermute(v, axis, [(i, (i + by) % n) for i in range(n)])


def dealt(v, axis):
    n, at = lax.axis_size(axis), lax.axis_index(axis)
    parts = [lax.dynamic_index_in_dim(v, (at + d) % n, 0, keepdims=False) for d in range(n)]
    return parts[:1] + [shift(parts[d], axis, d) for d in range(1, n)]


def passed(v, axis):
    return [v] + [shift(v, axis, d) for d in range(1, lax.axis_size(axis))]


def picks(ids, held):
    return (ids[:, None] == held[None, :]).astype(jnp.bfloat16)


def l_rows_kernel(at_ref, ts_ref, ks_ref, ids_ref, panels_ref, out_ref):
    zh, x, zl, c = at_ref[0], at_ref[1], at_ref[2], at_ref[3]
    lane = lax.broadcasted_iota(jnp.int32, (NB, 64), 0)
    held = (zh * 4 + x) * ROWS + zl * 64 + c * 32 + lane // 32 * 128 + lane % 32
    for m in range(8):
        t, k = ts_ref[m], ks_ref[m]
        put = jnp.where(held == ids_ref[pl.ds(k * STEPS + t, 1), :], 1.0, 0.0).astype(jnp.bfloat16)
        mine = panels_ref[:, pl.ds(k, 1)].reshape(NB, NB)
        rows = lax.dot_general(put, mine, (((0,), (0,)), ((), ())), preferred_element_type=jnp.float32)
        out_ref[:, m // 2, :, m % 2 * NB : m % 2 * NB + NB] = rows.astype(jnp.bfloat16).reshape(4, 16, NB)


def l_rows(at, ts, ks, ids, panels):
    vmem, smem = pl.BlockSpec(memory_space=pltpu.VMEM), pl.BlockSpec(memory_space=pltpu.SMEM)
    return pl.pallas_call(
        l_rows_kernel,
        out_shape=jax.ShapeDtypeStruct((4, 4, 16, 2 * NB), jnp.bfloat16),
        in_specs=[smem, smem, smem, vmem, vmem],
        out_specs=vmem,
        compiler_params=pltpu.CompilerParams(vmem_limit_bytes=16 * 2**20),
        cost_estimate=pl.CostEstimate(flops=2 * 8 * 64 * NB * NB, bytes_accessed=2**20, transcendentals=0),
    )(at, ts, ks, ids, panels)


def turned(zl, c, n):
    return lax.rem(zl + n // 2, 2), lax.rem(c + n % 2, 2)


def solve_kernel(at_ref, slot_ref, high_ref, low_ref, diag_ref, *refs):
    active_in, blocks_in, panels_in = refs[:4], refs[4:8], refs[8:12]
    u_ref, old_ref, send_ref, active, blocks, panels, active_sem, blocks_sem, panels_sem = refs[12:]
    zh, x, zl, c = at_ref[0], at_ref[1], at_ref[2], at_ref[3]
    me = zh * 4 + x
    width = diag_ref.shape[1]
    copies = []
    for d in range(4):
        for e in range(4):
            target = active.at[lax.rem(x - d + 4, 4), lax.rem(zh - e + 4, 4)]
            copies.append(pltpu.make_async_copy(active_in[d].at[e], target, active_sem.at[d * 4 + e]))
    for n in range(4):
        a, b = turned(zl, c, n)
        copies.append(pltpu.make_async_copy(blocks_in[n], blocks.at[:, a, b], blocks_sem.at[n]))
        copies.append(pltpu.make_async_copy(panels_in[n].at[0:2], panels.at[:, a, b], panels_sem.at[n]))
    for copy in copies:
        copy.start()
    for copy in copies:
        copy.wait()

    def rows_of(n):
        return active[:, :, n].reshape(NB, width)

    old_ref[...] = diag_ref[...]
    for s in range(STEPS):
        top = rows_of(s)
        u = (dot(high_ref[s], top) + dot(low_ref[s], top)).astype(jnp.bfloat16)
        u_ref[s] = u
        for t in range(s + 1, STEPS):
            n = PLACE[(t, s)]
            left = n // 2 % 2 * NB
            block = blocks[n % 2 * 4 : n % 2 * 4 + 4, :, :, n // 4, :, left : left + NB].reshape(NB, NB)
            less = rows_of(t).astype(jnp.float32) - dot(block, u)
            active[:, :, t] = less.astype(jnp.bfloat16).reshape(4, 4, 16, width)

        @pl.when(s < me)
        def _():
            panel = panels[:, :, :, s].reshape(NB, NB)
            old_ref[...] = (old_ref[...].astype(jnp.float32) - dot(panel, u)).astype(jnp.bfloat16)

    slot = lax.broadcasted_iota(jnp.int32, (16 * SLOTS, NB), 0)
    put = jnp.where(slot == slot_ref[...], 1.0, 0.0).astype(jnp.bfloat16)
    send_ref[...] = dot(put, old_ref[...]).astype(jnp.bfloat16)


def solve(at, slot, high, low, diag, active, blocks, panels):
    width = diag.shape[1]
    vmem, anywhere = pl.BlockSpec(memory_space=pltpu.VMEM), pl.BlockSpec(memory_space=pl.ANY)
    return pl.pallas_call(
        solve_kernel,
        out_shape=(
            jax.ShapeDtypeStruct((STEPS, NB, width), jnp.bfloat16),
            jax.ShapeDtypeStruct((NB, width), jnp.bfloat16),
            jax.ShapeDtypeStruct((16 * SLOTS, width), jnp.bfloat16),
        ),
        in_specs=[pl.BlockSpec(memory_space=pltpu.SMEM)] + [vmem] * 4 + [anywhere] * 12,
        out_specs=(vmem,) * 3,
        scratch_shapes=[
            pltpu.VMEM((4, 4, STEPS, 16, width), jnp.bfloat16),
            pltpu.VMEM((8, 2, 2, 4, 16, 2 * NB), jnp.bfloat16),
            pltpu.VMEM((2, 2, 2, STEPS, 32, NB), jnp.bfloat16),
            pltpu.SemaphoreType.DMA((16,)),
            pltpu.SemaphoreType.DMA((4,)),
            pltpu.SemaphoreType.DMA((4,)),
        ],
        compiler_params=pltpu.CompilerParams(vmem_limit_bytes=58 * 2**20),
        cost_estimate=pl.CostEstimate(flops=2 * 35 * NB * NB * width, bytes_accessed=9 * 2**20, transcendentals=0),
    )(at, slot, high, low, diag, *active, *blocks, *panels)


def update_kernel(at_ref, last_ref, u_ref, matrix_ref, *refs):
    panels_in, (out_ref, panels, panels_sem) = refs[:4], refs[4:]
    zl, c = at_ref[2], at_ref[3]
    width = matrix_ref.shape[1]
    copies = []
    for n in range(4):
        a, b = turned(zl, c, n)
        copies.append(pltpu.make_async_copy(panels_in[n], panels.at[:, a, b], panels_sem.at[n]))
    for copy in copies:
        copy.start()
    for copy in copies:
        copy.wait()
    tall = 256

    @pl.loop(0, ROWS // tall)
    def _(i):
        span = pl.ds(pl.multiple_of(i * tall, tall), tall)
        last = jnp.concatenate([last_ref[span, :]] * (width // 128), axis=1)
        rows = matrix_ref[span, :].astype(jnp.float32)
        for s in range(STEPS):
            panel = panels[pl.ds(i * (tall // 128), tall // 128), :, :, s].reshape(tall, NB)
            rows = jnp.where(last == s, 0.0, rows) - dot(panel, u_ref[s])
            rows = jnp.where(last >= 0, rows, rows.astype(jnp.bfloat16).astype(jnp.float32))
        out_ref[span, :] = rows


def update(at, last, u, matrix, panels):
    vmem, anywhere = pl.BlockSpec(memory_space=pltpu.VMEM), pl.BlockSpec(memory_space=pl.ANY)
    return pl.pallas_call(
        update_kernel,
        out_shape=jax.ShapeDtypeStruct(matrix.shape, jnp.float32),
        in_specs=[pl.BlockSpec(memory_space=pltpu.SMEM)] + [vmem] * 3 + [anywhere] * 4,
        out_specs=vmem,
        scratch_shapes=[pltpu.VMEM((8, 2, 2, STEPS, 32, NB), jnp.bfloat16), pltpu.SemaphoreType.DMA((4,))],
        compiler_params=pltpu.CompilerParams(vmem_limit_bytes=58 * 2**20),
        cost_estimate=pl.CostEstimate(
            flops=2 * matrix.size * STEPS * NB, bytes_accessed=8 * 2**20, transcendentals=0
        ),
    )(at, last, u, matrix, *panels)


def place_kernel(at_ref, own_ref, put_ref, got_ref, total_ref, out_ref):
    me = at_ref[0] * 4 + at_ref[1]
    width = out_ref.shape[1]
    got = got_ref[0:STEPS].reshape(STEPS * SLOTS, width)
    out_ref[...] = (total_ref[...] + dot(put_ref[...], got)).astype(jnp.bfloat16)

    @pl.when(me < STEPS)
    def _():
        out_ref[0:NB, :] = own_ref[pl.ds(jnp.minimum(me, STEPS - 1), 1)].reshape(NB, width)


def place(at, u, put, got, total):
    vmem = pl.BlockSpec(memory_space=pltpu.VMEM)
    return pl.pallas_call(
        place_kernel,
        out_shape=jax.ShapeDtypeStruct(total.shape, jnp.bfloat16),
        in_specs=[pl.BlockSpec(memory_space=pltpu.SMEM)] + [vmem] * 4,
        out_specs=vmem,
        compiler_params=pltpu.CompilerParams(vmem_limit_bytes=32 * 2**20),
        cost_estimate=pl.CostEstimate(
            flops=2 * total.size * STEPS * SLOTS, bytes_accessed=6 * 2**20, transcendentals=0
        ),
    )(at, u, put, got, total)


def body(matrix, panels, diag_blocks, pivots):
    width = matrix.shape[1]
    zh, x, y = lax.axis_index("zh"), lax.axis_index("x"), lax.axis_index("y")
    zl, c = lax.axis_index("zl"), lax.axis_index("c")
    at = jnp.stack([zh, x, zl, c]).astype(jnp.int32)
    me = zh * 4 + x
    local = me * ROWS + jnp.arange(ROWS, dtype=jnp.int32)
    t_ids = jnp.arange(STEPS, dtype=jnp.int32)
    i_ids = jnp.arange(NB, dtype=jnp.int32)

    wide, pivots, matrix = lax.optimization_barrier((jnp.broadcast_to(panels, (8,) + panels.shape), pivots, matrix))
    by_y = exchange(wide, "y")

    same = pivots[:, :, None, None] == pivots[None, None]
    before = (t_ids[None, :] < t_ids[:, None])[:, None, :, None]
    code = jnp.where(same & before, t_ids[:, None] * ROWS + i_ids[None, :], -1)
    origin = jnp.max(code, axis=(2, 3))
    base = jnp.where(origin >= 0, origin, pivots)

    picked = dot(picks(base.reshape(-1), local), matrix).astype(jnp.bfloat16)
    active = sum(dealt(picked.reshape(STEPS, 4, 64, width).transpose(1, 0, 2, 3), "x"))
    active = active.reshape(STEPS, 4, 16, width).transpose(1, 0, 2, 3)

    pair = jnp.array(PAIRS, jnp.int32).reshape(8, 2, 2)
    pair = lax.dynamic_index_in_dim(pair, y // 4, 1, keepdims=False)
    swapped_at = jnp.where(origin >= 0, origin // ROWS, -1)
    ids = jnp.where(swapped_at[None] > t_ids[:, None, None], origin[None], pivots[None])
    ids = lax.dynamic_slice_in_dim(ids.reshape(STEPS * STEPS, NB), y % 4 * 64, 64, 1)
    rows = l_rows(at, pair[:, 0], pair[:, 1], ids, by_y)

    across = shift(by_y, "zl", 1)
    high, low = inverses(diag_blocks)
    chunk = add_up(exchange(rows, ("zl", "c")))
    chunk = add_up(everyone(chunk, "x"))
    active, chunk, across, high, low, pivots = lax.optimization_barrier((active, chunk, across, high, low, pivots))
    both = jnp.concatenate([jnp.broadcast_to(chunk, (4,) + chunk.shape), active], axis=1)
    both = exchange(both, "zh")
    chunk, active = add_up(both[:, :4]), add_up(both[:, 4:])
    active = jnp.stack(passed(active, "zh"))
    chunk = everyone(chunk, "y")
    whole = [by_y, shift(by_y, "c", 1), across, shift(across, "c", 1)]
    active, chunk, whole[1], whole[3] = lax.optimization_barrier((active, chunk, whole[1], whole[3]))
    active = passed(active, "x")
    across = shift(chunk, "zl", 1)
    beside = shift(chunk, "c", 1)
    active[1], active[2], active[3], across = lax.optimization_barrier((*active[1:], across))
    blocks = [chunk, beside, across, shift(across, "c", 1)]

    same = pivots[:, :, None, None] == pivots[None, None]
    after = (t_ids[None, :] > t_ids[:, None])[:, None, :, None]
    stays = ~jnp.any(same & after, axis=(2, 3))
    owner = jnp.where(stays, pivots // ROWS, -1)
    ahead = (owner[:, :, None] == owner[:, None, :]) & (i_ids[None, :] < i_ids[:, None])
    rank = jnp.where(stays, jnp.sum(ahead, axis=2, dtype=jnp.int32), -1)
    rounds = (jnp.max(rank) + SLOTS) // SLOTS
    here = (pivots.reshape(-1)[None, :] == local[:, None]) & stays.reshape(-1)[None, :]
    tag = jnp.max(jnp.where(here, (t_ids[:, None] * NB + rank).reshape(-1)[None, :], -1), axis=1)
    last = jnp.where(tag >= 0, tag // NB, -1)
    at_rank = jnp.where(tag >= 0, tag % NB, -1)
    mine = jnp.minimum(me, STEPS - 1)
    my_rank = jnp.where(me < STEPS, lax.dynamic_index_in_dim(rank, mine, 0, keepdims=False), -1)
    my_owner = lax.dynamic_index_in_dim(owner, mine, 0, keepdims=False)

    def slots(q):
        n = my_rank - q * SLOTS
        return jnp.where((n >= 0) & (n < SLOTS), my_owner * SLOTS + n, -1)

    def landing(q):
        n = at_rank - q * SLOTS
        return picks(jnp.where((n >= 0) & (n < SLOTS), last * SLOTS + n, -1), jnp.arange(STEPS * SLOTS, dtype=jnp.int32))

    def deliver(sent):
        return exchange(sent.reshape(16, SLOTS, width), ("zh", "x"))

    u, old, send = solve(at, slots(0)[None], high, low, matrix[:NB], active, blocks, whole)
    total = update(at, jnp.broadcast_to(last[:, None], (ROWS, 128)), u, matrix, whole)
    got = deliver(send)
    total, got = lax.optimization_barrier((total, got))

    def more(state):
        q, total = state
        sent = dot(picks(jnp.arange(16 * SLOTS, dtype=jnp.int32), slots(q)), old).astype(jnp.bfloat16)
        got = deliver(sent)[:STEPS].reshape(STEPS * SLOTS, width)
        return q + 1, total + dot(landing(q), got)

    _, total = lax.while_loop(lambda state: state[0] < rounds, more, (jnp.int32(1), total))
    return place(at, u, landing(0), got, total)


def solution(mesh):
    fine = Mesh(mesh.devices.reshape(4, 4, 8, 2, 2), FINE)
    prow, pcol = ("zh", "x"), ("y", "zl", "c")
    return jax.shard_map(
        body,
        mesh=fine,
        in_specs=(P(prow, pcol), P(None, prow + pcol, None), P(), P()),
        out_specs=P(prow, pcol),
        check_vma=False,
    )
```

time: 284 us -> 204 us (0.72)
  the two profiles are of different devices: /device:TPU:192 before, /device:TPU:1 now
where the time goes in v2:
time: 204 us; the launch traced here: 202 us
  starting transfers between devices  85.9 us (42%)
  waiting for transfers between devices  33.8 us (17%)
  Pallas kernels  31.4 us (15%)
  blocking collectives  21.5 us (11%)
  local copies, waits for them, and re-layouts  13.2 us (6%)
  other arithmetic  12.2 us (6%)
  matrix products  3.04 us (1%)
    ppermute x15, starting transfers between devices, shift(): return lax.ppermute(v, axis, [(i, (i + by) % n) for i in range(n)])  58.2 us
    all_to_all x5, starting transfers between devices, exchange(): return lax.all_to_all(v, axis, 0, 0)  27.6 us
    all_to_all x1, blocking collectives, exchange(): return lax.all_to_all(v, axis, 0, 0)  21.5 us
    ppermute x15, waiting for transfers between devices, shift(): return lax.ppermute(v, axis, [(i, (i + by) % n) for i in range(n)])  17.9 us
    all_to_all x5, waiting for transfers between devices, exchange(): return lax.all_to_all(v, axis, 0, 0)  15.9 us
    pallas_call x1, Pallas kernels, inverses(): pl.pallas_call(inverse_kernel, out_shape=(out, out), in_specs=[spec], out...  9.88 us
    pallas_call x1, Pallas kernels, solve(): pl.pallas_call(solve_kernel, out_shape=(jax.ShapeDtypeStruct((STEPS, NB,...  8.89 us
    pallas_call x1, Pallas kernels, update(): pl.pallas_call(update_kernel, out_shape=jax.ShapeDtypeStruct(matrix.shape...  8.01 us
  transfers between devices with their start and end apart: 20, of which 9 were waited for; matrix products, arithmetic and copies ran while one was open for 9% of the time, Pallas kernels for 10%

profile of v2, /device:TPU:1, one launch (start us, length us, event | category | flops | bytes accessed | tf_op | source)
XLA Modules:
  0.0 202.3 jit_solution(15485673613767493388)
XLA Ops:
  2.0 3.2 %select_reduce_fusion = s32[6,256]{1,0:T(8,128)S(1)} fusion(s32[6,256]{1,0:T(8,128)S(1)} %iota_add_fusion, s32[6,256]{1,0:T(8,128)} %param.10, pred[6,6]{1,0:T(8,128)(4,1)S(1)} %iota_compare_fusion.7), kind=kLoop, calls=%fused_computation.8 | loop fusion | flops 9435648 | bytes 18468 | tf_op jit(solution)/shard_map/reduce_max | solution.py:278
  5.3 7.7 %all-to-all-start.1 = ((bf16[8,6,32,256]{3,2,1,0:T(8,128)(2,1)}), bf16[8,6,32,256]{3,2,1,0:T(8,128)(2,1)S(1)}, u32[]{:S(2)}, u32[]{:S(2)}) async-start(bf16[8,6,32,256]{3,2,1,0:T(8,128)(2,1)} %broadcast_in_dim.73), calls=%async_computation.1 | async-start | bytes 1572864 | tf_op jit(solution)/shard_map/all_to_all | solution.py:67
  13.1 3.0 %fusion.6 = bf16[1536,512]{1,0:T(8,128)(2,1)} fusion(bf16[1024,512]{1,0:T(8,128)(2,1)S(1)} %copy-done.9, s32[1024]{0:T(1024)S(1)} %iota_add_fusion.1, s32[1536]{0:T(1024)S(1)} %eq.119), kind=kOutput, calls=%fused_computation.15 | convolution fusion | flops 1612972032 | bytes 2631680 | tf_op jit(solution)/shard_map/dot_general | solution.py:24
  16.1 2.4 %dynamic-slice_bitcast_fusion.2 = (bf16[6,64,512]{2,1,0:T(8,128)(2,1)}, bf16[6,64,512]{2,1,0:T(8,128)(2,1)}, bf16[6,64,512]{2,1,0:T(8,128)(2,1)}) fusion(bf16[6,4,64,512]{3,2,1,0:T(8,128)(2,1)} %bitcast.6, s32[]{:T(128)S(6)} %select_n.188, s32[]{:T(128)S(6)} %select_n.192, s32[]{:T(128)S(6)} %select_n.190), kind=kLoop, calls=%fused_computation.27 | loop fusion | bytes 2359308 | tf_op jit(solution)/shard_map/jit(dynamic_index_in_dim)/squeeze | solution.py:86
  18.5 4.4 %collective-permute-start.2 = (bf16[6,64,512]{2,1,0:T(8,128)(2,1)}, bf16[6,64,512]{2,1,0:T(8,128)(2,1)}, u32[]{:S(2)}, u32[]{:S(2)}) collective-permute-start(bf16[6,64,512]{2,1,0:T(8,128)(2,1)} %get-tuple-element.119), channel_id=1, source_target_pairs={{0,96},{32,0},{64,32},{96,64},{1,97},{33,1},{65,33},{97,65},{2,98}... | collective-permute-start | bytes 1179656 | tf_op jit(solution)/shard_map/ppermute | solution.py:81
  22.9 2.4 %collective-permute-start.1 = (bf16[6,64,512]{2,1,0:T(8,128)(2,1)}, bf16[6,64,512]{2,1,0:T(8,128)(2,1)}, u32[]{:S(2)}, u32[]{:S(2)}) collective-permute-start(bf16[6,64,512]{2,1,0:T(8,128)(2,1)} %get-tuple-element.120), channel_id=1, source_target_pairs={{0,64},{32,96},{64,0},{96,32},{1,65},{33,97},{65,1},{97,33},{2,66}... | collective-permute-start | bytes 1179656 | tf_op jit(solution)/shard_map/ppermute | solution.py:81
  25.3 2.5 %collective-permute-start = (bf16[6,64,512]{2,1,0:T(8,128)(2,1)}, bf16[6,64,512]{2,1,0:T(8,128)(2,1)}, u32[]{:S(2)}, u32[]{:S(2)}) collective-permute-start(bf16[6,64,512]{2,1,0:T(8,128)(2,1)} %get-tuple-element.118), channel_id=1, source_target_pairs={{0,32},{32,64},{64,96},{96,0},{1,33},{33,65},{65,97},{97,1},{2,34}... | collective-permute-start | bytes 1179656 | tf_op jit(solution)/shard_map/ppermute | solution.py:81
  30.2 3.8 %all-to-all-done.1.panels_ref.refs_8_.refs_0_ = bf16[8,6,32,256]{3,2,1,0:T(8,128)(2,1)S(1)} async-done(((bf16[8,6,32,256]{3,2,1,0:T(8,128)(2,1)}), bf16[8,6,32,256]{3,2,1,0:T(8,128)(2,1)S(1)}, u32[]{:S(2)}, u32[]{:S(2)}) %all-to-all-start.1) | async-done | bytes 786464 | tf_op jit(solution)/shard_map/all_to_all | solution.py:67
  34.0 6.5 %collective-permute-start.3 = (bf16[8,6,32,256]{3,2,1,0:T(8,128)(2,1)S(1)}, bf16[8,6,32,256]{3,2,1,0:T(8,128)(2,1)}, u32[]{:S(2)}, u32[]{:S(2)}) collective-permute-start(bf16[8,6,32,256]{3,2,1,0:T(8,128)(2,1)S(1)} %all-to-all-done.1.panels_ref.refs_8_.refs_0_), channel_id=1, source_target_pairs={{0,2},{2,0},{1,3},{3,1},{4,6},{6,4},{5,7},{7,5},{8,10},{10,8},{9,1... | collective-permute-start | bytes 2359304 | tf_op jit(solution)/shard_map/ppermute | solution.py:81
  42.2 4.8 %all-to-all-start.2 = ((bf16[4,4,16,512]{3,2,1,0:T(8,128)(2,1)}), bf16[4,4,16,512]{3,2,1,0:T(8,128)(2,1)}, u32[]{:S(2)}, u32[]{:S(2)}) async-start(bf16[4,4,16,512]{3,2,1,0:T(8,128)(2,1)} %shard_map.55), calls=%async_computation.2 | async-start | bytes 524288 | tf_op jit(solution)/shard_map/all_to_all | solution.py:67
  46.9 9.9 %shard_map.56 = (bf16[6,256,256]{2,1,0:T(8,128)(2,1)S(1)}, bf16[6,256,256]{2,1,0:T(8,128)(2,1)S(1)}) custom-call(f32[6,256,256]{2,1,0:T(8,128)S(1)} %copy-done.4), custom_call_target="tpu_custom_call" | custom-call | flops 8455716864 | bytes 3145728 | tf_op jit(solution)/shard_map/pallas_call | solution.py:56
  58.6 2.3 %all-to-all-done.2 = bf16[4,4,16,512]{3,2,1,0:T(8,128)(2,1)} async-done(((bf16[4,4,16,512]{3,2,1,0:T(8,128)(2,1)}), bf16[4,4,16,512]{3,2,1,0:T(8,128)(2,1)}, u32[]{:S(2)}, u32[]{:S(2)}) %all-to-all-start.2) | async-done | bytes 262176 | tf_op jit(solution)/shard_map/all_to_all | solution.py:67
  62.6 4.0 %all-to-all-start.3 = ((bf16[4,4,16,512]{3,2,1,0:T(8,128)(2,1)}), bf16[4,4,16,512]{3,2,1,0:T(8,128)(2,1)S(1)}, u32[]{:S(2)}, u32[]{:S(2)}) async-start(bf16[4,4,16,512]{3,2,1,0:T(8,128)(2,1)} %broadcast_in_dim.126), calls=%async_computation.3 | async-start | bytes 524288 | tf_op jit(solution)/shard_map/all_to_all | solution.py:67
  68.1 4.1 %all-to-all-done.3 = bf16[4,4,16,512]{3,2,1,0:T(8,128)(2,1)S(1)} async-done(((bf16[4,4,16,512]{3,2,1,0:T(8,128)(2,1)}), bf16[4,4,16,512]{3,2,1,0:T(8,128)(2,1)S(1)}, u32[]{:S(2)}, u32[]{:S(2)}) %all-to-all-start.3) | async-done | bytes 262176 | tf_op jit(solution)/shard_map/all_to_all | solution.py:67
  72.4 21.5 %all_to_all.36 = bf16[4,10,16,512]{3,2,1,0:T(8,128)(2,1)S(1)} all-to-all(bf16[4,10,16,512]{3,2,1,0:T(8,128)(2,1)S(1)} %copy.7), channel_id=1, replica_groups=mesh['zh'=4,'x'=4,'y'=8,'zl'=2,'c'=2] {'zh'}, dimensions={0} | all-to-all | bytes 1310720 | tf_op jit(solution)/shard_map/all_to_all | solution.py:67
  94.8 4.1 %all-to-all-start.5 = ((bf16[8,4,16,512]{3,2,1,0:T(8,128)(2,1)}), bf16[8,4,16,512]{3,2,1,0:T(8,128)(2,1)}, u32[]{:S(2)}, u32[]{:S(2)}) async-start(bf16[8,4,16,512]{3,2,1,0:T(8,128)(2,1)} %broadcast_in_dim.129), calls=%async_computation.5 | async-start | bytes 1048576 | tf_op jit(solution)/shard_map/all_to_all | solution.py:67
  99.0 9.5 %collective-permute-start.7 = (bf16[8,6,32,256]{3,2,1,0:T(8,128)(2,1)S(1)}, bf16[8,6,32,256]{3,2,1,0:T(8,128)(2,1)S(1)}, u32[]{:S(2)}, u32[]{:S(2)}) collective-permute-start(bf16[8,6,32,256]{3,2,1,0:T(8,128)(2,1)S(1)} %all-to-all-done.1.panels_ref.refs_8_.refs_0_), channel_id=1, source_target_pairs={{0,1},{1,0},{2,3},{3,2},{4,5},{5,4},{6,7},{7,6},{8,9},{9,8},{10,11... | collective-permute-start | bytes 2359304 | tf_op jit(solution)/shard_map/ppermute | solution.py:81
  110.4 3.2 %collective-permute-start.6 = (bf16[6,16,512]{2,1,0:T(8,128)(2,1)S(1)}, bf16[6,16,512]{2,1,0:T(8,128)(2,1)S(1)}, u32[]{:S(2)}, u32[]{:S(2)}) collective-permute-start(bf16[6,16,512]{2,1,0:T(8,128)(2,1)S(1)} %slice_reduce_fusion), channel_id=1, source_target_pairs={{0,384},{128,0},{256,128},{384,256},{1,385},{129,1},{257,129},{385... | collective-permute-start | bytes 294920 | tf_op jit(solution)/shard_map/ppermute | solution.py:81
  113.6 5.2 %collective-permute-start.5 = (bf16[6,16,512]{2,1,0:T(8,128)(2,1)S(1)}, bf16[6,16,512]{2,1,0:T(8,128)(2,1)S(1)}, u32[]{:S(2)}, u32[]{:S(2)}) collective-permute-start(bf16[6,16,512]{2,1,0:T(8,128)(2,1)S(1)} %slice_reduce_fusion), channel_id=1, source_target_pairs={{0,256},{128,384},{256,0},{384,128},{1,257},{129,385},{257,1},{385... | collective-permute-start | bytes 294920 | tf_op jit(solution)/shard_map/ppermute | solution.py:81
  120.7 5.4 %collective-permute-done.5 = bf16[6,16,512]{2,1,0:T(8,128)(2,1)S(1)} collective-permute-done((bf16[6,16,512]{2,1,0:T(8,128)(2,1)S(1)}, bf16[6,16,512]{2,1,0:T(8,128)(2,1)S(1)}, u32[]{:S(2)}, u32[]{:S(2)}) %collective-permute-start.5) | collective-permute-done | bytes 98336 | tf_op jit(solution)/shard_map/ppermute | solution.py:81
  128.1 5.3 %collective-permute-start.12 = (bf16[8,4,16,512]{3,2,1,0:T(8,128)(2,1)}, bf16[8,4,16,512]{3,2,1,0:T(8,128)(2,1)S(1)}, u32[]{:S(2)}, u32[]{:S(2)}) collective-permute-start(bf16[8,4,16,512]{3,2,1,0:T(8,128)(2,1)} %all-to-all-done.5.refs_4_), channel_id=1, source_target_pairs={{0,2},{2,0},{1,3},{3,1},{4,6},{6,4},{5,7},{7,5},{8,10},{10,8},{9,1... | collective-permute-start | bytes 1572872 | tf_op jit(solution)/shard_map/ppermute | solution.py:81
  136.4 3.0 %collective-permute-start.10 = (bf16[4,6,16,512]{3,2,1,0:T(8,128)(2,1)S(1)}, bf16[4,6,16,512]{3,2,1,0:T(8,128)(2,1)S(1)}, u32[]{:S(2)}, u32[]{:S(2)}) collective-permute-start(bf16[4,6,16,512]{3,2,1,0:T(8,128)(2,1)S(1)} %pad_maximum_fusion.1.refs_0_), channel_id=1, source_target_pairs={{0,64},{32,96},{64,0},{96,32},{1,65},{33,97},{65,1},{97,33},{2,66}... | collective-permute-start | bytes 1179656 | tf_op jit(solution)/shard_map/ppermute | solution.py:81
  139.4 3.2 %collective-permute-start.11 = (bf16[4,6,16,512]{3,2,1,0:T(8,128)(2,1)S(1)}, bf16[4,6,16,512]{3,2,1,0:T(8,128)(2,1)S(1)}, u32[]{:S(2)}, u32[]{:S(2)}) collective-permute-start(bf16[4,6,16,512]{3,2,1,0:T(8,128)(2,1)S(1)} %pad_maximum_fusion.1.refs_0_), channel_id=1, source_target_pairs={{0,96},{32,0},{64,32},{96,64},{1,97},{33,1},{65,33},{97,65},{2,98}... | collective-permute-start | bytes 1179656 | tf_op jit(solution)/shard_map/ppermute | solution.py:81
  144.3 3.3 %collective-permute-start.13 = (bf16[8,4,16,512]{3,2,1,0:T(8,128)(2,1)}, bf16[8,4,16,512]{3,2,1,0:T(8,128)(2,1)S(1)}, u32[]{:S(2)}, u32[]{:S(2)}) collective-permute-start(bf16[8,4,16,512]{3,2,1,0:T(8,128)(2,1)} %all-to-all-done.5.refs_4_), channel_id=1, source_target_pairs={{0,1},{1,0},{2,3},{3,2},{4,5},{5,4},{6,7},{7,6},{8,9},{9,8},{10,11... | collective-permute-start | bytes 1572872 | tf_op jit(solution)/shard_map/ppermute | solution.py:81
  148.2 6.1 %collective-permute-done.10.refs_2_ = bf16[4,6,16,512]{3,2,1,0:T(8,128)(2,1)S(1)} collective-permute-done((bf16[4,6,16,512]{3,2,1,0:T(8,128)(2,1)S(1)}, bf16[4,6,16,512]{3,2,1,0:T(8,128)(2,1)S(1)}, u32[]{:S(2)}, u32[]{:S(2)}) %collective-permute-start.10) | collective-permute-done | bytes 393248 | tf_op jit(solution)/shard_map/ppermute | solution.py:81
  154.4 3.9 %collective-permute-done.11.refs_3_ = bf16[4,6,16,512]{3,2,1,0:T(8,128)(2,1)S(1)} collective-permute-done((bf16[4,6,16,512]{3,2,1,0:T(8,128)(2,1)S(1)}, bf16[4,6,16,512]{3,2,1,0:T(8,128)(2,1)S(1)}, u32[]{:S(2)}, u32[]{:S(2)}) %collective-permute-start.11) | collective-permute-done | bytes 393248 | tf_op jit(solution)/shard_map/ppermute | solution.py:81
  158.3 3.7 %collective-permute-start.14 = (bf16[8,4,16,512]{3,2,1,0:T(8,128)(2,1)S(1)}, bf16[8,4,16,512]{3,2,1,0:T(8,128)(2,1)S(1)}, u32[]{:S(2)}, u32[]{:S(2)}) collective-permute-start(bf16[8,4,16,512]{3,2,1,0:T(8,128)(2,1)S(1)} %collective-permute-done.12.refs_6_), channel_id=1, source_target_pairs={{0,1},{1,0},{2,3},{3,2},{4,5},{5,4},{6,7},{7,6},{8,9},{9,8},{10,11... | collective-permute-start | bytes 1572872 | tf_op jit(solution)/shard_map/ppermute | solution.py:81
  164.6 8.9 %shard_map.57 = (bf16[6,256,512]{2,1,0:T(8,128)(2,1)}, bf16[256,512]{1,0:T(8,128)(2,1)S(1)}, bf16[512,512]{1,0:T(8,128)(2,1)}) custom-call(s32[4]{0:T(128)} %copy-done.2, s32[1,256]{1,0:T(1,128)} %get-tuple-element.115.slot_ref, bf16[6,256,256]{2,1,0:T(8,128)(2,1)} %copy-done.5, bf16[6,256,256]{2,1,0:T(8,128)(2,1)} %copy-done.6, ...), custom_call_target="tpu_custom_call" | custom-call | flops 2348810240 | bytes 9437184 | tf_op jit(solution)/shard_map/pallas_call | solution.py:174
  173.5 7.1 %all-to-all-start.6 = ((bf16[16,32,512]{2,1,0:T(8,128)(2,1)}), bf16[16,32,512]{2,1,0:T(8,128)(2,1)S(1)}, u32[]{:S(2)}, u32[]{:S(2)}) async-start(bf16[16,32,512]{2,1,0:T(8,128)(2,1)} %bitcast.48), calls=%async_computation.6 | async-start | bytes 1048576 | tf_op jit(solution)/shard_map/all_to_all | solution.py:67
  184.1 8.0 %shard_map.58 = f32[1024,512]{1,0:T(8,128)} custom-call(s32[4]{0:T(128)} %copy-done.2, s32[1024,128]{1,0:T(8,128)} %broadcast_in_dim.133.last_ref, bf16[6,256,512]{2,1,0:T(8,128)(2,1)} %get-tuple-element.91.u_ref.own_ref, bf16[1024,512]{1,0:T(8,128)(2,1)} %matrix_ref, bf16[8,6,32,256]{3,2,1,0:T(8,128)(2,1)} %copy-done, bf16[8,6,32,256]{3,2,1,0:T(8,128)(2,1)} %copy-done.10, ...), custom_call_target="tpu_custom_call" | custom-call | flops 1610612736 | bytes 8388608 | tf_op jit(solution)/shard_map/pallas_call | solution.py:224
  192.1 5.8 %all-to-all-done.6.got_ref = bf16[16,32,512]{2,1,0:T(8,128)(2,1)S(1)} async-done(((bf16[16,32,512]{2,1,0:T(8,128)(2,1)}), bf16[16,32,512]{2,1,0:T(8,128)(2,1)S(1)}, u32[]{:S(2)}, u32[]{:S(2)}) %all-to-all-start.6) | async-done | bytes 524320 | tf_op jit(solution)/shard_map/all_to_all | solution.py:67
  199.3 3.0 %shard_map.59 = bf16[1024,512]{1,0:T(8,128)(2,1)} custom-call(s32[4]{0:T(128)S(1)} %copy-done.3, bf16[6,256,512]{2,1,0:T(8,128)(2,1)S(1)} %copy-done.1, bf16[1024,192]{1,0:T(8,128)(2,1)S(1)} %fusion.9.put_ref, bf16[16,32,512]{2,1,0:T(8,128)(2,1)S(1)} %all-to-all-done.6.got_ref, f32[1024,512]{1,0:T(8,128)} %get-tuple-element.96.total_ref), custom_call_target="tpu_custom_call" | custom-call | flops 201326592 | bytes 6291456 | tf_op jit(solution)/shard_map/pallas_call | solution.py:250
  (102 shorter events, 30.0 us)
Async XLA Ops:
  0.0 13.0 %copy-start.12 = (s32[6,256]{1,0:T(8,128)S(1)}, s32[6,256]{1,0:T(8,128)}, u32[]{:S(2)}) copy-start(s32[6,256]{1,0:T(8,128)} %param.10) | copy-start | bytes 18436
  0.0 13.1 %copy-start.9 = (bf16[1024,512]{1,0:T(8,128)(2,1)S(1)}, bf16[1024,512]{1,0:T(8,128)(2,1)}, u32[]{:S(2)}) copy-start(bf16[1024,512]{1,0:T(8,128)(2,1)} %matrix_ref) | copy-start | bytes 3145732
  5.3 28.7 %all-to-all-start.1 = ((bf16[8,6,32,256]{3,2,1,0:T(8,128)(2,1)}), bf16[8,6,32,256]{3,2,1,0:T(8,128)(2,1)S(1)}, u32[]{:S(2)}, u32[]{:S(2)}) async-start(bf16[8,6,32,256]{3,2,1,0:T(8,128)(2,1)} %broadcast_in_dim.73), calls=%async_computation.1 | async-start | bytes 1572864 | tf_op jit(solution)/shard_map/all_to_all | solution.py:67
  16.1 13.2 %copy-start.13 = (s32[8,2,2]{0,2,1:T(2,128)S(1)}, s32[8,2,2]{0,2,1:T(2,128)}, u32[]{:S(2)}) copy-start(s32[8,2,2]{0,2,1:T(2,128)} %constant.184) | copy-start | bytes 388
  16.1 30.8 %copy-start.4 = (f32[6,256,256]{2,1,0:T(8,128)S(1)}, f32[6,256,256]{2,1,0:T(8,128)}, u32[]{:S(2)}) copy-start(f32[6,256,256]{2,1,0:T(8,128)} %l_ref.1) | copy-start | bytes 4718596
  18.5 48.1 %collective-permute-start.2 = (bf16[6,64,512]{2,1,0:T(8,128)(2,1)}, bf16[6,64,512]{2,1,0:T(8,128)(2,1)}, u32[]{:S(2)}, u32[]{:S(2)}) collective-permute-start(bf16[6,64,512]{2,1,0:T(8,128)(2,1)} %get-tuple-element.119), channel_id=1, source_target_pairs={{0,96},{32,0},{64,32},{96,64},{1,97},{33,1},{65,33},{97,65},{2,98}... | collective-permute-start | bytes 1179656 | tf_op jit(solution)/shard_map/ppermute | solution.py:81
  22.9 43.7 %collective-permute-start.1 = (bf16[6,64,512]{2,1,0:T(8,128)(2,1)}, bf16[6,64,512]{2,1,0:T(8,128)(2,1)}, u32[]{:S(2)}, u32[]{:S(2)}) collective-permute-start(bf16[6,64,512]{2,1,0:T(8,128)(2,1)} %get-tuple-element.120), channel_id=1, source_target_pairs={{0,64},{32,96},{64,0},{96,32},{1,65},{33,97},{65,1},{97,33},{2,66}... | collective-permute-start | bytes 1179656 | tf_op jit(solution)/shard_map/ppermute | solution.py:81
  25.3 41.3 %collective-permute-start = (bf16[6,64,512]{2,1,0:T(8,128)(2,1)}, bf16[6,64,512]{2,1,0:T(8,128)(2,1)}, u32[]{:S(2)}, u32[]{:S(2)}) collective-permute-start(bf16[6,64,512]{2,1,0:T(8,128)(2,1)} %get-tuple-element.118), channel_id=1, source_target_pairs={{0,32},{32,64},{64,96},{96,0},{1,33},{33,65},{65,97},{97,1},{2,34}... | collective-permute-start | bytes 1179656 | tf_op jit(solution)/shard_map/ppermute | solution.py:81
  29.4 27.4 %copy-start.2 = (s32[4]{0:T(128)}, s32[4]{0:T(128)S(1)}, u32[]{:S(2)}) copy-start(s32[4]{0:T(128)S(1)} %pad_add_fusion.at_ref) | copy-start | bytes 52
  34.0 65.0 %copy-start = (bf16[8,6,32,256]{3,2,1,0:T(8,128)(2,1)}, bf16[8,6,32,256]{3,2,1,0:T(8,128)(2,1)S(1)}, u32[]{:S(2)}) copy-start(bf16[8,6,32,256]{3,2,1,0:T(8,128)(2,1)S(1)} %all-to-all-done.1.panels_ref.refs_8_.refs_0_) | copy-start | bytes 2359300
  34.0 38.2 %collective-permute-start.3 = (bf16[8,6,32,256]{3,2,1,0:T(8,128)(2,1)S(1)}, bf16[8,6,32,256]{3,2,1,0:T(8,128)(2,1)}, u32[]{:S(2)}, u32[]{:S(2)}) collective-permute-start(bf16[8,6,32,256]{3,2,1,0:T(8,128)(2,1)S(1)} %all-to-all-done.1.panels_ref.refs_8_.refs_0_), channel_id=1, source_target_pairs={{0,2},{2,0},{1,3},{3,1},{4,6},{6,4},{5,7},{7,5},{8,10},{10,8},{9,1... | collective-permute-start | bytes 2359304 | tf_op jit(solution)/shard_map/ppermute | solution.py:81
  42.2 18.7 %all-to-all-start.2 = ((bf16[4,4,16,512]{3,2,1,0:T(8,128)(2,1)}), bf16[4,4,16,512]{3,2,1,0:T(8,128)(2,1)}, u32[]{:S(2)}, u32[]{:S(2)}) async-start(bf16[4,4,16,512]{3,2,1,0:T(8,128)(2,1)} %shard_map.55), calls=%async_computation.2 | async-start | bytes 524288 | tf_op jit(solution)/shard_map/all_to_all | solution.py:67
  62.6 9.5 %all-to-all-start.3 = ((bf16[4,4,16,512]{3,2,1,0:T(8,128)(2,1)}), bf16[4,4,16,512]{3,2,1,0:T(8,128)(2,1)S(1)}, u32[]{:S(2)}, u32[]{:S(2)}) async-start(bf16[4,4,16,512]{3,2,1,0:T(8,128)(2,1)} %broadcast_in_dim.126), calls=%async_computation.3 | async-start | bytes 524288 | tf_op jit(solution)/shard_map/all_to_all | solution.py:67
  94.8 33.3 %all-to-all-start.5 = ((bf16[8,4,16,512]{3,2,1,0:T(8,128)(2,1)}), bf16[8,4,16,512]{3,2,1,0:T(8,128)(2,1)}, u32[]{:S(2)}, u32[]{:S(2)}) async-start(bf16[8,4,16,512]{3,2,1,0:T(8,128)(2,1)} %broadcast_in_dim.129), calls=%async_computation.5 | async-start | bytes 1048576 | tf_op jit(solution)/shard_map/all_to_all | solution.py:67
  99.0 29.1 %collective-permute-start.7 = (bf16[8,6,32,256]{3,2,1,0:T(8,128)(2,1)S(1)}, bf16[8,6,32,256]{3,2,1,0:T(8,128)(2,1)S(1)}, u32[]{:S(2)}, u32[]{:S(2)}) collective-permute-start(bf16[8,6,32,256]{3,2,1,0:T(8,128)(2,1)S(1)} %all-to-all-done.1.panels_ref.refs_8_.refs_0_), channel_id=1, source_target_pairs={{0,1},{1,0},{2,3},{3,2},{4,5},{5,4},{6,7},{7,6},{8,9},{9,8},{10,11... | collective-permute-start | bytes 2359304 | tf_op jit(solution)/shard_map/ppermute | solution.py:81
  108.4 19.7 %collective-permute-start.8 = (bf16[8,6,32,256]{3,2,1,0:T(8,128)(2,1)}, bf16[8,6,32,256]{3,2,1,0:T(8,128)(2,1)}, u32[]{:S(2)}, u32[]{:S(2)}) collective-permute-start(bf16[8,6,32,256]{3,2,1,0:T(8,128)(2,1)} %collective-permute-done.3.refs_10_.refs_2_), channel_id=1, source_target_pairs={{0,1},{1,0},{2,3},{3,2},{4,5},{5,4},{6,7},{7,6},{8,9},{9,8},{10,11... | collective-permute-start | bytes 2359304 | tf_op jit(solution)/shard_map/ppermute | solution.py:81
  110.4 10.3 %collective-permute-start.6 = (bf16[6,16,512]{2,1,0:T(8,128)(2,1)S(1)}, bf16[6,16,512]{2,1,0:T(8,128)(2,1)S(1)}, u32[]{:S(2)}, u32[]{:S(2)}) collective-permute-start(bf16[6,16,512]{2,1,0:T(8,128)(2,1)S(1)} %slice_reduce_fusion), channel_id=1, source_target_pairs={{0,384},{128,0},{256,128},{384,256},{1,385},{129,1},{257,129},{385... | collective-permute-start | bytes 294920 | tf_op jit(solution)/shard_map/ppermute | solution.py:81
  113.6 12.5 %collective-permute-start.5 = (bf16[6,16,512]{2,1,0:T(8,128)(2,1)S(1)}, bf16[6,16,512]{2,1,0:T(8,128)(2,1)S(1)}, u32[]{:S(2)}, u32[]{:S(2)}) collective-permute-start(bf16[6,16,512]{2,1,0:T(8,128)(2,1)S(1)} %slice_reduce_fusion), channel_id=1, source_target_pairs={{0,256},{128,384},{256,0},{384,128},{1,257},{129,385},{257,1},{385... | collective-permute-start | bytes 294920 | tf_op jit(solution)/shard_map/ppermute | solution.py:81
  118.8 9.2 %collective-permute-start.4 = (bf16[6,16,512]{2,1,0:T(8,128)(2,1)S(1)}, bf16[6,16,512]{2,1,0:T(8,128)(2,1)S(1)}, u32[]{:S(2)}, u32[]{:S(2)}) collective-permute-start(bf16[6,16,512]{2,1,0:T(8,128)(2,1)S(1)} %slice_reduce_fusion), channel_id=1, source_target_pairs={{0,128},{128,256},{256,384},{384,0},{1,129},{129,257},{257,385},{3... | collective-permute-start | bytes 294920 | tf_op jit(solution)/shard_map/ppermute | solution.py:81
  128.1 35.6 %copy-start.11 = (bf16[4,6,16,512]{3,2,1,0:T(8,128)(2,1)}, bf16[4,6,16,512]{3,2,1,0:T(8,128)(2,1)S(1)}, u32[]{:S(2)}) copy-start(bf16[4,6,16,512]{3,2,1,0:T(8,128)(2,1)S(1)} %pad_maximum_fusion.1.refs_0_) | copy-start | bytes 1179652
  128.1 35.6 %copy-start.10 = (bf16[8,6,32,256]{3,2,1,0:T(8,128)(2,1)}, bf16[8,6,32,256]{3,2,1,0:T(8,128)(2,1)S(1)}, u32[]{:S(2)}) copy-start(bf16[8,6,32,256]{3,2,1,0:T(8,128)(2,1)S(1)} %collective-permute-done.7.refs_9_.refs_1_) | copy-start | bytes 2359300
  128.1 30.1 %collective-permute-start.12 = (bf16[8,4,16,512]{3,2,1,0:T(8,128)(2,1)}, bf16[8,4,16,512]{3,2,1,0:T(8,128)(2,1)S(1)}, u32[]{:S(2)}, u32[]{:S(2)}) collective-permute-start(bf16[8,4,16,512]{3,2,1,0:T(8,128)(2,1)} %all-to-all-done.5.refs_4_), channel_id=1, source_target_pairs={{0,2},{2,0},{1,3},{3,1},{4,6},{6,4},{5,7},{7,5},{8,10},{10,8},{9,1... | collective-permute-start | bytes 1572872 | tf_op jit(solution)/shard_map/ppermute | solution.py:81
  134.2 14.0 %collective-permute-start.9 = (bf16[4,6,16,512]{3,2,1,0:T(8,128)(2,1)S(1)}, bf16[4,6,16,512]{3,2,1,0:T(8,128)(2,1)S(1)}, u32[]{:S(2)}, u32[]{:S(2)}) collective-permute-start(bf16[4,6,16,512]{3,2,1,0:T(8,128)(2,1)S(1)} %pad_maximum_fusion.1.refs_0_), channel_id=1, source_target_pairs={{0,32},{32,64},{64,96},{96,0},{1,33},{33,65},{65,97},{97,1},{2,34}... | collective-permute-start | bytes 1179656 | tf_op jit(solution)/shard_map/ppermute | solution.py:81
  136.4 18.0 %collective-permute-start.10 = (bf16[4,6,16,512]{3,2,1,0:T(8,128)(2,1)S(1)}, bf16[4,6,16,512]{3,2,1,0:T(8,128)(2,1)S(1)}, u32[]{:S(2)}, u32[]{:S(2)}) collective-permute-start(bf16[4,6,16,512]{3,2,1,0:T(8,128)(2,1)S(1)} %pad_maximum_fusion.1.refs_0_), channel_id=1, source_target_pairs={{0,64},{32,96},{64,0},{96,32},{1,65},{33,97},{65,1},{97,33},{2,66}... | collective-permute-start | bytes 1179656 | tf_op jit(solution)/shard_map/ppermute | solution.py:81
  139.4 18.8 %collective-permute-start.11 = (bf16[4,6,16,512]{3,2,1,0:T(8,128)(2,1)S(1)}, bf16[4,6,16,512]{3,2,1,0:T(8,128)(2,1)S(1)}, u32[]{:S(2)}, u32[]{:S(2)}) collective-permute-start(bf16[4,6,16,512]{3,2,1,0:T(8,128)(2,1)S(1)} %pad_maximum_fusion.1.refs_0_), channel_id=1, source_target_pairs={{0,96},{32,0},{64,32},{96,64},{1,97},{33,1},{65,33},{97,65},{2,98}... | collective-permute-start | bytes 1179656 | tf_op jit(solution)/shard_map/ppermute | solution.py:81
  144.3 19.4 %collective-permute-start.13 = (bf16[8,4,16,512]{3,2,1,0:T(8,128)(2,1)}, bf16[8,4,16,512]{3,2,1,0:T(8,128)(2,1)S(1)}, u32[]{:S(2)}, u32[]{:S(2)}) collective-permute-start(bf16[8,4,16,512]{3,2,1,0:T(8,128)(2,1)} %all-to-all-done.5.refs_4_), channel_id=1, source_target_pairs={{0,1},{1,0},{2,3},{3,2},{4,5},{5,4},{6,7},{7,6},{8,9},{9,8},{10,11... | collective-permute-start | bytes 1572872 | tf_op jit(solution)/shard_map/ppermute | solution.py:81
  148.2 15.5 %copy-start.17 = (bf16[4,6,16,512]{3,2,1,0:T(8,128)(2,1)}, bf16[4,6,16,512]{3,2,1,0:T(8,128)(2,1)S(1)}, u32[]{:S(2)}) copy-start(bf16[4,6,16,512]{3,2,1,0:T(8,128)(2,1)S(1)} %collective-permute-done.9.refs_1_) | copy-start | bytes 1179652
  154.4 9.4 %copy-start.18 = (bf16[4,6,16,512]{3,2,1,0:T(8,128)(2,1)}, bf16[4,6,16,512]{3,2,1,0:T(8,128)(2,1)S(1)}, u32[]{:S(2)}) copy-start(bf16[4,6,16,512]{3,2,1,0:T(8,128)(2,1)S(1)} %collective-permute-done.10.refs_2_) | copy-start | bytes 1179652
  158.3 5.5 %copy-start.19 = (bf16[4,6,16,512]{3,2,1,0:T(8,128)(2,1)}, bf16[4,6,16,512]{3,2,1,0:T(8,128)(2,1)S(1)}, u32[]{:S(2)}) copy-start(bf16[4,6,16,512]{3,2,1,0:T(8,128)(2,1)S(1)} %collective-permute-done.11.refs_3_) | copy-start | bytes 1179652
  158.3 5.5 %copy-start.14 = (bf16[8,4,16,512]{3,2,1,0:T(8,128)(2,1)}, bf16[8,4,16,512]{3,2,1,0:T(8,128)(2,1)S(1)}, u32[]{:S(2)}) copy-start(bf16[8,4,16,512]{3,2,1,0:T(8,128)(2,1)S(1)} %collective-permute-done.12.refs_6_) | copy-start | bytes 1572868
  158.3 5.4 %collective-permute-start.14 = (bf16[8,4,16,512]{3,2,1,0:T(8,128)(2,1)S(1)}, bf16[8,4,16,512]{3,2,1,0:T(8,128)(2,1)S(1)}, u32[]{:S(2)}, u32[]{:S(2)}) collective-permute-start(bf16[8,4,16,512]{3,2,1,0:T(8,128)(2,1)S(1)} %collective-permute-done.12.refs_6_), channel_id=1, source_target_pairs={{0,1},{1,0},{2,3},{3,2},{4,5},{5,4},{6,7},{7,6},{8,9},{9,8},{10,11... | collective-permute-start | bytes 1572872 | tf_op jit(solution)/shard_map/ppermute | solution.py:81
  173.5 24.3 %all-to-all-start.6 = ((bf16[16,32,512]{2,1,0:T(8,128)(2,1)}), bf16[16,32,512]{2,1,0:T(8,128)(2,1)S(1)}, u32[]{:S(2)}, u32[]{:S(2)}) async-start(bf16[16,32,512]{2,1,0:T(8,128)(2,1)} %bitcast.48), calls=%async_computation.6 | async-start | bytes 1048576 | tf_op jit(solution)/shard_map/all_to_all | solution.py:67
  (6 other events, 6.3 us)

commit v3 on v2

--- a/solution.py
+++ b/solution.py
@@ -123,34 +123,40 @@
     return lax.rem(zl + n // 2, 2), lax.rem(c + n % 2, 2)
 
 
-def solve_kernel(at_ref, slot_ref, high_ref, low_ref, diag_ref, *refs):
-    active_in, blocks_in, panels_in = refs[:4], refs[4:8], refs[8:12]
-    u_ref, old_ref, send_ref, active, blocks, panels, active_sem, blocks_sem, panels_sem = refs[12:]
+def solve_kernel(at_ref, slot_ref, high_ref, low_ref, matrix_ref, *refs):
+    active_in, blocks_in, panels_in = refs[:4], refs[4:6], refs[6:10]
+    u_ref, old_ref, send_ref, active, blocks, panels, active_sem, blocks_sem, panels_sem = refs[10:]
     zh, x, zl, c = at_ref[0], at_ref[1], at_ref[2], at_ref[3]
     me = zh * 4 + x
-    width = diag_ref.shape[1]
+    width = matrix_ref.shape[1]
     copies = []
     for d in range(4):
         for e in range(4):
             target = active.at[lax.rem(x - d + 4, 4), lax.rem(zh - e + 4, 4)]
             copies.append(pltpu.make_async_copy(active_in[d].at[e], target, active_sem.at[d * 4 + e]))
+    for n in range(2):
+        target = blocks.at[:, :, lax.rem(c + n, 2)]
+        copies.append(pltpu.make_async_copy(blocks_in[n], target, blocks_sem.at[n]))
     for n in range(4):
         a, b = turned(zl, c, n)
-        copies.append(pltpu.make_async_copy(blocks_in[n], blocks.at[:, a, b], blocks_sem.at[n]))
         copies.append(pltpu.make_async_copy(panels_in[n].at[0:2], panels.at[:, a, b], panels_sem.at[n]))
     for copy in copies:
         copy.start()
-    for copy in copies:
+    for copy in copies[:16]:
         copy.wait()
 
     def rows_of(n):
         return active[:, :, n].reshape(NB, width)
 
-    old_ref[...] = diag_ref[...]
+    old_ref[...] = matrix_ref[0:NB, :]
     for s in range(STEPS):
         top = rows_of(s)
         u = (dot(high_ref[s], top) + dot(low_ref[s], top)).astype(jnp.bfloat16)
         u_ref[s] = u
+
+        if s == 0:
+            for copy in copies[16:]:
+                copy.wait()
         for t in range(s + 1, STEPS):
             n = PLACE[(t, s)]
             left = n // 2 % 2 * NB
@@ -158,18 +164,20 @@
             less = rows_of(t).astype(jnp.float32) - dot(block, u)
             active[:, :, t] = less.astype(jnp.bfloat16).reshape(4, 4, 16, width)
 
-        @pl.when(s < me)
+    for s in range(STEPS - 1):
+
+        @pl.when((s < me) & (me < STEPS))
         def _():
             panel = panels[:, :, :, s].reshape(NB, NB)
-            old_ref[...] = (old_ref[...].astype(jnp.float32) - dot(panel, u)).astype(jnp.bfloat16)
+            old_ref[...] = (old_ref[...].astype(jnp.float32) - dot(panel, u_ref[s])).astype(jnp.bfloat16)
 
     slot = lax.broadcasted_iota(jnp.int32, (16 * SLOTS, NB), 0)
     put = jnp.where(slot == slot_ref[...], 1.0, 0.0).astype(jnp.bfloat16)
     send_ref[...] = dot(put, old_ref[...]).astype(jnp.bfloat16)
 
 
-def solve(at, slot, high, low, diag, active, blocks, panels):
-    width = diag.shape[1]
+def solve(at, slot, high, low, matrix, active, blocks, panels):
+    width = matrix.shape[1]
     vmem, anywhere = pl.BlockSpec(memory_space=pltpu.VMEM), pl.BlockSpec(memory_space=pl.ANY)
     return pl.pallas_call(
         solve_kernel,
@@ -178,19 +186,19 @@
             jax.ShapeDtypeStruct((NB, width), jnp.bfloat16),
             jax.ShapeDtypeStruct((16 * SLOTS, width), jnp.bfloat16),
         ),
-        in_specs=[pl.BlockSpec(memory_space=pltpu.SMEM)] + [vmem] * 4 + [anywhere] * 12,
+        in_specs=[pl.BlockSpec(memory_space=pltpu.SMEM)] + [vmem] * 4 + [anywhere] * 10,
         out_specs=(vmem,) * 3,
         scratch_shapes=[
             pltpu.VMEM((4, 4, STEPS, 16, width), jnp.bfloat16),
             pltpu.VMEM((8, 2, 2, 4, 16, 2 * NB), jnp.bfloat16),
             pltpu.VMEM((2, 2, 2, STEPS, 32, NB), jnp.bfloat16),
             pltpu.SemaphoreType.DMA((16,)),
-            pltpu.SemaphoreType.DMA((4,)),
+            pltpu.SemaphoreType.DMA((2,)),
             pltpu.SemaphoreType.DMA((4,)),
         ],
         compiler_params=pltpu.CompilerParams(vmem_limit_bytes=58 * 2**20),
         cost_estimate=pl.CostEstimate(flops=2 * 35 * NB * NB * width, bytes_accessed=9 * 2**20, transcendentals=0),
-    )(at, slot, high, low, diag, *active, *blocks, *panels)
+    )(at, slot, high, low, matrix, *active, *blocks, *panels)
 
 
 def update_kernel(at_ref, last_ref, u_ref, matrix_ref, *refs):
@@ -218,6 +226,13 @@
             rows = jnp.where(last >= 0, rows, rows.astype(jnp.bfloat16).astype(jnp.float32))
         out_ref[span, :] = rows
 
+    me = at_ref[0] * 4 + at_ref[1]
+
+    @pl.when(me < STEPS)
+    def _():
+        own = u_ref[pl.ds(jnp.minimum(me, STEPS - 1), 1)].reshape(NB, width)
+        out_ref[0:NB, :] = own.astype(jnp.float32)
+
 
 def update(at, last, u, matrix, panels):
     vmem, anywhere = pl.BlockSpec(memory_space=pltpu.VMEM), pl.BlockSpec(memory_space=pl.ANY)
@@ -234,29 +249,52 @@
     )(at, last, u, matrix, *panels)
 
 
-def place_kernel(at_ref, own_ref, put_ref, got_ref, total_ref, out_ref):
-    me = at_ref[0] * 4 + at_ref[1]
+def place_kernel(put_ref, got_ref, total_ref, out_ref):
     width = out_ref.shape[1]
     got = got_ref[0:STEPS].reshape(STEPS * SLOTS, width)
     out_ref[...] = (total_ref[...] + dot(put_ref[...], got)).astype(jnp.bfloat16)
 
-    @pl.when(me < STEPS)
-    def _():
-        out_ref[0:NB, :] = own_ref[pl.ds(jnp.minimum(me, STEPS - 1), 1)].reshape(NB, width)
-
-
-def place(at, u, put, got, total):
+
+def place(put, got, total):
     vmem = pl.BlockSpec(memory_space=pltpu.VMEM)
     return pl.pallas_call(
         place_kernel,
         out_shape=jax.ShapeDtypeStruct(total.shape, jnp.bfloat16),
-        in_specs=[pl.BlockSpec(memory_space=pltpu.SMEM)] + [vmem] * 4,
+        in_specs=[vmem] * 3,
         out_specs=vmem,
         compiler_params=pltpu.CompilerParams(vmem_limit_bytes=32 * 2**20),
         cost_estimate=pl.CostEstimate(
             flops=2 * total.size * STEPS * SLOTS, bytes_accessed=6 * 2**20, transcendentals=0
         ),
-    )(at, u, put, got, total)
+    )(put, got, total)
+
+
+def origin_kernel(pivots_ref, origin_ref, base_ref):
+    rows = pivots_ref[...]
+    columns = jnp.transpose(jnp.concatenate([rows, rows[: 8 - STEPS]], axis=0))
+    index = lax.broadcasted_iota(jnp.int32, (NB, NB), 0).astype(jnp.float32)
+    for s in range(STEPS):
+        row = rows[s : s + 1]
+        latest = jnp.full((1, NB), -1.0, jnp.float32)
+        for t in range(s):
+            code = jnp.where(columns[:, t : t + 1] == row, index + float(t * ROWS), -1.0)
+            latest = jnp.maximum(latest, jnp.max(code, axis=0, keepdims=True))
+        latest = latest.astype(jnp.int32)
+        origin_ref[s : s + 1, :] = latest
+        base_ref[s : s + 1, :] = jnp.where(latest >= 0, latest, row)
+
+
+def origins(pivots):
+    vmem = pl.BlockSpec(memory_space=pltpu.VMEM)
+    out = jax.ShapeDtypeStruct(pivots.shape, jnp.int32)
+    return pl.pallas_call(
+        origin_kernel,
+        out_shape=(out, out),
+        in_specs=[vmem],
+        out_specs=(vmem, vmem),
+        compiler_params=pltpu.CompilerParams(vmem_limit_bytes=16 * 2**20),
+        cost_estimate=pl.CostEstimate(flops=1000, bytes_accessed=20000, transcendentals=0),
+    )(pivots)
 
 
 def body(matrix, panels, diag_blocks, pivots):
@@ -272,11 +310,7 @@
     wide, pivots, matrix = lax.optimization_barrier((jnp.broadcast_to(panels, (8,) + panels.shape), pivots, matrix))
     by_y = exchange(wide, "y")
 
-    same = pivots[:, :, None, None] == pivots[None, None]
-    before = (t_ids[None, :] < t_ids[:, None])[:, None, :, None]
-    code = jnp.where(same & before, t_ids[:, None] * ROWS + i_ids[None, :], -1)
-    origin = jnp.max(code, axis=(2, 3))
-    base = jnp.where(origin >= 0, origin, pivots)
+    origin, base = origins(pivots)
 
     picked = dot(picks(base.reshape(-1), local), matrix).astype(jnp.bfloat16)
     active = sum(dealt(picked.reshape(STEPS, 4, 64, width).transpose(1, 0, 2, 3), "x"))
@@ -289,23 +323,23 @@
     ids = lax.dynamic_slice_in_dim(ids.reshape(STEPS * STEPS, NB), y % 4 * 64, 64, 1)
     rows = l_rows(at, pair[:, 0], pair[:, 1], ids, by_y)
 
-    across = shift(by_y, "zl", 1)
+    chunk = add_up(exchange(rows, ("zl", "c")))
+    both = jnp.concatenate([jnp.broadcast_to(chunk, (4,) + chunk.shape), active], axis=1)
+    both, pivots, diag_blocks = lax.optimization_barrier((both, pivots, diag_blocks))
     high, low = inverses(diag_blocks)
-    chunk = add_up(exchange(rows, ("zl", "c")))
-    chunk = add_up(everyone(chunk, "x"))
-    active, chunk, across, high, low, pivots = lax.optimization_barrier((active, chunk, across, high, low, pivots))
-    both = jnp.concatenate([jnp.broadcast_to(chunk, (4,) + chunk.shape), active], axis=1)
     both = exchange(both, "zh")
-    chunk, active = add_up(both[:, :4]), add_up(both[:, 4:])
+    chunk = add_up(both[:, :4])
+    wide = jnp.broadcast_to(chunk, (4,) + chunk.shape)
+    wide, both, high, low = lax.optimization_barrier((wide, both, high, low))
+    active = add_up(both[:, 4:])
+    chunk = add_up(exchange(wide, "x"))
     active = jnp.stack(passed(active, "zh"))
-    chunk = everyone(chunk, "y")
-    whole = [by_y, shift(by_y, "c", 1), across, shift(across, "c", 1)]
-    active, chunk, whole[1], whole[3] = lax.optimization_barrier((active, chunk, whole[1], whole[3]))
+    panels_across = shift(by_y, "zl", 1)
+    active, chunk, panels_across = lax.optimization_barrier((active, chunk, panels_across))
     active = passed(active, "x")
-    across = shift(chunk, "zl", 1)
-    beside = shift(chunk, "c", 1)
-    active[1], active[2], active[3], across = lax.optimization_barrier((*active[1:], across))
-    blocks = [chunk, beside, across, shift(across, "c", 1)]
+    chunk = everyone(chunk, ("y", "zl")).reshape(8, 2, 4, 16, 2 * NB)
+    whole = [by_y, shift(by_y, "c", 1), panels_across, shift(panels_across, "c", 1)]
+    active[1], pivots = lax.optimization_barrier((active[1], pivots))
 
     same = pivots[:, :, None, None] == pivots[None, None]
     after = (t_ids[None, :] > t_ids[:, None])[:, None, :, None]
@@ -314,17 +348,27 @@
     ahead = (owner[:, :, None] == owner[:, None, :]) & (i_ids[None, :] < i_ids[:, None])
     rank = jnp.where(stays, jnp.sum(ahead, axis=2, dtype=jnp.int32), -1)
     rounds = (jnp.max(rank) + SLOTS) // SLOTS
+    mine = jnp.minimum(me, STEPS - 1)
+    my_rank = jnp.where(me < STEPS, lax.dynamic_index_in_dim(rank, mine, 0, keepdims=False), -1)
+    my_owner = lax.dynamic_index_in_dim(owner, mine, 0, keepdims=False)
+
+    def slots(q):
+        n = my_rank - q * SLOTS
+        return jnp.where((n >= 0) & (n < SLOTS), my_owner * SLOTS + n, -1)
+
+    first = slots(0)[None]
+    active[2], active[3], chunk, whole[1], whole[3], first = lax.optimization_barrier(
+        (*active[2:], chunk, whole[1], whole[3], first)
+    )
+    blocks = [chunk, shift(chunk, "c", 1)]
+    u, old, send = solve(at, first, high, low, matrix, active, blocks, whole)
+
+    got = exchange(send.reshape(16, SLOTS, width), ("zh", "x"))
+    u, pivots = lax.optimization_barrier((u, pivots))
     here = (pivots.reshape(-1)[None, :] == local[:, None]) & stays.reshape(-1)[None, :]
     tag = jnp.max(jnp.where(here, (t_ids[:, None] * NB + rank).reshape(-1)[None, :], -1), axis=1)
     last = jnp.where(tag >= 0, tag // NB, -1)
     at_rank = jnp.where(tag >= 0, tag % NB, -1)
-    mine = jnp.minimum(me, STEPS - 1)
-    my_rank = jnp.where(me < STEPS, lax.dynamic_index_in_dim(rank, mine, 0, keepdims=False), -1)
-    my_owner = lax.dynamic_index_in_dim(owner, mine, 0, keepdims=False)
-
-    def slots(q):
-        n = my_rank - q * SLOTS
-        return jnp.where((n >= 0) & (n < SLOTS), my_owner * SLOTS + n, -1)
 
     def landing(q):
         n = at_rank - q * SLOTS
@@ -333,9 +377,7 @@
     def deliver(sent):
         return exchange(sent.reshape(16, SLOTS, width), ("zh", "x"))
 
-    u, old, send = solve(at, slots(0)[None], high, low, matrix[:NB], active, blocks, whole)
     total = update(at, jnp.broadcast_to(last[:, None], (ROWS, 128)), u, matrix, whole)
-    got = deliver(send)
     total, got = lax.optimization_barrier((total, got))
 
     def more(state):
@@ -345,7 +387,7 @@
         return q + 1, total + dot(landing(q), got)
 
     _, total = lax.while_loop(lambda state: state[0] < rounds, more, (jnp.int32(1), total))
-    return place(at, u, landing(0), got, total)
+    return place(landing(0), got, total)
 
 
 def solution(mesh):

time: 204 us -> 177 us (0.87)
  the two profiles are of different devices: /device:TPU:1 before, /device:TPU:73 now
where the time goes in v3:
time: 177 us; the launch traced here: 176 us
  starting transfers between devices  90 us (51%)
  waiting for transfers between devices  33.4 us (19%)
  Pallas kernels  28.9 us (16%)
  local copies, waits for them, and re-layouts  9.96 us (6%)
  other arithmetic  9.13 us (5%)
  matrix products  3.08 us (2%)
    ppermute x13, starting transfers between devices, shift(): return lax.ppermute(v, axis, [(i, (i + by) % n) for i in range(n)])  49.2 us
    all_to_all x6, starting transfers between devices, exchange(): return lax.all_to_all(v, axis, 0, 0)  40.9 us
    all_to_all x6, waiting for transfers between devices, exchange(): return lax.all_to_all(v, axis, 0, 0)  17.2 us
    ppermute x13, waiting for transfers between devices, shift(): return lax.ppermute(v, axis, [(i, (i + by) % n) for i in range(n)])  16.3 us
    pallas_call x1, Pallas kernels, inverses(): pl.pallas_call(inverse_kernel, out_shape=(out, out), in_specs=[spec], out...  10 us
    pallas_call x1, Pallas kernels, solve(): pl.pallas_call(solve_kernel, out_shape=(jax.ShapeDtypeStruct((STEPS, NB,...  8.3 us
    pallas_call x1, Pallas kernels, update(): pl.pallas_call(update_kernel, out_shape=jax.ShapeDtypeStruct(matrix.shape...  6.91 us
  transfers between devices with their start and end apart: 19, of which 9 were waited for; matrix products, arithmetic and copies ran while one was open for 8% of the time, Pallas kernels for 11%

profile of v3, /device:TPU:73, one launch (start us, length us, event | category | flops | bytes accessed | tf_op | source)
XLA Modules:
  0.0 175.7 jit_solution(1938267835634906780)
XLA Ops:
  0.0 1.9 %broadcast_in_dim.70 = bf16[8,6,32,256]{3,2,1,0:T(8,128)(2,1)} broadcast(bf16[6,32,256]{2,1,0:T(8,128)(2,1)} %param.8), dimensions={1,2,3} | broadcast | bytes 884736 | tf_op jit(solution)/shard_map/broadcast_in_dim | solution.py:310
  3.3 7.0 %all-to-all-start.1 = ((bf16[8,6,32,256]{3,2,1,0:T(8,128)(2,1)}), bf16[8,6,32,256]{3,2,1,0:T(8,128)(2,1)S(1)}, u32[]{:S(2)}, u32[]{:S(2)}) async-start(bf16[8,6,32,256]{3,2,1,0:T(8,128)(2,1)} %broadcast_in_dim.70), calls=%async_computation.1 | async-start | bytes 1572864 | tf_op jit(solution)/shard_map/all_to_all | solution.py:67
  10.3 3.1 %fusion.6 = bf16[1536,512]{1,0:T(8,128)(2,1)S(1)} fusion(bf16[1024,512]{1,0:T(8,128)(2,1)} %matrix_ref.1, s32[1024]{0:T(1024)S(1)} %iota_add_fusion, s32[1536]{0:T(1024)S(1)} %eq.103), kind=kOutput, calls=%fused_computation.14 | convolution fusion | flops 1612972032 | bytes 2631680 | tf_op jit(solution)/shard_map/dot_general | solution.py:24
  14.2 3.1 %collective-permute-start = (bf16[6,64,512]{2,1,0:T(8,128)(2,1)}, bf16[6,64,512]{2,1,0:T(8,128)(2,1)}, u32[]{:S(2)}, u32[]{:S(2)}) collective-permute-start(bf16[6,64,512]{2,1,0:T(8,128)(2,1)} %get-tuple-element.134), channel_id=1, source_target_pairs={{0,32},{32,64},{64,96},{96,0},{1,33},{33,65},{65,97},{97,1},{2,34}... | collective-permute-start | bytes 1179656 | tf_op jit(solution)/shard_map/ppermute | solution.py:81
  17.3 4.4 %collective-permute-start.1 = (bf16[6,64,512]{2,1,0:T(8,128)(2,1)S(1)}, bf16[6,64,512]{2,1,0:T(8,128)(2,1)}, u32[]{:S(2)}, u32[]{:S(2)}) collective-permute-start(bf16[6,64,512]{2,1,0:T(8,128)(2,1)S(1)} %get-tuple-element.136), channel_id=1, source_target_pairs={{0,64},{32,96},{64,0},{96,32},{1,65},{33,97},{65,1},{97,33},{2,66}... | collective-permute-start | bytes 1179656 | tf_op jit(solution)/shard_map/ppermute | solution.py:81
  21.7 3.1 %collective-permute-start.2 = (bf16[6,64,512]{2,1,0:T(8,128)(2,1)S(1)}, bf16[6,64,512]{2,1,0:T(8,128)(2,1)}, u32[]{:S(2)}, u32[]{:S(2)}) collective-permute-start(bf16[6,64,512]{2,1,0:T(8,128)(2,1)S(1)} %get-tuple-element.135), channel_id=1, source_target_pairs={{0,96},{32,0},{64,32},{96,64},{1,97},{33,1},{65,33},{97,65},{2,98}... | collective-permute-start | bytes 1179656 | tf_op jit(solution)/shard_map/ppermute | solution.py:81
  25.2 5.3 %all-to-all-done.1.panels_ref.refs_6_.refs_0_ = bf16[8,6,32,256]{3,2,1,0:T(8,128)(2,1)S(1)} async-done(((bf16[8,6,32,256]{3,2,1,0:T(8,128)(2,1)}), bf16[8,6,32,256]{3,2,1,0:T(8,128)(2,1)S(1)}, u32[]{:S(2)}, u32[]{:S(2)}) %all-to-all-start.1) | async-done | bytes 786464 | tf_op jit(solution)/shard_map/all_to_all | solution.py:67
  32.1 5.6 %all-to-all-start.2 = ((bf16[4,4,16,512]{3,2,1,0:T(8,128)(2,1)}), bf16[4,4,16,512]{3,2,1,0:T(8,128)(2,1)S(1)}, u32[]{:S(2)}, u32[]{:S(2)}) async-start(bf16[4,4,16,512]{3,2,1,0:T(8,128)(2,1)} %shard_map.56), calls=%async_computation.2 | async-start | bytes 524288 | tf_op jit(solution)/shard_map/all_to_all | solution.py:67
  39.6 2.3 %all-to-all-done.2 = bf16[4,4,16,512]{3,2,1,0:T(8,128)(2,1)S(1)} async-done(((bf16[4,4,16,512]{3,2,1,0:T(8,128)(2,1)}), bf16[4,4,16,512]{3,2,1,0:T(8,128)(2,1)S(1)}, u32[]{:S(2)}, u32[]{:S(2)}) %all-to-all-start.2) | async-done | bytes 262176 | tf_op jit(solution)/shard_map/all_to_all | solution.py:67
  42.9 9.7 %all-to-all-start.3 = ((bf16[4,10,16,512]{3,2,1,0:T(8,128)(2,1)}), bf16[4,10,16,512]{3,2,1,0:T(8,128)(2,1)}, u32[]{:S(2)}, u32[]{:S(2)}) async-start(bf16[4,10,16,512]{3,2,1,0:T(8,128)(2,1)} %copy.7), calls=%async_computation.3 | async-start | bytes 1310720 | tf_op jit(solution)/shard_map/all_to_all | solution.py:67
  52.6 3.2 %collective-permute-start.6 = (bf16[8,6,32,256]{3,2,1,0:T(8,128)(2,1)S(1)}, bf16[8,6,32,256]{3,2,1,0:T(8,128)(2,1)S(1)}, u32[]{:S(2)}, u32[]{:S(2)}) collective-permute-start(bf16[8,6,32,256]{3,2,1,0:T(8,128)(2,1)S(1)} %all-to-all-done.1.panels_ref.refs_6_.refs_0_), channel_id=1, source_target_pairs={{0,2},{2,0},{1,3},{3,1},{4,6},{6,4},{5,7},{7,5},{8,10},{10,8},{9,1... | collective-permute-start | bytes 2359304 | tf_op jit(solution)/shard_map/ppermute | solution.py:81
  55.8 10.0 %shard_map.57 = (bf16[6,256,256]{2,1,0:T(8,128)(2,1)S(1)}, bf16[6,256,256]{2,1,0:T(8,128)(2,1)S(1)}) custom-call(f32[6,256,256]{2,1,0:T(8,128)S(1)} %copy-done.6), custom_call_target="tpu_custom_call" | custom-call | flops 8455716864 | bytes 3145728 | tf_op jit(solution)/shard_map/pallas_call | solution.py:56
  70.4 4.3 %collective-permute-start.3 = (bf16[6,16,512]{2,1,0:T(8,128)(2,1)S(1)}, bf16[6,16,512]{2,1,0:T(8,128)(2,1)S(1)}, u32[]{:S(2)}, u32[]{:S(2)}) collective-permute-start(bf16[6,16,512]{2,1,0:T(8,128)(2,1)S(1)} %slice_reduce_fusion), channel_id=1, source_target_pairs={{0,128},{128,256},{256,384},{384,0},{1,129},{129,257},{257,385},{3... | collective-permute-start | bytes 294920 | tf_op jit(solution)/shard_map/ppermute | solution.py:81
  74.7 5.2 %collective-permute-start.4 = (bf16[6,16,512]{2,1,0:T(8,128)(2,1)S(1)}, bf16[6,16,512]{2,1,0:T(8,128)(2,1)S(1)}, u32[]{:S(2)}, u32[]{:S(2)}) collective-permute-start(bf16[6,16,512]{2,1,0:T(8,128)(2,1)S(1)} %slice_reduce_fusion), channel_id=1, source_target_pairs={{0,256},{128,384},{256,0},{384,128},{1,257},{129,385},{257,1},{385... | collective-permute-start | bytes 294920 | tf_op jit(solution)/shard_map/ppermute | solution.py:81
  79.9 5.2 %collective-permute-start.5 = (bf16[6,16,512]{2,1,0:T(8,128)(2,1)S(1)}, bf16[6,16,512]{2,1,0:T(8,128)(2,1)S(1)}, u32[]{:S(2)}, u32[]{:S(2)}) collective-permute-start(bf16[6,16,512]{2,1,0:T(8,128)(2,1)S(1)} %slice_reduce_fusion), channel_id=1, source_target_pairs={{0,384},{128,0},{256,128},{384,256},{1,385},{129,1},{257,129},{385... | collective-permute-start | bytes 294920 | tf_op jit(solution)/shard_map/ppermute | solution.py:81
  85.1 4.0 %all-to-all-start.4 = ((bf16[4,4,16,512]{3,2,1,0:T(8,128)(2,1)}), bf16[4,4,16,512]{3,2,1,0:T(8,128)(2,1)S(1)}, u32[]{:S(2)}, u32[]{:S(2)}) async-start(bf16[4,4,16,512]{3,2,1,0:T(8,128)(2,1)} %broadcast_in_dim.107), calls=%async_computation.4 | async-start | bytes 524288 | tf_op jit(solution)/shard_map/all_to_all | solution.py:67
  89.2 4.0 %collective-permute-done.4 = bf16[6,16,512]{2,1,0:T(8,128)(2,1)S(1)} collective-permute-done((bf16[6,16,512]{2,1,0:T(8,128)(2,1)S(1)}, bf16[6,16,512]{2,1,0:T(8,128)(2,1)S(1)}, u32[]{:S(2)}, u32[]{:S(2)}) %collective-permute-start.4) | collective-permute-done | bytes 98336 | tf_op jit(solution)/shard_map/ppermute | solution.py:81
  93.2 1.8 %all-to-all-done.4 = bf16[4,4,16,512]{3,2,1,0:T(8,128)(2,1)S(1)} async-done(((bf16[4,4,16,512]{3,2,1,0:T(8,128)(2,1)}), bf16[4,4,16,512]{3,2,1,0:T(8,128)(2,1)S(1)}, u32[]{:S(2)}, u32[]{:S(2)}) %all-to-all-start.4) | async-done | bytes 262176 | tf_op jit(solution)/shard_map/all_to_all | solution.py:67
  96.3 5.6 %all-to-all-start.5 = ((bf16[16,4,16,512]{3,2,1,0:T(8,128)(2,1)}), bf16[16,4,16,512]{3,2,1,0:T(8,128)(2,1)S(1)}, u32[]{:S(2)}, u32[]{:S(2)}) async-start(bf16[16,4,16,512]{3,2,1,0:T(8,128)(2,1)} %broadcast_in_dim.108), calls=%async_computation.5 | async-start | bytes 2097152 | tf_op jit(solution)/shard_map/all_to_all | solution.py:67
  101.9 4.2 %collective-permute-start.11 = (bf16[4,6,16,512]{3,2,1,0:T(8,128)(2,1)S(1)}, bf16[4,6,16,512]{3,2,1,0:T(8,128)(2,1)S(1)}, u32[]{:S(2)}, u32[]{:S(2)}) collective-permute-start(bf16[4,6,16,512]{3,2,1,0:T(8,128)(2,1)S(1)} %pad_maximum_fusion.1.refs_0_), channel_id=1, source_target_pairs={{0,32},{32,64},{64,96},{96,0},{1,33},{33,65},{65,97},{97,1},{2,34}... | collective-permute-start | bytes 1179656 | tf_op jit(solution)/shard_map/ppermute | solution.py:81
  106.2 5.1 %collective-permute-start.9 = (bf16[8,6,32,256]{3,2,1,0:T(8,128)(2,1)S(1)}, bf16[8,6,32,256]{3,2,1,0:T(8,128)(2,1)S(1)}, u32[]{:S(2)}, u32[]{:S(2)}) collective-permute-start(bf16[8,6,32,256]{3,2,1,0:T(8,128)(2,1)S(1)} %all-to-all-done.1.panels_ref.refs_6_.refs_0_), channel_id=1, source_target_pairs={{0,1},{1,0},{2,3},{3,2},{4,5},{5,4},{6,7},{7,6},{8,9},{9,8},{10,11... | collective-permute-start | bytes 2359304 | tf_op jit(solution)/shard_map/ppermute | solution.py:81
  111.3 3.3 %collective-permute-start.7 = (bf16[4,6,16,512]{3,2,1,0:T(8,128)(2,1)S(1)}, bf16[4,6,16,512]{3,2,1,0:T(8,128)(2,1)S(1)}, u32[]{:S(2)}, u32[]{:S(2)}) collective-permute-start(bf16[4,6,16,512]{3,2,1,0:T(8,128)(2,1)S(1)} %pad_maximum_fusion.1.refs_0_), channel_id=1, source_target_pairs={{0,64},{32,96},{64,0},{96,32},{1,65},{33,97},{65,1},{97,33},{2,66}... | collective-permute-start | bytes 1179656 | tf_op jit(solution)/shard_map/ppermute | solution.py:81
  114.7 2.7 %collective-permute-start.8 = (bf16[4,6,16,512]{3,2,1,0:T(8,128)(2,1)S(1)}, bf16[4,6,16,512]{3,2,1,0:T(8,128)(2,1)S(1)}, u32[]{:S(2)}, u32[]{:S(2)}) collective-permute-start(bf16[4,6,16,512]{3,2,1,0:T(8,128)(2,1)S(1)} %pad_maximum_fusion.1.refs_0_), channel_id=1, source_target_pairs={{0,96},{32,0},{64,32},{96,64},{1,97},{33,1},{65,33},{97,65},{2,98}... | collective-permute-start | bytes 1179656 | tf_op jit(solution)/shard_map/ppermute | solution.py:81
  117.3 2.5 %collective-permute-start.10 = (bf16[8,6,32,256]{3,2,1,0:T(8,128)(2,1)S(1)}, bf16[8,6,32,256]{3,2,1,0:T(8,128)(2,1)}, u32[]{:S(2)}, u32[]{:S(2)}) collective-permute-start(bf16[8,6,32,256]{3,2,1,0:T(8,128)(2,1)S(1)} %collective-permute-done.6.refs_8_.refs_2_), channel_id=1, source_target_pairs={{0,1},{1,0},{2,3},{3,2},{4,5},{5,4},{6,7},{7,6},{8,9},{9,8},{10,11... | collective-permute-start | bytes 2359304 | tf_op jit(solution)/shard_map/ppermute | solution.py:81
  123.3 2.1 %collective-permute-done.7.refs_2_ = bf16[4,6,16,512]{3,2,1,0:T(8,128)(2,1)S(1)} collective-permute-done((bf16[4,6,16,512]{3,2,1,0:T(8,128)(2,1)S(1)}, bf16[4,6,16,512]{3,2,1,0:T(8,128)(2,1)S(1)}, u32[]{:S(2)}, u32[]{:S(2)}) %collective-permute-start.7) | collective-permute-done | bytes 393248 | tf_op jit(solution)/shard_map/ppermute | solution.py:81
  125.4 7.4 %collective-permute-done.8.refs_3_ = bf16[4,6,16,512]{3,2,1,0:T(8,128)(2,1)S(1)} collective-permute-done((bf16[4,6,16,512]{3,2,1,0:T(8,128)(2,1)S(1)}, bf16[4,6,16,512]{3,2,1,0:T(8,128)(2,1)S(1)}, u32[]{:S(2)}, u32[]{:S(2)}) %collective-permute-start.8) | collective-permute-done | bytes 393248 | tf_op jit(solution)/shard_map/ppermute | solution.py:81
  133.6 2.9 %collective-permute-start.12 = (bf16[8,2,4,16,512]{4,3,2,1,0:T(8,128)(2,1)S(1)}, bf16[8,2,4,16,512]{4,3,2,1,0:T(8,128)(2,1)}, u32[]{:S(2)}, u32[]{:S(2)}) collective-permute-start(bf16[8,2,4,16,512]{4,3,2,1,0:T(8,128)(2,1)S(1)} %bitcast.49), channel_id=1, source_target_pairs={{0,1},{1,0},{2,3},{3,2},{4,5},{5,4},{6,7},{7,6},{8,9},{9,8},{10,11... | collective-permute-start | bytes 3145736 | tf_op jit(solution)/shard_map/ppermute | solution.py:81
  136.6 2.2 %collective-permute-done.12.refs_5_ = bf16[8,2,4,16,512]{4,3,2,1,0:T(8,128)(2,1)} collective-permute-done((bf16[8,2,4,16,512]{4,3,2,1,0:T(8,128)(2,1)S(1)}, bf16[8,2,4,16,512]{4,3,2,1,0:T(8,128)(2,1)}, u32[]{:S(2)}, u32[]{:S(2)}) %collective-permute-start.12) | collective-permute-done | bytes 1048608 | tf_op jit(solution)/shard_map/ppermute | solution.py:81
  138.8 8.3 %shard_map.58 = (bf16[6,256,512]{2,1,0:T(8,128)(2,1)}, bf16[256,512]{1,0:T(8,128)(2,1)S(1)}, bf16[512,512]{1,0:T(8,128)(2,1)}) custom-call(s32[4]{0:T(128)} %copy-done.5, s32[1,256]{1,0:T(1,128)} %get-tuple-element.96.slot_ref, bf16[6,256,256]{2,1,0:T(8,128)(2,1)} %copy-done.1, bf16[6,256,256]{2,1,0:T(8,128)(2,1)} %copy-done.2, ...), custom_call_target="tpu_custom_call" | custom-call | flops 2348810240 | bytes 9437184 | tf_op jit(solution)/shard_map/pallas_call | solution.py:182
  147.1 8.9 %all-to-all-start.6 = ((bf16[16,32,512]{2,1,0:T(8,128)(2,1)}), bf16[16,32,512]{2,1,0:T(8,128)(2,1)S(1)}, u32[]{:S(2)}, u32[]{:S(2)}) async-start(bf16[16,32,512]{2,1,0:T(8,128)(2,1)} %bitcast.54), calls=%async_computation.6 | async-start | bytes 1048576 | tf_op jit(solution)/shard_map/all_to_all | solution.py:67
  159.4 6.9 %shard_map.59 = f32[1024,512]{1,0:T(8,128)S(1)} custom-call(s32[4]{0:T(128)} %copy-done.5, s32[1024,128]{1,0:T(8,128)} %broadcast_in_dim.113.last_ref, bf16[6,256,512]{2,1,0:T(8,128)(2,1)} %get-tuple-element.107.u_ref, bf16[1024,512]{1,0:T(8,128)(2,1)} %matrix_ref.1, bf16[8,6,32,256]{3,2,1,0:T(8,128)(2,1)} %copy-done, bf16[8,6,32,256]{3,2,1,0:T(8,128)(2,1)} %copy-done.9, ...), custom_call_target="tpu_custom_call" | custom-call | flops 1610612736 | bytes 8388608 | tf_op jit(solution)/shard_map/pallas_call | solution.py:239
  166.5 7.8 %all-to-all-done.6.got_ref = bf16[16,32,512]{2,1,0:T(8,128)(2,1)S(1)} async-done(((bf16[16,32,512]{2,1,0:T(8,128)(2,1)}), bf16[16,32,512]{2,1,0:T(8,128)(2,1)S(1)}, u32[]{:S(2)}, u32[]{:S(2)}) %all-to-all-start.6) | async-done | bytes 524320 | tf_op jit(solution)/shard_map/all_to_all | solution.py:67
  (89 shorter events, 21.5 us)
Async XLA Ops:
  3.3 27.3 %all-to-all-start.1 = ((bf16[8,6,32,256]{3,2,1,0:T(8,128)(2,1)}), bf16[8,6,32,256]{3,2,1,0:T(8,128)(2,1)S(1)}, u32[]{:S(2)}, u32[]{:S(2)}) async-start(bf16[8,6,32,256]{3,2,1,0:T(8,128)(2,1)} %broadcast_in_dim.70), calls=%async_computation.1 | async-start | bytes 1572864 | tf_op jit(solution)/shard_map/all_to_all | solution.py:67
  13.3 11.4 %copy-start.14 = (s32[8,2,2]{0,2,1:T(2,128)S(1)}, s32[8,2,2]{0,2,1:T(2,128)}, u32[]{:S(2)}) copy-start(s32[8,2,2]{0,2,1:T(2,128)} %constant.183) | copy-start | bytes 388
  13.3 11.6 %copy-start.4 = (s32[6,256]{1,0:T(8,128)S(1)}, s32[6,256]{1,0:T(8,128)}, u32[]{:S(2)}) copy-start(s32[6,256]{1,0:T(8,128)} %pivots_ref) | copy-start | bytes 18436
  14.2 23.5 %collective-permute-start = (bf16[6,64,512]{2,1,0:T(8,128)(2,1)}, bf16[6,64,512]{2,1,0:T(8,128)(2,1)}, u32[]{:S(2)}, u32[]{:S(2)}) collective-permute-start(bf16[6,64,512]{2,1,0:T(8,128)(2,1)} %get-tuple-element.134), channel_id=1, source_target_pairs={{0,32},{32,64},{64,96},{96,0},{1,33},{33,65},{65,97},{97,1},{2,34}... | collective-permute-start | bytes 1179656 | tf_op jit(solution)/shard_map/ppermute | solution.py:81
  17.3 20.4 %collective-permute-start.1 = (bf16[6,64,512]{2,1,0:T(8,128)(2,1)S(1)}, bf16[6,64,512]{2,1,0:T(8,128)(2,1)}, u32[]{:S(2)}, u32[]{:S(2)}) collective-permute-start(bf16[6,64,512]{2,1,0:T(8,128)(2,1)S(1)} %get-tuple-element.136), channel_id=1, source_target_pairs={{0,64},{32,96},{64,0},{96,32},{1,65},{33,97},{65,1},{97,33},{2,66}... | collective-permute-start | bytes 1179656 | tf_op jit(solution)/shard_map/ppermute | solution.py:81
  21.7 16.6 %collective-permute-start.2 = (bf16[6,64,512]{2,1,0:T(8,128)(2,1)S(1)}, bf16[6,64,512]{2,1,0:T(8,128)(2,1)}, u32[]{:S(2)}, u32[]{:S(2)}) collective-permute-start(bf16[6,64,512]{2,1,0:T(8,128)(2,1)S(1)} %get-tuple-element.135), channel_id=1, source_target_pairs={{0,96},{32,0},{64,32},{96,64},{1,97},{33,1},{65,33},{97,65},{2,98}... | collective-permute-start | bytes 1179656 | tf_op jit(solution)/shard_map/ppermute | solution.py:81
  24.9 17.0 %copy-start.5 = (s32[4]{0:T(128)}, s32[4]{0:T(128)S(1)}, u32[]{:S(2)}) copy-start(s32[4]{0:T(128)S(1)} %pad_add_fusion.at_ref) | copy-start | bytes 52
  30.5 75.6 %copy-start = (bf16[8,6,32,256]{3,2,1,0:T(8,128)(2,1)}, bf16[8,6,32,256]{3,2,1,0:T(8,128)(2,1)S(1)}, u32[]{:S(2)}) copy-start(bf16[8,6,32,256]{3,2,1,0:T(8,128)(2,1)S(1)} %all-to-all-done.1.panels_ref.refs_6_.refs_0_) | copy-start | bytes 2359300
  32.1 9.7 %all-to-all-start.2 = ((bf16[4,4,16,512]{3,2,1,0:T(8,128)(2,1)}), bf16[4,4,16,512]{3,2,1,0:T(8,128)(2,1)S(1)}, u32[]{:S(2)}, u32[]{:S(2)}) async-start(bf16[4,4,16,512]{3,2,1,0:T(8,128)(2,1)} %shard_map.56), calls=%async_computation.2 | async-start | bytes 524288 | tf_op jit(solution)/shard_map/all_to_all | solution.py:67
  41.9 13.9 %copy-start.6 = (f32[6,256,256]{2,1,0:T(8,128)S(1)}, f32[6,256,256]{2,1,0:T(8,128)}, u32[]{:S(2)}) copy-start(f32[6,256,256]{2,1,0:T(8,128)} %l_ref) | copy-start | bytes 4718596
  42.9 24.8 %all-to-all-start.3 = ((bf16[4,10,16,512]{3,2,1,0:T(8,128)(2,1)}), bf16[4,10,16,512]{3,2,1,0:T(8,128)(2,1)}, u32[]{:S(2)}, u32[]{:S(2)}) async-start(bf16[4,10,16,512]{3,2,1,0:T(8,128)(2,1)} %copy.7), calls=%async_computation.3 | async-start | bytes 1310720 | tf_op jit(solution)/shard_map/all_to_all | solution.py:67
  52.6 42.4 %collective-permute-start.6 = (bf16[8,6,32,256]{3,2,1,0:T(8,128)(2,1)S(1)}, bf16[8,6,32,256]{3,2,1,0:T(8,128)(2,1)S(1)}, u32[]{:S(2)}, u32[]{:S(2)}) collective-permute-start(bf16[8,6,32,256]{3,2,1,0:T(8,128)(2,1)S(1)} %all-to-all-done.1.panels_ref.refs_6_.refs_0_), channel_id=1, source_target_pairs={{0,2},{2,0},{1,3},{3,1},{4,6},{6,4},{5,7},{7,5},{8,10},{10,8},{9,1... | collective-permute-start | bytes 2359304 | tf_op jit(solution)/shard_map/ppermute | solution.py:81
  65.9 0.9 copy-start.1
  66.8 0.9 copy-start.2
  70.4 18.7 %collective-permute-start.3 = (bf16[6,16,512]{2,1,0:T(8,128)(2,1)S(1)}, bf16[6,16,512]{2,1,0:T(8,128)(2,1)S(1)}, u32[]{:S(2)}, u32[]{:S(2)}) collective-permute-start(bf16[6,16,512]{2,1,0:T(8,128)(2,1)S(1)} %slice_reduce_fusion), channel_id=1, source_target_pairs={{0,128},{128,256},{256,384},{384,0},{1,129},{129,257},{257,385},{3... | collective-permute-start | bytes 294920 | tf_op jit(solution)/shard_map/ppermute | solution.py:81
  74.7 18.4 %collective-permute-start.4 = (bf16[6,16,512]{2,1,0:T(8,128)(2,1)S(1)}, bf16[6,16,512]{2,1,0:T(8,128)(2,1)S(1)}, u32[]{:S(2)}, u32[]{:S(2)}) collective-permute-start(bf16[6,16,512]{2,1,0:T(8,128)(2,1)S(1)} %slice_reduce_fusion), channel_id=1, source_target_pairs={{0,256},{128,384},{256,0},{384,128},{1,257},{129,385},{257,1},{385... | collective-permute-start | bytes 294920 | tf_op jit(solution)/shard_map/ppermute | solution.py:81
  79.9 13.2 %collective-permute-start.5 = (bf16[6,16,512]{2,1,0:T(8,128)(2,1)S(1)}, bf16[6,16,512]{2,1,0:T(8,128)(2,1)S(1)}, u32[]{:S(2)}, u32[]{:S(2)}) collective-permute-start(bf16[6,16,512]{2,1,0:T(8,128)(2,1)S(1)} %slice_reduce_fusion), channel_id=1, source_target_pairs={{0,384},{128,0},{256,128},{384,256},{1,385},{129,1},{257,129},{385... | collective-permute-start | bytes 294920 | tf_op jit(solution)/shard_map/ppermute | solution.py:81
  85.1 9.8 %all-to-all-start.4 = ((bf16[4,4,16,512]{3,2,1,0:T(8,128)(2,1)}), bf16[4,4,16,512]{3,2,1,0:T(8,128)(2,1)S(1)}, u32[]{:S(2)}, u32[]{:S(2)}) async-start(bf16[4,4,16,512]{3,2,1,0:T(8,128)(2,1)} %broadcast_in_dim.107), calls=%async_computation.4 | async-start | bytes 524288 | tf_op jit(solution)/shard_map/all_to_all | solution.py:67
  93.2 45.5 %copy-start.10 = (bf16[4,6,16,512]{3,2,1,0:T(8,128)(2,1)}, bf16[4,6,16,512]{3,2,1,0:T(8,128)(2,1)S(1)}, u32[]{:S(2)}) copy-start(bf16[4,6,16,512]{3,2,1,0:T(8,128)(2,1)S(1)} %pad_maximum_fusion.1.refs_0_) | copy-start | bytes 1179652
  95.0 43.7 %copy-start.8 = (bf16[8,6,32,256]{3,2,1,0:T(8,128)(2,1)}, bf16[8,6,32,256]{3,2,1,0:T(8,128)(2,1)S(1)}, u32[]{:S(2)}) copy-start(bf16[8,6,32,256]{3,2,1,0:T(8,128)(2,1)S(1)} %collective-permute-done.6.refs_8_.refs_2_) | copy-start | bytes 2359300
  96.3 37.4 %all-to-all-start.5 = ((bf16[16,4,16,512]{3,2,1,0:T(8,128)(2,1)}), bf16[16,4,16,512]{3,2,1,0:T(8,128)(2,1)S(1)}, u32[]{:S(2)}, u32[]{:S(2)}) async-start(bf16[16,4,16,512]{3,2,1,0:T(8,128)(2,1)} %broadcast_in_dim.108), calls=%async_computation.5 | async-start | bytes 2097152 | tf_op jit(solution)/shard_map/all_to_all | solution.py:67
  101.9 17.9 %collective-permute-start.11 = (bf16[4,6,16,512]{3,2,1,0:T(8,128)(2,1)S(1)}, bf16[4,6,16,512]{3,2,1,0:T(8,128)(2,1)S(1)}, u32[]{:S(2)}, u32[]{:S(2)}) collective-permute-start(bf16[4,6,16,512]{3,2,1,0:T(8,128)(2,1)S(1)} %pad_maximum_fusion.1.refs_0_), channel_id=1, source_target_pairs={{0,32},{32,64},{64,96},{96,0},{1,33},{33,65},{65,97},{97,1},{2,34}... | collective-permute-start | bytes 1179656 | tf_op jit(solution)/shard_map/ppermute | solution.py:81
  106.2 17.1 %collective-permute-start.9 = (bf16[8,6,32,256]{3,2,1,0:T(8,128)(2,1)S(1)}, bf16[8,6,32,256]{3,2,1,0:T(8,128)(2,1)S(1)}, u32[]{:S(2)}, u32[]{:S(2)}) collective-permute-start(bf16[8,6,32,256]{3,2,1,0:T(8,128)(2,1)S(1)} %all-to-all-done.1.panels_ref.refs_6_.refs_0_), channel_id=1, source_target_pairs={{0,1},{1,0},{2,3},{3,2},{4,5},{5,4},{6,7},{7,6},{8,9},{9,8},{10,11... | collective-permute-start | bytes 2359304 | tf_op jit(solution)/shard_map/ppermute | solution.py:81
  111.3 14.1 %collective-permute-start.7 = (bf16[4,6,16,512]{3,2,1,0:T(8,128)(2,1)S(1)}, bf16[4,6,16,512]{3,2,1,0:T(8,128)(2,1)S(1)}, u32[]{:S(2)}, u32[]{:S(2)}) collective-permute-start(bf16[4,6,16,512]{3,2,1,0:T(8,128)(2,1)S(1)} %pad_maximum_fusion.1.refs_0_), channel_id=1, source_target_pairs={{0,64},{32,96},{64,0},{96,32},{1,65},{33,97},{65,1},{97,33},{2,66}... | collective-permute-start | bytes 1179656 | tf_op jit(solution)/shard_map/ppermute | solution.py:81
  114.7 18.2 %collective-permute-start.8 = (bf16[4,6,16,512]{3,2,1,0:T(8,128)(2,1)S(1)}, bf16[4,6,16,512]{3,2,1,0:T(8,128)(2,1)S(1)}, u32[]{:S(2)}, u32[]{:S(2)}) collective-permute-start(bf16[4,6,16,512]{3,2,1,0:T(8,128)(2,1)S(1)} %pad_maximum_fusion.1.refs_0_), channel_id=1, source_target_pairs={{0,96},{32,0},{64,32},{96,64},{1,97},{33,1},{65,33},{97,65},{2,98}... | collective-permute-start | bytes 1179656 | tf_op jit(solution)/shard_map/ppermute | solution.py:81
  117.3 16.3 %collective-permute-start.10 = (bf16[8,6,32,256]{3,2,1,0:T(8,128)(2,1)S(1)}, bf16[8,6,32,256]{3,2,1,0:T(8,128)(2,1)}, u32[]{:S(2)}, u32[]{:S(2)}) collective-permute-start(bf16[8,6,32,256]{3,2,1,0:T(8,128)(2,1)S(1)} %collective-permute-done.6.refs_8_.refs_2_), channel_id=1, source_target_pairs={{0,1},{1,0},{2,3},{3,2},{4,5},{5,4},{6,7},{7,6},{8,9},{9,8},{10,11... | collective-permute-start | bytes 2359304 | tf_op jit(solution)/shard_map/ppermute | solution.py:81
  119.8 18.9 %copy-start.11 = (bf16[4,6,16,512]{3,2,1,0:T(8,128)(2,1)}, bf16[4,6,16,512]{3,2,1,0:T(8,128)(2,1)S(1)}, u32[]{:S(2)}) copy-start(bf16[4,6,16,512]{3,2,1,0:T(8,128)(2,1)S(1)} %collective-permute-done.11.refs_1_) | copy-start | bytes 1179652
  123.3 9.5 %copy-start.9 = (bf16[8,6,32,256]{3,2,1,0:T(8,128)(2,1)}, bf16[8,6,32,256]{3,2,1,0:T(8,128)(2,1)S(1)}, u32[]{:S(2)}) copy-start(bf16[8,6,32,256]{3,2,1,0:T(8,128)(2,1)S(1)} %collective-permute-done.9.refs_7_.refs_1_) | copy-start | bytes 2359300
  125.4 7.4 %copy-start.12 = (bf16[4,6,16,512]{3,2,1,0:T(8,128)(2,1)}, bf16[4,6,16,512]{3,2,1,0:T(8,128)(2,1)S(1)}, u32[]{:S(2)}) copy-start(bf16[4,6,16,512]{3,2,1,0:T(8,128)(2,1)S(1)} %collective-permute-done.7.refs_2_) | copy-start | bytes 1179652
  133.6 5.1 %copy-start.7 = (bf16[16,4,16,512]{3,2,1,0:T(8,128)(2,1)}, bf16[16,4,16,512]{3,2,1,0:T(8,128)(2,1)S(1)}, u32[]{:S(2)}) copy-start(bf16[16,4,16,512]{3,2,1,0:T(8,128)(2,1)S(1)} %all-to-all-done.5) | copy-start | bytes 3145732
  133.6 5.1 %collective-permute-start.12 = (bf16[8,2,4,16,512]{4,3,2,1,0:T(8,128)(2,1)S(1)}, bf16[8,2,4,16,512]{4,3,2,1,0:T(8,128)(2,1)}, u32[]{:S(2)}, u32[]{:S(2)}) collective-permute-start(bf16[8,2,4,16,512]{4,3,2,1,0:T(8,128)(2,1)S(1)} %bitcast.49), channel_id=1, source_target_pairs={{0,1},{1,0},{2,3},{3,2},{4,5},{5,4},{6,7},{7,6},{8,9},{9,8},{10,11... | collective-permute-start | bytes 3145736 | tf_op jit(solution)/shard_map/ppermute | solution.py:81
  147.1 27.3 %all-to-all-start.6 = ((bf16[16,32,512]{2,1,0:T(8,128)(2,1)}), bf16[16,32,512]{2,1,0:T(8,128)(2,1)S(1)}, u32[]{:S(2)}, u32[]{:S(2)}) async-start(bf16[16,32,512]{2,1,0:T(8,128)(2,1)} %bitcast.54), calls=%async_computation.6 | async-start | bytes 1048576 | tf_op jit(solution)/shard_map/all_to_all | solution.py:67
  (2 other events, 1.4 us)

commit v4 on v3

--- a/solution.py
+++ b/solution.py
@@ -12,6 +12,7 @@
 FINE = ("zh", "x", "y", "zl", "c")
 PAIRS = [(s, k) for k in range(STEPS) for s in range(k + 1, STEPS)] + [(0, 0)]
 PLACE = {pair: n for n, pair in enumerate(PAIRS)}
+CAP = 144
 SLOTS = 32
 
 
@@ -124,16 +125,12 @@
 
 
 def solve_kernel(at_ref, slot_ref, high_ref, low_ref, matrix_ref, *refs):
-    active_in, blocks_in, panels_in = refs[:4], refs[4:6], refs[6:10]
-    u_ref, old_ref, send_ref, active, blocks, panels, active_sem, blocks_sem, panels_sem = refs[10:]
+    active_in, blocks_in, panels_in = refs[0], refs[1:3], refs[3:7]
+    u_ref, old_ref, send_ref, active, blocks, panels, active_sem, blocks_sem, panels_sem = refs[7:]
     zh, x, zl, c = at_ref[0], at_ref[1], at_ref[2], at_ref[3]
     me = zh * 4 + x
     width = matrix_ref.shape[1]
-    copies = []
-    for d in range(4):
-        for e in range(4):
-            target = active.at[lax.rem(x - d + 4, 4), lax.rem(zh - e + 4, 4)]
-            copies.append(pltpu.make_async_copy(active_in[d].at[e], target, active_sem.at[d * 4 + e]))
+    copies = [pltpu.make_async_copy(active_in, active, active_sem.at[0])]
     for n in range(2):
         target = blocks.at[:, :, lax.rem(c + n, 2)]
         copies.append(pltpu.make_async_copy(blocks_in[n], target, blocks_sem.at[n]))
@@ -142,11 +139,11 @@
         copies.append(pltpu.make_async_copy(panels_in[n].at[0:2], panels.at[:, a, b], panels_sem.at[n]))
     for copy in copies:
         copy.start()
-    for copy in copies[:16]:
+    for copy in copies[:1]:
         copy.wait()
 
     def rows_of(n):
-        return active[:, :, n].reshape(NB, width)
+        return active[n]
 
     old_ref[...] = matrix_ref[0:NB, :]
     for s in range(STEPS):
@@ -155,14 +152,14 @@
         u_ref[s] = u
 
         if s == 0:
-            for copy in copies[16:]:
+            for copy in copies[1:]:
                 copy.wait()
         for t in range(s + 1, STEPS):
             n = PLACE[(t, s)]
             left = n // 2 % 2 * NB
             block = blocks[n % 2 * 4 : n % 2 * 4 + 4, :, :, n // 4, :, left : left + NB].reshape(NB, NB)
             less = rows_of(t).astype(jnp.float32) - dot(block, u)
-            active[:, :, t] = less.astype(jnp.bfloat16).reshape(4, 4, 16, width)
+            active[t] = less.astype(jnp.bfloat16)
 
     for s in range(STEPS - 1):
 
@@ -186,19 +183,19 @@
             jax.ShapeDtypeStruct((NB, width), jnp.bfloat16),
             jax.ShapeDtypeStruct((16 * SLOTS, width), jnp.bfloat16),
         ),
-        in_specs=[pl.BlockSpec(memory_space=pltpu.SMEM)] + [vmem] * 4 + [anywhere] * 10,
+        in_specs=[pl.BlockSpec(memory_space=pltpu.SMEM)] + [vmem] * 4 + [anywhere] * 7,
         out_specs=(vmem,) * 3,
         scratch_shapes=[
-            pltpu.VMEM((4, 4, STEPS, 16, width), jnp.bfloat16),
+            pltpu.VMEM((STEPS, NB, width), jnp.bfloat16),
             pltpu.VMEM((8, 2, 2, 4, 16, 2 * NB), jnp.bfloat16),
             pltpu.VMEM((2, 2, 2, STEPS, 32, NB), jnp.bfloat16),
-            pltpu.SemaphoreType.DMA((16,)),
+            pltpu.SemaphoreType.DMA((1,)),
             pltpu.SemaphoreType.DMA((2,)),
             pltpu.SemaphoreType.DMA((4,)),
         ],
         compiler_params=pltpu.CompilerParams(vmem_limit_bytes=58 * 2**20),
         cost_estimate=pl.CostEstimate(flops=2 * 35 * NB * NB * width, bytes_accessed=9 * 2**20, transcendentals=0),
-    )(at, slot, high, low, matrix, *active, *blocks, *panels)
+    )(at, slot, high, low, matrix, active, *blocks, *panels)
 
 
 def update_kernel(at_ref, last_ref, u_ref, matrix_ref, *refs):
@@ -269,10 +266,14 @@
     )(put, got, total)
 
 
-def origin_kernel(pivots_ref, origin_ref, base_ref):
+def origin_kernel(pivots_ref, origin_ref, base_ref, rank_ref):
     rows = pivots_ref[...]
     columns = jnp.transpose(jnp.concatenate([rows, rows[: 8 - STEPS]], axis=0))
-    index = lax.broadcasted_iota(jnp.int32, (NB, NB), 0).astype(jnp.float32)
+    down = lax.broadcasted_iota(jnp.int32, (NB, NB), 0)
+    index = down.astype(jnp.float32)
+    earlier = jnp.where(down < lax.broadcasted_iota(jnp.int32, (NB, NB), 1), 1.0, 0.0).astype(jnp.bfloat16)
+    prow = lax.broadcasted_iota(jnp.int32, (16, NB), 0)
+    so_far = jnp.zeros((16, 1), jnp.float32)
     for s in range(STEPS):
         row = rows[s : s + 1]
         latest = jnp.full((1, NB), -1.0, jnp.float32)
@@ -280,8 +281,13 @@
             code = jnp.where(columns[:, t : t + 1] == row, index + float(t * ROWS), -1.0)
             latest = jnp.maximum(latest, jnp.max(code, axis=0, keepdims=True))
         latest = latest.astype(jnp.int32)
+        base = jnp.where(latest >= 0, latest, row)
         origin_ref[s : s + 1, :] = latest
-        base_ref[s : s + 1, :] = jnp.where(latest >= 0, latest, row)
+        base_ref[s : s + 1, :] = base
+        holds = jnp.where(prow == base // ROWS, 1.0, 0.0)
+        ahead = dot(holds.astype(jnp.bfloat16), earlier) + so_far
+        rank_ref[s : s + 1, :] = jnp.sum(holds * ahead, axis=0, keepdims=True).astype(jnp.int32)
+        so_far = so_far + jnp.sum(holds, axis=1, keepdims=True)
 
 
 def origins(pivots):
@@ -289,12 +295,74 @@
     out = jax.ShapeDtypeStruct(pivots.shape, jnp.int32)
     return pl.pallas_call(
         origin_kernel,
-        out_shape=(out, out),
+        out_shape=(out,) * 3,
         in_specs=[vmem],
-        out_specs=(vmem, vmem),
+        out_specs=(vmem,) * 3,
         compiler_params=pltpu.CompilerParams(vmem_limit_bytes=16 * 2**20),
         cost_estimate=pl.CostEstimate(flops=1000, bytes_accessed=20000, transcendentals=0),
     )(pivots)
+
+
+def pack_kernel(at_ref, base_ref, rank_ref, matrix_ref, out_ref):
+    me, skip = at_ref[0], at_ref[1]
+    slot = lax.broadcasted_iota(jnp.int32, (CAP, NB), 0)
+    ids = jnp.zeros((CAP, 1), jnp.float32)
+    for s in range(STEPS):
+        base = base_ref[s : s + 1, :]
+        code = jnp.where(base // ROWS == me, rank_ref[s : s + 1, :] - skip, -1)
+        ids = ids + jnp.sum(jnp.where(slot == code, (base + 1).astype(jnp.float32), 0.0), axis=1, keepdims=True)
+    local = ids.astype(jnp.int32) - 1 - me * ROWS
+    put = jnp.where(lax.broadcasted_iota(jnp.int32, (CAP, ROWS), 1) == local, 1.0, 0.0).astype(jnp.bfloat16)
+    out_ref[...] = dot(put, matrix_ref[...]).astype(jnp.bfloat16)
+
+
+def pack(me, skip, base, rank, matrix):
+    vmem = pl.BlockSpec(memory_space=pltpu.VMEM)
+    return pl.pallas_call(
+        pack_kernel,
+        out_shape=jax.ShapeDtypeStruct((CAP, matrix.shape[1]), jnp.bfloat16),
+        in_specs=[pl.BlockSpec(memory_space=pltpu.SMEM)] + [vmem] * 3,
+        out_specs=vmem,
+        compiler_params=pltpu.CompilerParams(vmem_limit_bytes=16 * 2**20),
+        cost_estimate=pl.CostEstimate(flops=2 * CAP * matrix.size, bytes_accessed=2**20, transcendentals=0),
+    )(jnp.stack([me, skip]).astype(jnp.int32), base, rank, matrix)
+
+
+def unpack_kernel(at_ref, base_ref, rank_ref, *refs):
+    parts, (out_ref, rows, sem) = refs[:4], refs[4:]
+    zh, x, skip = at_ref[0], at_ref[1], at_ref[2]
+    copies = []
+    for d in range(4):
+        for e in range(4):
+            target = rows.at[lax.rem(zh - e + 4, 4) * 4 + lax.rem(x - d + 4, 4)]
+            copies.append(pltpu.make_async_copy(parts[d].at[e], target, sem.at[d * 4 + e]))
+    for copy in copies:
+        copy.start()
+    rank = rank_ref[...] - skip
+    code = jnp.where((rank >= 0) & (rank < CAP), base_ref[...] // ROWS * CAP + rank, -1)
+    columns = jnp.transpose(jnp.concatenate([code, code[: 8 - STEPS]], axis=0))
+    place = lax.broadcasted_iota(jnp.int32, (NB, 16 * CAP), 1)
+    for copy in copies:
+        copy.wait()
+    for s in range(STEPS):
+        put = jnp.where(columns[:, s : s + 1] == place, 1.0, 0.0).astype(jnp.bfloat16)
+        out_ref[s] = dot(put, rows[...].reshape(16 * CAP, rows.shape[2])).astype(jnp.bfloat16)
+
+
+def unpack(zh, x, skip, base, rank, parts):
+    width = parts[0].shape[2]
+    vmem, anywhere = pl.BlockSpec(memory_space=pltpu.VMEM), pl.BlockSpec(memory_space=pl.ANY)
+    return pl.pallas_call(
+        unpack_kernel,
+        out_shape=jax.ShapeDtypeStruct((STEPS, NB, width), jnp.bfloat16),
+        in_specs=[pl.BlockSpec(memory_space=pltpu.SMEM)] + [vmem] * 2 + [anywhere] * 4,
+        out_specs=vmem,
+        scratch_shapes=[pltpu.VMEM((16, CAP, width), jnp.bfloat16), pltpu.SemaphoreType.DMA((16,))],
+        compiler_params=pltpu.CompilerParams(vmem_limit_bytes=32 * 2**20),
+        cost_estimate=pl.CostEstimate(
+            flops=2 * STEPS * NB * 16 * CAP * width, bytes_accessed=4 * 2**20, transcendentals=0
+        ),
+    )(jnp.stack([zh, x, skip]).astype(jnp.int32), base, rank, *parts)
 
 
 def body(matrix, panels, diag_blocks, pivots):
@@ -310,11 +378,9 @@
     wide, pivots, matrix = lax.optimization_barrier((jnp.broadcast_to(panels, (8,) + panels.shape), pivots, matrix))
     by_y = exchange(wide, "y")
 
-    origin, base = origins(pivots)
-
-    picked = dot(picks(base.reshape(-1), local), matrix).astype(jnp.bfloat16)
-    active = sum(dealt(picked.reshape(STEPS, 4, 64, width).transpose(1, 0, 2, 3), "x"))
-    active = active.reshape(STEPS, 4, 16, width).transpose(1, 0, 2, 3)
+    origin, base, rank = origins(pivots)
+    packed = passed(pack(me, jnp.int32(0), base, rank, matrix), "zh")
+    packed[1], packed[2], packed[3], by_y = lax.optimization_barrier((*packed[1:], by_y))
 
     pair = jnp.array(PAIRS, jnp.int32).reshape(8, 2, 2)
     pair = lax.dynamic_index_in_dim(pair, y // 4, 1, keepdims=False)
@@ -323,33 +389,28 @@
     ids = lax.dynamic_slice_in_dim(ids.reshape(STEPS * STEPS, NB), y % 4 * 64, 64, 1)
     rows = l_rows(at, pair[:, 0], pair[:, 1], ids, by_y)
 
+    packed = passed(jnp.stack(packed), "x")
     chunk = add_up(exchange(rows, ("zl", "c")))
-    both = jnp.concatenate([jnp.broadcast_to(chunk, (4,) + chunk.shape), active], axis=1)
-    both, pivots, diag_blocks = lax.optimization_barrier((both, pivots, diag_blocks))
+    chunk, pivots, diag_blocks = lax.optimization_barrier((chunk, pivots, diag_blocks))
     high, low = inverses(diag_blocks)
-    both = exchange(both, "zh")
-    chunk = add_up(both[:, :4])
-    wide = jnp.broadcast_to(chunk, (4,) + chunk.shape)
-    wide, both, high, low = lax.optimization_barrier((wide, both, high, low))
-    active = add_up(both[:, 4:])
-    chunk = add_up(exchange(wide, "x"))
-    active = jnp.stack(passed(active, "zh"))
+    chunk = add_up(everyone(chunk, "zh"))
+    packed[1], packed[2], packed[3], chunk, high, low = lax.optimization_barrier((*packed[1:], chunk, high, low))
+    chunk = add_up(everyone(chunk, "x"))
     panels_across = shift(by_y, "zl", 1)
-    active, chunk, panels_across = lax.optimization_barrier((active, chunk, panels_across))
-    active = passed(active, "x")
+    packed[0], chunk, panels_across, pivots = lax.optimization_barrier((packed[0], chunk, panels_across, pivots))
     chunk = everyone(chunk, ("y", "zl")).reshape(8, 2, 4, 16, 2 * NB)
     whole = [by_y, shift(by_y, "c", 1), panels_across, shift(panels_across, "c", 1)]
-    active[1], pivots = lax.optimization_barrier((active[1], pivots))
+    tops = unpack(zh, x, jnp.int32(0), base, rank, packed)
 
     same = pivots[:, :, None, None] == pivots[None, None]
     after = (t_ids[None, :] > t_ids[:, None])[:, None, :, None]
     stays = ~jnp.any(same & after, axis=(2, 3))
     owner = jnp.where(stays, pivots // ROWS, -1)
     ahead = (owner[:, :, None] == owner[:, None, :]) & (i_ids[None, :] < i_ids[:, None])
-    rank = jnp.where(stays, jnp.sum(ahead, axis=2, dtype=jnp.int32), -1)
-    rounds = (jnp.max(rank) + SLOTS) // SLOTS
+    order = jnp.where(stays, jnp.sum(ahead, axis=2, dtype=jnp.int32), -1)
+    rounds = (jnp.max(order) + SLOTS) // SLOTS
     mine = jnp.minimum(me, STEPS - 1)
-    my_rank = jnp.where(me < STEPS, lax.dynamic_index_in_dim(rank, mine, 0, keepdims=False), -1)
+    my_rank = jnp.where(me < STEPS, lax.dynamic_index_in_dim(order, mine, 0, keepdims=False), -1)
     my_owner = lax.dynamic_index_in_dim(owner, mine, 0, keepdims=False)
 
     def slots(q):
@@ -357,16 +418,25 @@
         return jnp.where((n >= 0) & (n < SLOTS), my_owner * SLOTS + n, -1)
 
     first = slots(0)[None]
-    active[2], active[3], chunk, whole[1], whole[3], first = lax.optimization_barrier(
-        (*active[2:], chunk, whole[1], whole[3], first)
-    )
+    tops, chunk, whole[1], whole[3], first = lax.optimization_barrier((tops, chunk, whole[1], whole[3], first))
+
+    def more_tops(state):
+        q, tops = state
+        held = pack(me, q * CAP, base, rank, matrix)
+        held = everyone(held, ("zh", "x")).reshape(4, 4, CAP, width)
+        held = [jnp.stack([held[(4 - e) % 4, (4 - d) % 4] for e in range(4)]) for d in range(4)]
+        zero = jnp.int32(0)
+        return q + 1, tops + unpack(zero, zero, q * CAP, base, rank, held)
+
+    top_rounds = (jnp.max(rank) + CAP) // CAP
+    _, tops = lax.while_loop(lambda state: state[0] < top_rounds, more_tops, (jnp.int32(1), tops))
     blocks = [chunk, shift(chunk, "c", 1)]
-    u, old, send = solve(at, first, high, low, matrix, active, blocks, whole)
+    u, old, send = solve(at, first, high, low, matrix, tops, blocks, whole)
 
     got = exchange(send.reshape(16, SLOTS, width), ("zh", "x"))
     u, pivots = lax.optimization_barrier((u, pivots))
     here = (pivots.reshape(-1)[None, :] == local[:, None]) & stays.reshape(-1)[None, :]
-    tag = jnp.max(jnp.where(here, (t_ids[:, None] * NB + rank).reshape(-1)[None, :], -1), axis=1)
+    tag = jnp.max(jnp.where(here, (t_ids[:, None] * NB + order).reshape(-1)[None, :], -1), axis=1)
     last = jnp.where(tag >= 0, tag // NB, -1)
     at_rank = jnp.where(tag >= 0, tag % NB, -1)
 

time: 177 us -> 167 us (0.944)
  the two profiles are of different devices: /device:TPU:73 before, /device:TPU:1 now
where the time goes in v4:
time: 167 us; the launch traced here: 166 us
  starting transfers between devices  75.5 us (45%)
  Pallas kernels  37.7 us (23%)
  waiting for transfers between devices  28.4 us (17%)
  blocking collectives  7.92 us (5%)
  local copies, waits for them, and re-layouts  7.67 us (5%)
  other arithmetic  7.42 us (4%)
  between operations  1.74 us (1%)
    ppermute x10, starting transfers between devices, shift(): return lax.ppermute(v, axis, [(i, (i + by) % n) for i in range(n)])  47.6 us
    all_to_all x5, starting transfers between devices, exchange(): return lax.all_to_all(v, axis, 0, 0)  28 us
    all_to_all x5, waiting for transfers between devices, exchange(): return lax.all_to_all(v, axis, 0, 0)  14.9 us
    ppermute x10, waiting for transfers between devices, shift(): return lax.ppermute(v, axis, [(i, (i + by) % n) for i in range(n)])  13.5 us
    pallas_call x1, Pallas kernels, inverses(): pl.pallas_call(inverse_kernel, out_shape=(out, out), in_specs=[spec], out...  10 us
    pallas_call x1, Pallas kernels, unpack(): pl.pallas_call(unpack_kernel, out_shape=jax.ShapeDtypeStruct((STEPS, NB,...  8.01 us
    all_to_all x1, blocking collectives, exchange(): return lax.all_to_all(v, axis, 0, 0)  7.92 us
    pallas_call x1, Pallas kernels, solve(): pl.pallas_call(solve_kernel, out_shape=(jax.ShapeDtypeStruct((STEPS, NB,...  7.88 us
  transfers between devices with their start and end apart: 15, of which 6 were waited for; matrix products, arithmetic and copies ran while one was open for 6% of the time, Pallas kernels for 16%

profile of v4, /device:TPU:1, one launch (start us, length us, event | category | flops | bytes accessed | tf_op | source)
XLA Modules:
  0.0 166.4 jit_solution(7197244518806471485)
XLA Ops:
  0.0 2.0 %broadcast_in_dim.70 = bf16[8,6,32,256]{3,2,1,0:T(8,128)(2,1)} broadcast(bf16[6,32,256]{2,1,0:T(8,128)(2,1)} %param.10), dimensions={1,2,3} | broadcast | bytes 884736 | tf_op jit(solution)/shard_map/broadcast_in_dim | solution.py:378
  2.0 7.7 %all-to-all-start.2 = ((bf16[8,6,32,256]{3,2,1,0:T(8,128)(2,1)}), bf16[8,6,32,256]{3,2,1,0:T(8,128)(2,1)S(1)}, u32[]{:S(2)}, u32[]{:S(2)}) async-start(bf16[8,6,32,256]{3,2,1,0:T(8,128)(2,1)} %broadcast_in_dim.70), calls=%async_computation.2 | async-start | bytes 1572864 | tf_op jit(solution)/shard_map/all_to_all | solution.py:68
  11.6 5.8 %collective-permute-start = (bf16[144,512]{1,0:T(8,128)(2,1)S(1)}, bf16[144,512]{1,0:T(8,128)(2,1)S(1)}, u32[]{:S(2)}, u32[]{:S(2)}) collective-permute-start(bf16[144,512]{1,0:T(8,128)(2,1)S(1)} %shard_map.56), channel_id=1, source_target_pairs={{0,128},{128,256},{256,384},{384,0},{1,129},{129,257},{257,385},{3... | collective-permute-start | bytes 442376 | tf_op jit(solution)/shard_map/ppermute | solution.py:82
  17.4 8.8 %collective-permute-start.1 = (bf16[144,512]{1,0:T(8,128)(2,1)S(1)}, bf16[144,512]{1,0:T(8,128)(2,1)S(1)}, u32[]{:S(2)}, u32[]{:S(2)}) collective-permute-start(bf16[144,512]{1,0:T(8,128)(2,1)S(1)} %shard_map.56), channel_id=1, source_target_pairs={{0,256},{128,384},{256,0},{384,128},{1,257},{129,385},{257,1},{385... | collective-permute-start | bytes 442376 | tf_op jit(solution)/shard_map/ppermute | solution.py:82
  26.3 3.4 %collective-permute-start.2 = (bf16[144,512]{1,0:T(8,128)(2,1)S(1)}, bf16[144,512]{1,0:T(8,128)(2,1)S(1)}, u32[]{:S(2)}, u32[]{:S(2)}) collective-permute-start(bf16[144,512]{1,0:T(8,128)(2,1)S(1)} %shard_map.56), channel_id=1, source_target_pairs={{0,384},{128,0},{256,128},{384,256},{1,385},{129,1},{257,129},{385... | collective-permute-start | bytes 442376 | tf_op jit(solution)/shard_map/ppermute | solution.py:82
  30.1 5.3 %collective-permute-done.1 = bf16[144,512]{1,0:T(8,128)(2,1)S(1)} collective-permute-done((bf16[144,512]{1,0:T(8,128)(2,1)S(1)}, bf16[144,512]{1,0:T(8,128)(2,1)S(1)}, u32[]{:S(2)}, u32[]{:S(2)}) %collective-permute-start.1) | collective-permute-done | bytes 147488 | tf_op jit(solution)/shard_map/ppermute | solution.py:82
  35.4 5.6 %collective-permute-done.2 = bf16[144,512]{1,0:T(8,128)(2,1)S(1)} collective-permute-done((bf16[144,512]{1,0:T(8,128)(2,1)S(1)}, bf16[144,512]{1,0:T(8,128)(2,1)S(1)}, u32[]{:S(2)}, u32[]{:S(2)}) %collective-permute-start.2) | collective-permute-done | bytes 147488 | tf_op jit(solution)/shard_map/ppermute | solution.py:82
  41.0 1.6 shard_map.57
  42.6 3.9 %all-to-all-start.3 = ((bf16[4,4,16,512]{3,2,1,0:T(8,128)(2,1)}), bf16[4,4,16,512]{3,2,1,0:T(8,128)(2,1)S(1)}, u32[]{:S(2)}, u32[]{:S(2)}) async-start(bf16[4,4,16,512]{3,2,1,0:T(8,128)(2,1)} %shard_map.57), calls=%async_computation.3 | async-start | bytes 524288 | tf_op jit(solution)/shard_map/all_to_all | solution.py:68
  47.6 3.2 %collective-permute-start.3 = (bf16[4,144,512]{2,1,0:T(8,128)(2,1)S(1)}, bf16[4,144,512]{2,1,0:T(8,128)(2,1)}, u32[]{:S(2)}, u32[]{:S(2)}) collective-permute-start(bf16[4,144,512]{2,1,0:T(8,128)(2,1)S(1)} %pad_maximum_fusion.4.refs_0_), channel_id=1, source_target_pairs={{0,32},{32,64},{64,96},{96,0},{1,33},{33,65},{65,97},{97,1},{2,34}... | collective-permute-start | bytes 1769480 | tf_op jit(solution)/shard_map/ppermute | solution.py:82
  50.8 4.3 %collective-permute-start.4 = (bf16[4,144,512]{2,1,0:T(8,128)(2,1)S(1)}, bf16[4,144,512]{2,1,0:T(8,128)(2,1)}, u32[]{:S(2)}, u32[]{:S(2)}) collective-permute-start(bf16[4,144,512]{2,1,0:T(8,128)(2,1)S(1)} %pad_maximum_fusion.4.refs_0_), channel_id=1, source_target_pairs={{0,64},{32,96},{64,0},{96,32},{1,65},{33,97},{65,1},{97,33},{2,66}... | collective-permute-start | bytes 1769480 | tf_op jit(solution)/shard_map/ppermute | solution.py:82
  55.1 3.1 %collective-permute-start.5 = (bf16[4,144,512]{2,1,0:T(8,128)(2,1)S(1)}, bf16[4,144,512]{2,1,0:T(8,128)(2,1)}, u32[]{:S(2)}, u32[]{:S(2)}) collective-permute-start(bf16[4,144,512]{2,1,0:T(8,128)(2,1)S(1)} %pad_maximum_fusion.4.refs_0_), channel_id=1, source_target_pairs={{0,96},{32,0},{64,32},{96,64},{1,97},{33,1},{65,33},{97,65},{2,98}... | collective-permute-start | bytes 1769480 | tf_op jit(solution)/shard_map/ppermute | solution.py:82
  58.1 3.3 %collective-permute-start.6 = (bf16[8,6,32,256]{3,2,1,0:T(8,128)(2,1)S(1)}, bf16[8,6,32,256]{3,2,1,0:T(8,128)(2,1)}, u32[]{:S(2)}, u32[]{:S(2)}) collective-permute-start(bf16[8,6,32,256]{3,2,1,0:T(8,128)(2,1)S(1)} %all-to-all-done.2.panels_ref.refs_3_.refs_0_), channel_id=1, source_target_pairs={{0,2},{2,0},{1,3},{3,1},{4,6},{6,4},{5,7},{7,5},{8,10},{10,8},{9,1... | collective-permute-start | bytes 2359304 | tf_op jit(solution)/shard_map/ppermute | solution.py:82
  62.2 4.8 %all-to-all-start.4 = ((bf16[4,4,16,512]{3,2,1,0:T(8,128)(2,1)}), bf16[4,4,16,512]{3,2,1,0:T(8,128)(2,1)S(1)}, u32[]{:S(2)}, u32[]{:S(2)}) async-start(bf16[4,4,16,512]{3,2,1,0:T(8,128)(2,1)} %broadcast_in_dim.77), calls=%async_computation.4 | async-start | bytes 524288 | tf_op jit(solution)/shard_map/all_to_all | solution.py:68
  67.0 10.0 %shard_map.58 = (bf16[6,256,256]{2,1,0:T(8,128)(2,1)S(1)}, bf16[6,256,256]{2,1,0:T(8,128)(2,1)S(1)}) custom-call(f32[6,256,256]{2,1,0:T(8,128)S(1)} %copy-done.5), custom_call_target="tpu_custom_call" | custom-call | flops 8455716864 | bytes 3145728 | tf_op jit(solution)/shard_map/pallas_call | solution.py:57
  78.8 7.1 %all-to-all-done.4 = bf16[4,4,16,512]{3,2,1,0:T(8,128)(2,1)S(1)} async-done(((bf16[4,4,16,512]{3,2,1,0:T(8,128)(2,1)}), bf16[4,4,16,512]{3,2,1,0:T(8,128)(2,1)S(1)}, u32[]{:S(2)}, u32[]{:S(2)}) %all-to-all-start.4) | async-done | bytes 262176 | tf_op jit(solution)/shard_map/all_to_all | solution.py:68
  86.0 7.9 %all_to_all.42 = bf16[4,4,16,512]{3,2,1,0:T(8,128)(2,1)S(1)} all-to-all(bf16[4,4,16,512]{3,2,1,0:T(8,128)(2,1)S(1)} %broadcast_in_dim.82), channel_id=1, replica_groups=mesh['zh'=4,'x'=4,'y'=8,'zl'=2,'c'=2] {'x'}, dimensions={0} | all-to-all | bytes 524288 | tf_op jit(solution)/shard_map/all_to_all | solution.py:68
  94.0 1.1 broadcast_in_dim.83
  95.1 6.8 %all-to-all-start.6 = ((bf16[16,4,16,512]{3,2,1,0:T(8,128)(2,1)}), bf16[16,4,16,512]{3,2,1,0:T(8,128)(2,1)}, u32[]{:S(2)}, u32[]{:S(2)}) async-start(bf16[16,4,16,512]{3,2,1,0:T(8,128)(2,1)} %broadcast_in_dim.83), calls=%async_computation.6 | async-start | bytes 2097152 | tf_op jit(solution)/shard_map/all_to_all | solution.py:68
  103.2 6.5 %collective-permute-start.7 = (bf16[8,6,32,256]{3,2,1,0:T(8,128)(2,1)S(1)}, bf16[8,6,32,256]{3,2,1,0:T(8,128)(2,1)S(1)}, u32[]{:S(2)}, u32[]{:S(2)}) collective-permute-start(bf16[8,6,32,256]{3,2,1,0:T(8,128)(2,1)S(1)} %all-to-all-done.2.panels_ref.refs_3_.refs_0_), channel_id=1, source_target_pairs={{0,1},{1,0},{2,3},{3,2},{4,5},{5,4},{6,7},{7,6},{8,9},{9,8},{10,11... | collective-permute-start | bytes 2359304 | tf_op jit(solution)/shard_map/ppermute | solution.py:82
  109.7 2.1 %collective-permute-start.8 = (bf16[8,6,32,256]{3,2,1,0:T(8,128)(2,1)}, bf16[8,6,32,256]{3,2,1,0:T(8,128)(2,1)}, u32[]{:S(2)}, u32[]{:S(2)}) collective-permute-start(bf16[8,6,32,256]{3,2,1,0:T(8,128)(2,1)} %collective-permute-done.6.refs_5_.refs_2_), channel_id=1, source_target_pairs={{0,1},{1,0},{2,3},{3,2},{4,5},{5,4},{6,7},{7,6},{8,9},{9,8},{10,11... | collective-permute-start | bytes 2359304 | tf_op jit(solution)/shard_map/ppermute | solution.py:82
  111.8 1.7 %and_reduce_fusion = pred[6,256]{1,0:T(8,128)(4,1)S(1)} fusion(s32[6,256]{1,0:T(8,128)S(1)} %copy-done.3, pred[6,6]{1,0:T(8,128)(4,1)S(1)} %iota_compare_fusion.6), kind=kLoop, calls=%fused_computation.29 | loop fusion | flops 7076352 | bytes 7716 | tf_op jit(solution)/shard_map/reduce_or | solution.py:407
  115.2 8.0 %shard_map.59 = bf16[6,256,512]{2,1,0:T(8,128)(2,1)} custom-call(s32[3]{0:T(128)S(1)} %pad_add_fusion.2.at_ref, s32[6,256]{1,0:T(8,128)S(1)} %get-tuple-element.360.base_ref, s32[6,256]{1,0:T(8,128)S(1)} %get-tuple-element.361.rank_ref, bf16[4,144,512]{2,1,0:T(8,128)(2,1)S(1)} %pad_maximum_fusion.4.refs_0_, ...), custom_call_target="tpu_custom_call" | custom-call | flops 3623878656 | bytes 4194304 | tf_op jit(solution)/shard_map/pallas_call | solution.py:355
  124.2 1.2 all-to-all-done.6
  125.4 7.1 %collective-permute-start.9 = (bf16[8,2,4,16,512]{4,3,2,1,0:T(8,128)(2,1)}, bf16[8,2,4,16,512]{4,3,2,1,0:T(8,128)(2,1)}, u32[]{:S(2)}, u32[]{:S(2)}) collective-permute-start(bf16[8,2,4,16,512]{4,3,2,1,0:T(8,128)(2,1)} %bitcast.33.refs_1_), channel_id=1, source_target_pairs={{0,1},{1,0},{2,3},{3,2},{4,5},{5,4},{6,7},{7,6},{8,9},{9,8},{10,11... | collective-permute-start | bytes 3145736 | tf_op jit(solution)/shard_map/ppermute | solution.py:82
  132.6 2.6 %collective-permute-done.9.refs_2_ = bf16[8,2,4,16,512]{4,3,2,1,0:T(8,128)(2,1)} collective-permute-done((bf16[8,2,4,16,512]{4,3,2,1,0:T(8,128)(2,1)}, bf16[8,2,4,16,512]{4,3,2,1,0:T(8,128)(2,1)}, u32[]{:S(2)}, u32[]{:S(2)}) %collective-permute-start.9) | collective-permute-done | bytes 1048608 | tf_op jit(solution)/shard_map/ppermute | solution.py:82
  135.1 7.9 %shard_map.60 = (bf16[6,256,512]{2,1,0:T(8,128)(2,1)}, bf16[256,512]{1,0:T(8,128)(2,1)S(1)}, bf16[512,512]{1,0:T(8,128)(2,1)}) custom-call(s32[4]{0:T(128)} %copy-done.4, s32[1,256]{1,0:T(1,128)} %get-tuple-element.146.slot_ref, bf16[6,256,256]{2,1,0:T(8,128)(2,1)} %copy-done.1, bf16[6,256,256]{2,1,0:T(8,128)(2,1)} %copy-done.2, ...), custom_call_target="tpu_custom_call" | custom-call | flops 2348810240 | bytes 9437184 | tf_op jit(solution)/shard_map/pallas_call | solution.py:179
  143.0 4.9 %all-to-all-start.7 = ((bf16[16,32,512]{2,1,0:T(8,128)(2,1)}), bf16[16,32,512]{2,1,0:T(8,128)(2,1)S(1)}, u32[]{:S(2)}, u32[]{:S(2)}) async-start(bf16[16,32,512]{2,1,0:T(8,128)(2,1)} %bitcast.77), calls=%async_computation.7 | async-start | bytes 1048576 | tf_op jit(solution)/shard_map/all_to_all | solution.py:68
  148.7 1.6 select_reduce_fusion
  151.3 6.9 %shard_map.61 = f32[1024,512]{1,0:T(8,128)S(1)} custom-call(s32[4]{0:T(128)} %copy-done.4, s32[1024,128]{1,0:T(8,128)} %broadcast_in_dim.124.last_ref, bf16[6,256,512]{2,1,0:T(8,128)(2,1)} %get-tuple-element.156.u_ref, bf16[1024,512]{1,0:T(8,128)(2,1)} %matrix_ref.2, bf16[8,6,32,256]{3,2,1,0:T(8,128)(2,1)} %copy-done, bf16[8,6,32,256]{3,2,1,0:T(8,128)(2,1)} %copy-done.8, ...), custom_call_target="tpu_custom_call" | custom-call | flops 1610612736 | bytes 8388608 | tf_op jit(solution)/shard_map/pallas_call | solution.py:236
  158.4 6.6 %all-to-all-done.7.got_ref = bf16[16,32,512]{2,1,0:T(8,128)(2,1)S(1)} async-done(((bf16[16,32,512]{2,1,0:T(8,128)(2,1)}), bf16[16,32,512]{2,1,0:T(8,128)(2,1)S(1)}, u32[]{:S(2)}, u32[]{:S(2)}) %all-to-all-start.7) | async-done | bytes 524320 | tf_op jit(solution)/shard_map/all_to_all | solution.py:68
  165.0 1.4 shard_map.62
  (75 shorter events, 10.8 us)
Async XLA Ops:
  0.0 29.9 %copy-start.11 = (s32[8,2,2]{0,2,1:T(2,128)S(1)}, s32[8,2,2]{0,2,1:T(2,128)}, u32[]{:S(2)}) copy-start(s32[8,2,2]{0,2,1:T(2,128)} %constant.170) | copy-start | bytes 388
  0.0 9.6 %copy-start.3 = (s32[6,256]{1,0:T(8,128)S(1)}, s32[6,256]{1,0:T(8,128)}, u32[]{:S(2)}) copy-start(s32[6,256]{1,0:T(8,128)} %pivots_ref) | copy-start | bytes 18436
  0.0 10.6 %copy-start.6 = (bf16[1024,512]{1,0:T(8,128)(2,1)S(1)}, bf16[1024,512]{1,0:T(8,128)(2,1)}, u32[]{:S(2)}) copy-start(bf16[1024,512]{1,0:T(8,128)(2,1)} %matrix_ref.2) | copy-start | bytes 3145732
  2.0 39.1 %all-to-all-start.2 = ((bf16[8,6,32,256]{3,2,1,0:T(8,128)(2,1)}), bf16[8,6,32,256]{3,2,1,0:T(8,128)(2,1)S(1)}, u32[]{:S(2)}, u32[]{:S(2)}) async-start(bf16[8,6,32,256]{3,2,1,0:T(8,128)(2,1)} %broadcast_in_dim.70), calls=%async_computation.2 | async-start | bytes 1572864 | tf_op jit(solution)/shard_map/all_to_all | solution.py:68
  11.6 18.5 %collective-permute-start = (bf16[144,512]{1,0:T(8,128)(2,1)S(1)}, bf16[144,512]{1,0:T(8,128)(2,1)S(1)}, u32[]{:S(2)}, u32[]{:S(2)}) collective-permute-start(bf16[144,512]{1,0:T(8,128)(2,1)S(1)} %shard_map.56), channel_id=1, source_target_pairs={{0,128},{128,256},{256,384},{384,0},{1,129},{129,257},{257,385},{3... | collective-permute-start | bytes 442376 | tf_op jit(solution)/shard_map/ppermute | solution.py:82
  17.4 17.9 %collective-permute-start.1 = (bf16[144,512]{1,0:T(8,128)(2,1)S(1)}, bf16[144,512]{1,0:T(8,128)(2,1)S(1)}, u32[]{:S(2)}, u32[]{:S(2)}) collective-permute-start(bf16[144,512]{1,0:T(8,128)(2,1)S(1)} %shard_map.56), channel_id=1, source_target_pairs={{0,256},{128,384},{256,0},{384,128},{1,257},{129,385},{257,1},{385... | collective-permute-start | bytes 442376 | tf_op jit(solution)/shard_map/ppermute | solution.py:82
  26.3 14.7 %collective-permute-start.2 = (bf16[144,512]{1,0:T(8,128)(2,1)S(1)}, bf16[144,512]{1,0:T(8,128)(2,1)S(1)}, u32[]{:S(2)}, u32[]{:S(2)}) collective-permute-start(bf16[144,512]{1,0:T(8,128)(2,1)S(1)} %shard_map.56), channel_id=1, source_target_pairs={{0,384},{128,0},{256,128},{384,256},{1,385},{129,1},{257,129},{385... | collective-permute-start | bytes 442376 | tf_op jit(solution)/shard_map/ppermute | solution.py:82
  29.8 37.2 %copy-start.5 = (f32[6,256,256]{2,1,0:T(8,128)S(1)}, f32[6,256,256]{2,1,0:T(8,128)}, u32[]{:S(2)}) copy-start(f32[6,256,256]{2,1,0:T(8,128)} %l_ref) | copy-start | bytes 4718596
  30.1 46.9 %copy-start.4 = (s32[4]{0:T(128)}, s32[4]{0:T(128)S(1)}, u32[]{:S(2)}) copy-start(s32[4]{0:T(128)S(1)} %pad_add_fusion.1.at_ref) | copy-start | bytes 52
  35.4 11.1 %copy-start.9 = (bf16[144,512]{1,0:T(8,128)(2,1)}, bf16[144,512]{1,0:T(8,128)(2,1)S(1)}, u32[]{:S(2)}) copy-start(bf16[144,512]{1,0:T(8,128)(2,1)S(1)} %collective-permute-done.1) | copy-start | bytes 442372
  41.0 5.5 %copy-start.10 = (bf16[144,512]{1,0:T(8,128)(2,1)}, bf16[144,512]{1,0:T(8,128)(2,1)S(1)}, u32[]{:S(2)}) copy-start(bf16[144,512]{1,0:T(8,128)(2,1)S(1)} %collective-permute-done.2) | copy-start | bytes 442372
  41.0 62.2 %copy-start = (bf16[8,6,32,256]{3,2,1,0:T(8,128)(2,1)}, bf16[8,6,32,256]{3,2,1,0:T(8,128)(2,1)S(1)}, u32[]{:S(2)}) copy-start(bf16[8,6,32,256]{3,2,1,0:T(8,128)(2,1)S(1)} %all-to-all-done.2.panels_ref.refs_3_.refs_0_) | copy-start | bytes 2359300
  42.6 18.8 %all-to-all-start.3 = ((bf16[4,4,16,512]{3,2,1,0:T(8,128)(2,1)}), bf16[4,4,16,512]{3,2,1,0:T(8,128)(2,1)S(1)}, u32[]{:S(2)}, u32[]{:S(2)}) async-start(bf16[4,4,16,512]{3,2,1,0:T(8,128)(2,1)} %shard_map.57), calls=%async_computation.3 | async-start | bytes 524288 | tf_op jit(solution)/shard_map/all_to_all | solution.py:68
  47.6 38.4 %collective-permute-start.3 = (bf16[4,144,512]{2,1,0:T(8,128)(2,1)S(1)}, bf16[4,144,512]{2,1,0:T(8,128)(2,1)}, u32[]{:S(2)}, u32[]{:S(2)}) collective-permute-start(bf16[4,144,512]{2,1,0:T(8,128)(2,1)S(1)} %pad_maximum_fusion.4.refs_0_), channel_id=1, source_target_pairs={{0,32},{32,64},{64,96},{96,0},{1,33},{33,65},{65,97},{97,1},{2,34}... | collective-permute-start | bytes 1769480 | tf_op jit(solution)/shard_map/ppermute | solution.py:82
  50.8 35.2 %collective-permute-start.4 = (bf16[4,144,512]{2,1,0:T(8,128)(2,1)S(1)}, bf16[4,144,512]{2,1,0:T(8,128)(2,1)}, u32[]{:S(2)}, u32[]{:S(2)}) collective-permute-start(bf16[4,144,512]{2,1,0:T(8,128)(2,1)S(1)} %pad_maximum_fusion.4.refs_0_), channel_id=1, source_target_pairs={{0,64},{32,96},{64,0},{96,32},{1,65},{33,97},{65,1},{97,33},{2,66}... | collective-permute-start | bytes 1769480 | tf_op jit(solution)/shard_map/ppermute | solution.py:82
  55.1 30.9 %collective-permute-start.5 = (bf16[4,144,512]{2,1,0:T(8,128)(2,1)S(1)}, bf16[4,144,512]{2,1,0:T(8,128)(2,1)}, u32[]{:S(2)}, u32[]{:S(2)}) collective-permute-start(bf16[4,144,512]{2,1,0:T(8,128)(2,1)S(1)} %pad_maximum_fusion.4.refs_0_), channel_id=1, source_target_pairs={{0,96},{32,0},{64,32},{96,64},{1,97},{33,1},{65,33},{97,65},{2,98}... | collective-permute-start | bytes 1769480 | tf_op jit(solution)/shard_map/ppermute | solution.py:82
  58.1 35.8 %collective-permute-start.6 = (bf16[8,6,32,256]{3,2,1,0:T(8,128)(2,1)S(1)}, bf16[8,6,32,256]{3,2,1,0:T(8,128)(2,1)}, u32[]{:S(2)}, u32[]{:S(2)}) collective-permute-start(bf16[8,6,32,256]{3,2,1,0:T(8,128)(2,1)S(1)} %all-to-all-done.2.panels_ref.refs_3_.refs_0_), channel_id=1, source_target_pairs={{0,2},{2,0},{1,3},{3,1},{4,6},{6,4},{5,7},{7,5},{8,10},{10,8},{9,1... | collective-permute-start | bytes 2359304 | tf_op jit(solution)/shard_map/ppermute | solution.py:82
  62.2 23.7 %all-to-all-start.4 = ((bf16[4,4,16,512]{3,2,1,0:T(8,128)(2,1)}), bf16[4,4,16,512]{3,2,1,0:T(8,128)(2,1)S(1)}, u32[]{:S(2)}, u32[]{:S(2)}) async-start(bf16[4,4,16,512]{3,2,1,0:T(8,128)(2,1)} %broadcast_in_dim.77), calls=%async_computation.4 | async-start | bytes 524288 | tf_op jit(solution)/shard_map/all_to_all | solution.py:68
  77.0 0.9 copy-start.1
  77.9 0.9 copy-start.2
  95.1 30.3 %all-to-all-start.6 = ((bf16[16,4,16,512]{3,2,1,0:T(8,128)(2,1)}), bf16[16,4,16,512]{3,2,1,0:T(8,128)(2,1)}, u32[]{:S(2)}, u32[]{:S(2)}) async-start(bf16[16,4,16,512]{3,2,1,0:T(8,128)(2,1)} %broadcast_in_dim.83), calls=%async_computation.6 | async-start | bytes 2097152 | tf_op jit(solution)/shard_map/all_to_all | solution.py:68
  103.2 20.1 %collective-permute-start.7 = (bf16[8,6,32,256]{3,2,1,0:T(8,128)(2,1)S(1)}, bf16[8,6,32,256]{3,2,1,0:T(8,128)(2,1)S(1)}, u32[]{:S(2)}, u32[]{:S(2)}) collective-permute-start(bf16[8,6,32,256]{3,2,1,0:T(8,128)(2,1)S(1)} %all-to-all-done.2.panels_ref.refs_3_.refs_0_), channel_id=1, source_target_pairs={{0,1},{1,0},{2,3},{3,2},{4,5},{5,4},{6,7},{7,6},{8,9},{9,8},{10,11... | collective-permute-start | bytes 2359304 | tf_op jit(solution)/shard_map/ppermute | solution.py:82
  109.7 14.5 %collective-permute-start.8 = (bf16[8,6,32,256]{3,2,1,0:T(8,128)(2,1)}, bf16[8,6,32,256]{3,2,1,0:T(8,128)(2,1)}, u32[]{:S(2)}, u32[]{:S(2)}) collective-permute-start(bf16[8,6,32,256]{3,2,1,0:T(8,128)(2,1)} %collective-permute-done.6.refs_5_.refs_2_), channel_id=1, source_target_pairs={{0,1},{1,0},{2,3},{3,2},{4,5},{5,4},{6,7},{7,6},{8,9},{9,8},{10,11... | collective-permute-start | bytes 2359304 | tf_op jit(solution)/shard_map/ppermute | solution.py:82
  115.2 17.3 %copy-start.7 = (bf16[1024,512]{1,0:T(8,128)(2,1)S(1)}, bf16[1024,512]{1,0:T(8,128)(2,1)}, u32[]{:S(2)}) copy-start(bf16[1024,512]{1,0:T(8,128)(2,1)} %matrix_ref.2) | copy-start | bytes 3145732
  123.3 0.9 copy-start.8
  125.4 9.7 %collective-permute-start.9 = (bf16[8,2,4,16,512]{4,3,2,1,0:T(8,128)(2,1)}, bf16[8,2,4,16,512]{4,3,2,1,0:T(8,128)(2,1)}, u32[]{:S(2)}, u32[]{:S(2)}) collective-permute-start(bf16[8,2,4,16,512]{4,3,2,1,0:T(8,128)(2,1)} %bitcast.33.refs_1_), channel_id=1, source_target_pairs={{0,1},{1,0},{2,3},{3,2},{4,5},{5,4},{6,7},{7,6},{8,9},{9,8},{10,11... | collective-permute-start | bytes 3145736 | tf_op jit(solution)/shard_map/ppermute | solution.py:82
  143.0 22.0 %all-to-all-start.7 = ((bf16[16,32,512]{2,1,0:T(8,128)(2,1)}), bf16[16,32,512]{2,1,0:T(8,128)(2,1)S(1)}, u32[]{:S(2)}, u32[]{:S(2)}) async-start(bf16[16,32,512]{2,1,0:T(8,128)(2,1)} %bitcast.77), calls=%async_computation.7 | async-start | bytes 1048576 | tf_op jit(solution)/shard_map/all_to_all | solution.py:68

commit v5 on v4

--- a/solution.py
+++ b/solution.py
@@ -389,15 +389,16 @@
     ids = lax.dynamic_slice_in_dim(ids.reshape(STEPS * STEPS, NB), y % 4 * 64, 64, 1)
     rows = l_rows(at, pair[:, 0], pair[:, 1], ids, by_y)
 
-    packed = passed(jnp.stack(packed), "x")
+    packed = jnp.stack(packed)
     chunk = add_up(exchange(rows, ("zl", "c")))
-    chunk, pivots, diag_blocks = lax.optimization_barrier((chunk, pivots, diag_blocks))
+    packed, chunk, pivots, diag_blocks = lax.optimization_barrier((packed, chunk, pivots, diag_blocks))
+    packed = passed(packed, "x")
     high, low = inverses(diag_blocks)
     chunk = add_up(everyone(chunk, "zh"))
-    packed[1], packed[2], packed[3], chunk, high, low = lax.optimization_barrier((*packed[1:], chunk, high, low))
+    chunk, high, low = lax.optimization_barrier((chunk, high, low))
     chunk = add_up(everyone(chunk, "x"))
     panels_across = shift(by_y, "zl", 1)
-    packed[0], chunk, panels_across, pivots = lax.optimization_barrier((packed[0], chunk, panels_across, pivots))
+    *packed, chunk, panels_across, pivots = lax.optimization_barrier((*packed, chunk, panels_across, pivots))
     chunk = everyone(chunk, ("y", "zl")).reshape(8, 2, 4, 16, 2 * NB)
     whole = [by_y, shift(by_y, "c", 1), panels_across, shift(panels_across, "c", 1)]
     tops = unpack(zh, x, jnp.int32(0), base, rank, packed)

time: 167 us -> 164 us (0.982)
  waiting for transfers between devices: 28.4 us -> 22.5 us
  starting transfers between devices: 75.5 us -> 77.9 us
    all_to_all x5, waiting for transfers between devices: 14.9 us -> 9.05 us  [exchange(): return lax.all_to_all(v, axis, 0, 0)]
    all_to_all x5, starting transfers between devices: 28 us -> 30.6 us  [exchange(): return lax.all_to_all(v, axis, 0, 0)]
where the time goes in v5:
time: 164 us; the launch traced here: 163 us
  starting transfers between devices  77.9 us (48%)
  Pallas kernels  37.7 us (23%)
  waiting for transfers between devices  22.5 us (14%)
  blocking collectives  7.92 us (5%)
  local copies, waits for them, and re-layouts  7.67 us (5%)
  other arithmetic  7.42 us (5%)
  between operations  1.75 us (1%)
    ppermute x10, starting transfers between devices, shift(): return lax.ppermute(v, axis, [(i, (i + by) % n) for i in range(n)])  47.3 us
    all_to_all x5, starting transfers between devices, exchange(): return lax.all_to_all(v, axis, 0, 0)  30.6 us
    ppermute x10, waiting for transfers between devices, shift(): return lax.ppermute(v, axis, [(i, (i + by) % n) for i in range(n)])  13.5 us
    pallas_call x1, Pallas kernels, inverses(): pl.pallas_call(inverse_kernel, out_shape=(out, out), in_specs=[spec], out...  10 us
    all_to_all x5, waiting for transfers between devices, exchange(): return lax.all_to_all(v, axis, 0, 0)  9.05 us
    pallas_call x1, Pallas kernels, unpack(): pl.pallas_call(unpack_kernel, out_shape=jax.ShapeDtypeStruct((STEPS, NB,...  8.01 us
    all_to_all x1, blocking collectives, exchange(): return lax.all_to_all(v, axis, 0, 0)  7.92 us
    pallas_call x1, Pallas kernels, solve(): pl.pallas_call(solve_kernel, out_shape=(jax.ShapeDtypeStruct((STEPS, NB,...  7.88 us
  transfers between devices with their start and end apart: 15, of which 6 were waited for; matrix products, arithmetic and copies ran while one was open for 6% of the time, Pallas kernels for 16%

profile of v5, /device:TPU:1, one launch (start us, length us, event | category | flops | bytes accessed | tf_op | source)
XLA Modules:
  0.0 162.9 jit_solution(7602140730942647847)
XLA Ops:
  0.0 2.0 %broadcast_in_dim.70 = bf16[8,6,32,256]{3,2,1,0:T(8,128)(2,1)} broadcast(bf16[6,32,256]{2,1,0:T(8,128)(2,1)} %param.10), dimensions={1,2,3} | broadcast | bytes 884736 | tf_op jit(solution)/shard_map/broadcast_in_dim | solution.py:378
  2.0 7.7 %all-to-all-start.2 = ((bf16[8,6,32,256]{3,2,1,0:T(8,128)(2,1)}), bf16[8,6,32,256]{3,2,1,0:T(8,128)(2,1)S(1)}, u32[]{:S(2)}, u32[]{:S(2)}) async-start(bf16[8,6,32,256]{3,2,1,0:T(8,128)(2,1)} %broadcast_in_dim.70), calls=%async_computation.2 | async-start | bytes 1572864 | tf_op jit(solution)/shard_map/all_to_all | solution.py:68
  11.6 5.8 %collective-permute-start = (bf16[144,512]{1,0:T(8,128)(2,1)S(1)}, bf16[144,512]{1,0:T(8,128)(2,1)S(1)}, u32[]{:S(2)}, u32[]{:S(2)}) collective-permute-start(bf16[144,512]{1,0:T(8,128)(2,1)S(1)} %shard_map.56), channel_id=1, source_target_pairs={{0,128},{128,256},{256,384},{384,0},{1,129},{129,257},{257,385},{3... | collective-permute-start | bytes 442376 | tf_op jit(solution)/shard_map/ppermute | solution.py:82
  17.4 8.8 %collective-permute-start.1 = (bf16[144,512]{1,0:T(8,128)(2,1)S(1)}, bf16[144,512]{1,0:T(8,128)(2,1)S(1)}, u32[]{:S(2)}, u32[]{:S(2)}) collective-permute-start(bf16[144,512]{1,0:T(8,128)(2,1)S(1)} %shard_map.56), channel_id=1, source_target_pairs={{0,256},{128,384},{256,0},{384,128},{1,257},{129,385},{257,1},{385... | collective-permute-start | bytes 442376 | tf_op jit(solution)/shard_map/ppermute | solution.py:82
  26.3 3.4 %collective-permute-start.2 = (bf16[144,512]{1,0:T(8,128)(2,1)S(1)}, bf16[144,512]{1,0:T(8,128)(2,1)S(1)}, u32[]{:S(2)}, u32[]{:S(2)}) collective-permute-start(bf16[144,512]{1,0:T(8,128)(2,1)S(1)} %shard_map.56), channel_id=1, source_target_pairs={{0,384},{128,0},{256,128},{384,256},{1,385},{129,1},{257,129},{385... | collective-permute-start | bytes 442376 | tf_op jit(solution)/shard_map/ppermute | solution.py:82
  30.1 5.3 %collective-permute-done.1 = bf16[144,512]{1,0:T(8,128)(2,1)S(1)} collective-permute-done((bf16[144,512]{1,0:T(8,128)(2,1)S(1)}, bf16[144,512]{1,0:T(8,128)(2,1)S(1)}, u32[]{:S(2)}, u32[]{:S(2)}) %collective-permute-start.1) | collective-permute-done | bytes 147488 | tf_op jit(solution)/shard_map/ppermute | solution.py:82
  35.4 5.6 %collective-permute-done.2 = bf16[144,512]{1,0:T(8,128)(2,1)S(1)} collective-permute-done((bf16[144,512]{1,0:T(8,128)(2,1)S(1)}, bf16[144,512]{1,0:T(8,128)(2,1)S(1)}, u32[]{:S(2)}, u32[]{:S(2)}) %collective-permute-start.2) | collective-permute-done | bytes 147488 | tf_op jit(solution)/shard_map/ppermute | solution.py:82
  41.0 1.6 shard_map.57
  42.6 3.9 %all-to-all-start.3 = ((bf16[4,4,16,512]{3,2,1,0:T(8,128)(2,1)}), bf16[4,4,16,512]{3,2,1,0:T(8,128)(2,1)S(1)}, u32[]{:S(2)}, u32[]{:S(2)}) async-start(bf16[4,4,16,512]{3,2,1,0:T(8,128)(2,1)} %shard_map.57), calls=%async_computation.3 | async-start | bytes 524288 | tf_op jit(solution)/shard_map/all_to_all | solution.py:68
  46.5 3.3 %collective-permute-start.6 = (bf16[8,6,32,256]{3,2,1,0:T(8,128)(2,1)S(1)}, bf16[8,6,32,256]{3,2,1,0:T(8,128)(2,1)}, u32[]{:S(2)}, u32[]{:S(2)}) collective-permute-start(bf16[8,6,32,256]{3,2,1,0:T(8,128)(2,1)S(1)} %all-to-all-done.2.panels_ref.refs_3_.refs_0_), channel_id=1, source_target_pairs={{0,2},{2,0},{1,3},{3,1},{4,6},{6,4},{5,7},{7,5},{8,10},{10,8},{9,1... | collective-permute-start | bytes 2359304 | tf_op jit(solution)/shard_map/ppermute | solution.py:82
  49.8 1.1 pad_maximum_fusion.4.refs_0_
  51.7 3.2 %collective-permute-start.3 = (bf16[4,144,512]{2,1,0:T(8,128)(2,1)S(1)}, bf16[4,144,512]{2,1,0:T(8,128)(2,1)}, u32[]{:S(2)}, u32[]{:S(2)}) collective-permute-start(bf16[4,144,512]{2,1,0:T(8,128)(2,1)S(1)} %pad_maximum_fusion.4.refs_0_), channel_id=1, source_target_pairs={{0,32},{32,64},{64,96},{96,0},{1,33},{33,65},{65,97},{97,1},{2,34}... | collective-permute-start | bytes 1769480 | tf_op jit(solution)/shard_map/ppermute | solution.py:82
  54.9 4.3 %collective-permute-start.4 = (bf16[4,144,512]{2,1,0:T(8,128)(2,1)S(1)}, bf16[4,144,512]{2,1,0:T(8,128)(2,1)}, u32[]{:S(2)}, u32[]{:S(2)}) collective-permute-start(bf16[4,144,512]{2,1,0:T(8,128)(2,1)S(1)} %pad_maximum_fusion.4.refs_0_), channel_id=1, source_target_pairs={{0,64},{32,96},{64,0},{96,32},{1,65},{33,97},{65,1},{97,33},{2,66}... | collective-permute-start | bytes 1769480 | tf_op jit(solution)/shard_map/ppermute | solution.py:82
  59.2 3.1 %collective-permute-start.5 = (bf16[4,144,512]{2,1,0:T(8,128)(2,1)S(1)}, bf16[4,144,512]{2,1,0:T(8,128)(2,1)}, u32[]{:S(2)}, u32[]{:S(2)}) collective-permute-start(bf16[4,144,512]{2,1,0:T(8,128)(2,1)S(1)} %pad_maximum_fusion.4.refs_0_), channel_id=1, source_target_pairs={{0,96},{32,0},{64,32},{96,64},{1,97},{33,1},{65,33},{97,65},{2,98}... | collective-permute-start | bytes 1769480 | tf_op jit(solution)/shard_map/ppermute | solution.py:82
  63.0 4.8 %all-to-all-start.4 = ((bf16[4,4,16,512]{3,2,1,0:T(8,128)(2,1)}), bf16[4,4,16,512]{3,2,1,0:T(8,128)(2,1)S(1)}, u32[]{:S(2)}, u32[]{:S(2)}) async-start(bf16[4,4,16,512]{3,2,1,0:T(8,128)(2,1)} %broadcast_in_dim.77), calls=%async_computation.4 | async-start | bytes 524288 | tf_op jit(solution)/shard_map/all_to_all | solution.py:68
  67.8 10.0 %shard_map.58 = (bf16[6,256,256]{2,1,0:T(8,128)(2,1)S(1)}, bf16[6,256,256]{2,1,0:T(8,128)(2,1)S(1)}) custom-call(f32[6,256,256]{2,1,0:T(8,128)S(1)} %copy-done.5), custom_call_target="tpu_custom_call" | custom-call | flops 8455716864 | bytes 3145728 | tf_op jit(solution)/shard_map/pallas_call | solution.py:57
  79.7 7.9 %all_to_all.42 = bf16[4,4,16,512]{3,2,1,0:T(8,128)(2,1)S(1)} all-to-all(bf16[4,4,16,512]{3,2,1,0:T(8,128)(2,1)S(1)} %broadcast_in_dim.82), channel_id=1, replica_groups=mesh['zh'=4,'x'=4,'y'=8,'zl'=2,'c'=2] {'x'}, dimensions={0} | all-to-all | bytes 524288 | tf_op jit(solution)/shard_map/all_to_all | solution.py:68
  87.7 1.1 broadcast_in_dim.83
  88.8 6.9 %all-to-all-start.6 = ((bf16[16,4,16,512]{3,2,1,0:T(8,128)(2,1)}), bf16[16,4,16,512]{3,2,1,0:T(8,128)(2,1)}, u32[]{:S(2)}, u32[]{:S(2)}) async-start(bf16[16,4,16,512]{3,2,1,0:T(8,128)(2,1)} %broadcast_in_dim.83), calls=%async_computation.6 | async-start | bytes 2097152 | tf_op jit(solution)/shard_map/all_to_all | solution.py:68
  97.0 5.7 %collective-permute-start.7 = (bf16[8,6,32,256]{3,2,1,0:T(8,128)(2,1)S(1)}, bf16[8,6,32,256]{3,2,1,0:T(8,128)(2,1)S(1)}, u32[]{:S(2)}, u32[]{:S(2)}) collective-permute-start(bf16[8,6,32,256]{3,2,1,0:T(8,128)(2,1)S(1)} %all-to-all-done.2.panels_ref.refs_3_.refs_0_), channel_id=1, source_target_pairs={{0,1},{1,0},{2,3},{3,2},{4,5},{5,4},{6,7},{7,6},{8,9},{9,8},{10,11... | collective-permute-start | bytes 2359304 | tf_op jit(solution)/shard_map/ppermute | solution.py:82
  102.7 2.1 %collective-permute-start.8 = (bf16[8,6,32,256]{3,2,1,0:T(8,128)(2,1)}, bf16[8,6,32,256]{3,2,1,0:T(8,128)(2,1)}, u32[]{:S(2)}, u32[]{:S(2)}) collective-permute-start(bf16[8,6,32,256]{3,2,1,0:T(8,128)(2,1)} %collective-permute-done.6.refs_5_.refs_2_), channel_id=1, source_target_pairs={{0,1},{1,0},{2,3},{3,2},{4,5},{5,4},{6,7},{7,6},{8,9},{9,8},{10,11... | collective-permute-start | bytes 2359304 | tf_op jit(solution)/shard_map/ppermute | solution.py:82
  104.9 1.7 %and_reduce_fusion = pred[6,256]{1,0:T(8,128)(4,1)S(1)} fusion(s32[6,256]{1,0:T(8,128)S(1)} %copy-done.3, pred[6,6]{1,0:T(8,128)(4,1)S(1)} %iota_compare_fusion.6), kind=kLoop, calls=%fused_computation.29 | loop fusion | flops 7076352 | bytes 7716 | tf_op jit(solution)/shard_map/reduce_or | solution.py:408
  108.3 8.0 %shard_map.59 = bf16[6,256,512]{2,1,0:T(8,128)(2,1)} custom-call(s32[3]{0:T(128)S(1)} %pad_add_fusion.2.at_ref, s32[6,256]{1,0:T(8,128)S(1)} %get-tuple-element.362.base_ref, s32[6,256]{1,0:T(8,128)S(1)} %get-tuple-element.363.rank_ref, bf16[4,144,512]{2,1,0:T(8,128)(2,1)S(1)} %pad_maximum_fusion.4.refs_0_, ...), custom_call_target="tpu_custom_call" | custom-call | flops 3623878656 | bytes 4194304 | tf_op jit(solution)/shard_map/pallas_call | solution.py:355
  117.3 1.8 %all-to-all-done.6 = bf16[16,4,16,512]{3,2,1,0:T(8,128)(2,1)} async-done(((bf16[16,4,16,512]{3,2,1,0:T(8,128)(2,1)}), bf16[16,4,16,512]{3,2,1,0:T(8,128)(2,1)}, u32[]{:S(2)}, u32[]{:S(2)}) %all-to-all-start.6) | async-done | bytes 1048608 | tf_op jit(solution)/shard_map/all_to_all | solution.py:68
  119.1 7.6 %collective-permute-start.9 = (bf16[8,2,4,16,512]{4,3,2,1,0:T(8,128)(2,1)}, bf16[8,2,4,16,512]{4,3,2,1,0:T(8,128)(2,1)}, u32[]{:S(2)}, u32[]{:S(2)}) collective-permute-start(bf16[8,2,4,16,512]{4,3,2,1,0:T(8,128)(2,1)} %bitcast.33.refs_1_), channel_id=1, source_target_pairs={{0,1},{1,0},{2,3},{3,2},{4,5},{5,4},{6,7},{7,6},{8,9},{9,8},{10,11... | collective-permute-start | bytes 3145736 | tf_op jit(solution)/shard_map/ppermute | solution.py:82
  126.7 2.6 %collective-permute-done.9.refs_2_ = bf16[8,2,4,16,512]{4,3,2,1,0:T(8,128)(2,1)} collective-permute-done((bf16[8,2,4,16,512]{4,3,2,1,0:T(8,128)(2,1)}, bf16[8,2,4,16,512]{4,3,2,1,0:T(8,128)(2,1)}, u32[]{:S(2)}, u32[]{:S(2)}) %collective-permute-start.9) | collective-permute-done | bytes 1048608 | tf_op jit(solution)/shard_map/ppermute | solution.py:82
  129.3 7.9 %shard_map.60 = (bf16[6,256,512]{2,1,0:T(8,128)(2,1)}, bf16[256,512]{1,0:T(8,128)(2,1)S(1)}, bf16[512,512]{1,0:T(8,128)(2,1)}) custom-call(s32[4]{0:T(128)} %copy-done.4, s32[1,256]{1,0:T(1,128)} %get-tuple-element.148.slot_ref, bf16[6,256,256]{2,1,0:T(8,128)(2,1)} %copy-done.1, bf16[6,256,256]{2,1,0:T(8,128)(2,1)} %copy-done.2, ...), custom_call_target="tpu_custom_call" | custom-call | flops 2348810240 | bytes 9437184 | tf_op jit(solution)/shard_map/pallas_call | solution.py:179
  137.2 7.4 %all-to-all-start.7 = ((bf16[16,32,512]{2,1,0:T(8,128)(2,1)}), bf16[16,32,512]{2,1,0:T(8,128)(2,1)S(1)}, u32[]{:S(2)}, u32[]{:S(2)}) async-start(bf16[16,32,512]{2,1,0:T(8,128)(2,1)} %bitcast.77), calls=%async_computation.7 | async-start | bytes 1048576 | tf_op jit(solution)/shard_map/all_to_all | solution.py:68
  145.4 1.6 select_reduce_fusion
  148.0 6.9 %shard_map.61 = f32[1024,512]{1,0:T(8,128)S(1)} custom-call(s32[4]{0:T(128)} %copy-done.4, s32[1024,128]{1,0:T(8,128)} %broadcast_in_dim.124.last_ref, bf16[6,256,512]{2,1,0:T(8,128)(2,1)} %get-tuple-element.158.u_ref, bf16[1024,512]{1,0:T(8,128)(2,1)} %matrix_ref.2, bf16[8,6,32,256]{3,2,1,0:T(8,128)(2,1)} %copy-done, bf16[8,6,32,256]{3,2,1,0:T(8,128)(2,1)} %copy-done.8, ...), custom_call_target="tpu_custom_call" | custom-call | flops 1610612736 | bytes 8388608 | tf_op jit(solution)/shard_map/pallas_call | solution.py:236
  155.1 6.4 %all-to-all-done.7.got_ref = bf16[16,32,512]{2,1,0:T(8,128)(2,1)S(1)} async-done(((bf16[16,32,512]{2,1,0:T(8,128)(2,1)}), bf16[16,32,512]{2,1,0:T(8,128)(2,1)S(1)}, u32[]{:S(2)}, u32[]{:S(2)}) %all-to-all-start.7) | async-done | bytes 524320 | tf_op jit(solution)/shard_map/all_to_all | solution.py:68
  161.5 1.4 shard_map.62
  (75 shorter events, 10.5 us)
Async XLA Ops:
  0.0 29.9 %copy-start.11 = (s32[8,2,2]{0,2,1:T(2,128)S(1)}, s32[8,2,2]{0,2,1:T(2,128)}, u32[]{:S(2)}) copy-start(s32[8,2,2]{0,2,1:T(2,128)} %constant.170) | copy-start | bytes 388
  0.0 9.6 %copy-start.3 = (s32[6,256]{1,0:T(8,128)S(1)}, s32[6,256]{1,0:T(8,128)}, u32[]{:S(2)}) copy-start(s32[6,256]{1,0:T(8,128)} %pivots_ref) | copy-start | bytes 18436
  0.0 10.6 %copy-start.6 = (bf16[1024,512]{1,0:T(8,128)(2,1)S(1)}, bf16[1024,512]{1,0:T(8,128)(2,1)}, u32[]{:S(2)}) copy-start(bf16[1024,512]{1,0:T(8,128)(2,1)} %matrix_ref.2) | copy-start | bytes 3145732
  2.0 39.1 %all-to-all-start.2 = ((bf16[8,6,32,256]{3,2,1,0:T(8,128)(2,1)}), bf16[8,6,32,256]{3,2,1,0:T(8,128)(2,1)S(1)}, u32[]{:S(2)}, u32[]{:S(2)}) async-start(bf16[8,6,32,256]{3,2,1,0:T(8,128)(2,1)} %broadcast_in_dim.70), calls=%async_computation.2 | async-start | bytes 1572864 | tf_op jit(solution)/shard_map/all_to_all | solution.py:68
  11.6 18.5 %collective-permute-start = (bf16[144,512]{1,0:T(8,128)(2,1)S(1)}, bf16[144,512]{1,0:T(8,128)(2,1)S(1)}, u32[]{:S(2)}, u32[]{:S(2)}) collective-permute-start(bf16[144,512]{1,0:T(8,128)(2,1)S(1)} %shard_map.56), channel_id=1, source_target_pairs={{0,128},{128,256},{256,384},{384,0},{1,129},{129,257},{257,385},{3... | collective-permute-start | bytes 442376 | tf_op jit(solution)/shard_map/ppermute | solution.py:82
  17.4 17.9 %collective-permute-start.1 = (bf16[144,512]{1,0:T(8,128)(2,1)S(1)}, bf16[144,512]{1,0:T(8,128)(2,1)S(1)}, u32[]{:S(2)}, u32[]{:S(2)}) collective-permute-start(bf16[144,512]{1,0:T(8,128)(2,1)S(1)} %shard_map.56), channel_id=1, source_target_pairs={{0,256},{128,384},{256,0},{384,128},{1,257},{129,385},{257,1},{385... | collective-permute-start | bytes 442376 | tf_op jit(solution)/shard_map/ppermute | solution.py:82
  26.3 14.7 %collective-permute-start.2 = (bf16[144,512]{1,0:T(8,128)(2,1)S(1)}, bf16[144,512]{1,0:T(8,128)(2,1)S(1)}, u32[]{:S(2)}, u32[]{:S(2)}) collective-permute-start(bf16[144,512]{1,0:T(8,128)(2,1)S(1)} %shard_map.56), channel_id=1, source_target_pairs={{0,384},{128,0},{256,128},{384,256},{1,385},{129,1},{257,129},{385... | collective-permute-start | bytes 442376 | tf_op jit(solution)/shard_map/ppermute | solution.py:82
  29.8 38.0 %copy-start.5 = (f32[6,256,256]{2,1,0:T(8,128)S(1)}, f32[6,256,256]{2,1,0:T(8,128)}, u32[]{:S(2)}) copy-start(f32[6,256,256]{2,1,0:T(8,128)} %l_ref) | copy-start | bytes 4718596
  30.1 47.7 %copy-start.4 = (s32[4]{0:T(128)}, s32[4]{0:T(128)S(1)}, u32[]{:S(2)}) copy-start(s32[4]{0:T(128)S(1)} %pad_add_fusion.1.at_ref) | copy-start | bytes 52
  35.4 14.4 %copy-start.9 = (bf16[144,512]{1,0:T(8,128)(2,1)}, bf16[144,512]{1,0:T(8,128)(2,1)S(1)}, u32[]{:S(2)}) copy-start(bf16[144,512]{1,0:T(8,128)(2,1)S(1)} %collective-permute-done.1) | copy-start | bytes 442372
  41.0 8.8 %copy-start.10 = (bf16[144,512]{1,0:T(8,128)(2,1)}, bf16[144,512]{1,0:T(8,128)(2,1)S(1)}, u32[]{:S(2)}) copy-start(bf16[144,512]{1,0:T(8,128)(2,1)S(1)} %collective-permute-done.2) | copy-start | bytes 442372
  41.0 56.0 %copy-start = (bf16[8,6,32,256]{3,2,1,0:T(8,128)(2,1)}, bf16[8,6,32,256]{3,2,1,0:T(8,128)(2,1)S(1)}, u32[]{:S(2)}) copy-start(bf16[8,6,32,256]{3,2,1,0:T(8,128)(2,1)S(1)} %all-to-all-done.2.panels_ref.refs_3_.refs_0_) | copy-start | bytes 2359300
  42.6 9.0 %all-to-all-start.3 = ((bf16[4,4,16,512]{3,2,1,0:T(8,128)(2,1)}), bf16[4,4,16,512]{3,2,1,0:T(8,128)(2,1)S(1)}, u32[]{:S(2)}, u32[]{:S(2)}) async-start(bf16[4,4,16,512]{3,2,1,0:T(8,128)(2,1)} %shard_map.57), calls=%async_computation.3 | async-start | bytes 524288 | tf_op jit(solution)/shard_map/all_to_all | solution.py:68
  46.5 41.1 %collective-permute-start.6 = (bf16[8,6,32,256]{3,2,1,0:T(8,128)(2,1)S(1)}, bf16[8,6,32,256]{3,2,1,0:T(8,128)(2,1)}, u32[]{:S(2)}, u32[]{:S(2)}) collective-permute-start(bf16[8,6,32,256]{3,2,1,0:T(8,128)(2,1)S(1)} %all-to-all-done.2.panels_ref.refs_3_.refs_0_), channel_id=1, source_target_pairs={{0,2},{2,0},{1,3},{3,1},{4,6},{6,4},{5,7},{7,5},{8,10},{10,8},{9,1... | collective-permute-start | bytes 2359304 | tf_op jit(solution)/shard_map/ppermute | solution.py:82
  51.7 35.9 %collective-permute-start.3 = (bf16[4,144,512]{2,1,0:T(8,128)(2,1)S(1)}, bf16[4,144,512]{2,1,0:T(8,128)(2,1)}, u32[]{:S(2)}, u32[]{:S(2)}) collective-permute-start(bf16[4,144,512]{2,1,0:T(8,128)(2,1)S(1)} %pad_maximum_fusion.4.refs_0_), channel_id=1, source_target_pairs={{0,32},{32,64},{64,96},{96,0},{1,33},{33,65},{65,97},{97,1},{2,34}... | collective-permute-start | bytes 1769480 | tf_op jit(solution)/shard_map/ppermute | solution.py:82
  54.9 32.7 %collective-permute-start.4 = (bf16[4,144,512]{2,1,0:T(8,128)(2,1)S(1)}, bf16[4,144,512]{2,1,0:T(8,128)(2,1)}, u32[]{:S(2)}, u32[]{:S(2)}) collective-permute-start(bf16[4,144,512]{2,1,0:T(8,128)(2,1)S(1)} %pad_maximum_fusion.4.refs_0_), channel_id=1, source_target_pairs={{0,64},{32,96},{64,0},{96,32},{1,65},{33,97},{65,1},{97,33},{2,66}... | collective-permute-start | bytes 1769480 | tf_op jit(solution)/shard_map/ppermute | solution.py:82
  59.2 28.5 %collective-permute-start.5 = (bf16[4,144,512]{2,1,0:T(8,128)(2,1)S(1)}, bf16[4,144,512]{2,1,0:T(8,128)(2,1)}, u32[]{:S(2)}, u32[]{:S(2)}) collective-permute-start(bf16[4,144,512]{2,1,0:T(8,128)(2,1)S(1)} %pad_maximum_fusion.4.refs_0_), channel_id=1, source_target_pairs={{0,96},{32,0},{64,32},{96,64},{1,97},{33,1},{65,33},{97,65},{2,98}... | collective-permute-start | bytes 1769480 | tf_op jit(solution)/shard_map/ppermute | solution.py:82
  63.0 16.6 %all-to-all-start.4 = ((bf16[4,4,16,512]{3,2,1,0:T(8,128)(2,1)}), bf16[4,4,16,512]{3,2,1,0:T(8,128)(2,1)S(1)}, u32[]{:S(2)}, u32[]{:S(2)}) async-start(bf16[4,4,16,512]{3,2,1,0:T(8,128)(2,1)} %broadcast_in_dim.77), calls=%async_computation.4 | async-start | bytes 524288 | tf_op jit(solution)/shard_map/all_to_all | solution.py:68
  77.8 0.9 copy-start.1
  78.7 0.9 copy-start.2
  88.8 30.3 %all-to-all-start.6 = ((bf16[16,4,16,512]{3,2,1,0:T(8,128)(2,1)}), bf16[16,4,16,512]{3,2,1,0:T(8,128)(2,1)}, u32[]{:S(2)}, u32[]{:S(2)}) async-start(bf16[16,4,16,512]{3,2,1,0:T(8,128)(2,1)} %broadcast_in_dim.83), calls=%async_computation.6 | async-start | bytes 2097152 | tf_op jit(solution)/shard_map/all_to_all | solution.py:68
  97.0 19.3 %collective-permute-start.7 = (bf16[8,6,32,256]{3,2,1,0:T(8,128)(2,1)S(1)}, bf16[8,6,32,256]{3,2,1,0:T(8,128)(2,1)S(1)}, u32[]{:S(2)}, u32[]{:S(2)}) collective-permute-start(bf16[8,6,32,256]{3,2,1,0:T(8,128)(2,1)S(1)} %all-to-all-done.2.panels_ref.refs_3_.refs_0_), channel_id=1, source_target_pairs={{0,1},{1,0},{2,3},{3,2},{4,5},{5,4},{6,7},{7,6},{8,9},{9,8},{10,11... | collective-permute-start | bytes 2359304 | tf_op jit(solution)/shard_map/ppermute | solution.py:82
  102.7 14.5 %collective-permute-start.8 = (bf16[8,6,32,256]{3,2,1,0:T(8,128)(2,1)}, bf16[8,6,32,256]{3,2,1,0:T(8,128)(2,1)}, u32[]{:S(2)}, u32[]{:S(2)}) collective-permute-start(bf16[8,6,32,256]{3,2,1,0:T(8,128)(2,1)} %collective-permute-done.6.refs_5_.refs_2_), channel_id=1, source_target_pairs={{0,1},{1,0},{2,3},{3,2},{4,5},{5,4},{6,7},{7,6},{8,9},{9,8},{10,11... | collective-permute-start | bytes 2359304 | tf_op jit(solution)/shard_map/ppermute | solution.py:82
  108.3 18.4 %copy-start.7 = (bf16[1024,512]{1,0:T(8,128)(2,1)S(1)}, bf16[1024,512]{1,0:T(8,128)(2,1)}, u32[]{:S(2)}) copy-start(bf16[1024,512]{1,0:T(8,128)(2,1)} %matrix_ref.2) | copy-start | bytes 3145732
  116.3 0.9 copy-start.8
  119.1 10.2 %collective-permute-start.9 = (bf16[8,2,4,16,512]{4,3,2,1,0:T(8,128)(2,1)}, bf16[8,2,4,16,512]{4,3,2,1,0:T(8,128)(2,1)}, u32[]{:S(2)}, u32[]{:S(2)}) collective-permute-start(bf16[8,2,4,16,512]{4,3,2,1,0:T(8,128)(2,1)} %bitcast.33.refs_1_), channel_id=1, source_target_pairs={{0,1},{1,0},{2,3},{3,2},{4,5},{5,4},{6,7},{7,6},{8,9},{9,8},{10,11... | collective-permute-start | bytes 3145736 | tf_op jit(solution)/shard_map/ppermute | solution.py:82
  137.2 24.4 %all-to-all-start.7 = ((bf16[16,32,512]{2,1,0:T(8,128)(2,1)}), bf16[16,32,512]{2,1,0:T(8,128)(2,1)S(1)}, u32[]{:S(2)}, u32[]{:S(2)}) async-start(bf16[16,32,512]{2,1,0:T(8,128)(2,1)} %bitcast.77), calls=%async_computation.7 | async-start | bytes 1048576 | tf_op jit(solution)/shard_map/all_to_all | solution.py:68
